TPU v7x, 32 devices: a whole 2x2x4 slice. The times are simulated.
32 devices in a mesh: grp: 2 (over x), blk: 16 (over z, y, core).
Axes of the slice: x: 2, y: 2, z: 4, core: 2. Of those that a mesh axis runs over, the one named last changes fastest.
Arguments:
- tokens: bfloat16 [4096, 1152], P(('grp', 'blk')), may hold values from -6 to 6
- segment_ids: int32 [4096], P(('grp', 'blk')), may hold values from 0 to 3, as said below
- ln1_gain: float32 [1152], replicated, may hold values from 0.5 to 1.5
- ln1_bias: float32 [1152], replicated, may hold values from -4 to 4
- qkv_weight: bfloat16 [1152, 3456], P('blk'), may hold values from -0.1875 to 0.1875
- q_bias: float32 [1152], replicated, may hold values from -4 to 4
- v_bias: float32 [1152], replicated, may hold values from -0.8 to 0.8
- out_weight: bfloat16 [1152, 1152], P('blk'), may hold values from -1.5 to 1.5
- out_bias: float32 [1152], replicated, may hold values from -2.4 to 2.4
- ln2_gain: float32 [1152], replicated, may hold values from 0.5 to 1.5
- ln2_bias: float32 [1152], replicated, may hold values from -4 to 4
- fc1_weight: bfloat16 [1152, 4304], P('blk'), may hold values from -0.1875 to 0.1875
- fc1_bias: float32 [4304], replicated, may hold values from -4 to 4
- fc2_weight: bfloat16 [1152, 4304], P('blk'), may hold values from -0.09375 to 0.09375
- fc2_bias: float32 [1152], replicated, may hold values from -2.4 to 2.4
- bridge_gate: bfloat16 [1152, 14336], P(None, 'blk'), may hold values from -0.1875 to 0.1875
- bridge_up: bfloat16 [1152, 14336], P(None, 'blk'), may hold values from -0.1875 to 0.1875
- bridge_down: bfloat16 [14336, 4096], P('blk'), may hold values from -0.046875 to 0.046875
- context_gain: float32 [4096], replicated, may hold values from 0.5 to 1.5
- latents: bfloat16 [64, 4096], replicated, may hold values from -6 to 6
- latent_gain: float32 [4096], replicated, may hold values from 0.5 to 1.5
- query_weight: bfloat16 [4096, 1536], P('blk'), may hold values from -0.09375 to 0.09375
- key_weight: bfloat16 [4096, 384], P('blk'), may hold values from -0.09375 to 0.09375
- value_weight: bfloat16 [4096, 384], P('blk'), may hold values from -0.09375 to 0.09375
- mixer_weight: bfloat16 [1536, 4096], P('blk'), may hold values from -0.875 to 0.875
- post_gain: float32 [4096], replicated, may hold values from 0.5 to 1.5
- latent_gate: bfloat16 [4096, 16384], P(None, 'blk'), may hold values from -0.09375 to 0.09375
- latent_up: bfloat16 [4096, 16384], P(None, 'blk'), may hold values from -0.09375 to 0.09375
- latent_down: bfloat16 [16384, 4096], P('blk'), may hold values from -0.046875 to 0.046875
- cotangent: bfloat16 [512, 4096], P('grp'), may hold values from -6 to 6
Outputs:
- latents_out: bfloat16 [512, 4096], P(('grp', 'blk'))
- grad_tokens: float32 [4096, 1152], P(('grp', 'blk'))
- grad_ln1_gain: float32 [1152], replicated
- grad_ln1_bias: float32 [1152], replicated
- grad_qkv_weight: float32 [1152, 3456], P(('grp', 'blk'))
- grad_q_bias: float32 [1152], replicated
- grad_v_bias: float32 [1152], replicated
- grad_out_weight: float32 [1152, 1152], P(('grp', 'blk'))
- grad_out_bias: float32 [1152], replicated
- grad_ln2_gain: float32 [1152], replicated
- grad_ln2_bias: float32 [1152], replicated
- grad_fc1_weight: float32 [1152, 4304], P(('grp', 'blk'))
- grad_fc1_bias: float32 [4304], replicated
- grad_fc2_weight: float32 [1152, 4304], P(('grp', 'blk'))
- grad_fc2_bias: float32 [1152], replicated
- grad_bridge_gate: float32 [1152, 14336], P(None, 'blk')
- grad_bridge_up: float32 [1152, 14336], P(None, 'blk')
- grad_bridge_down: float32 [14336, 4096], P('blk')
- grad_context_gain: float32 [4096], replicated
- grad_latents: float32 [64, 4096], replicated
- grad_latent_gain: float32 [4096], replicated
- grad_query_weight: float32 [4096, 1536], P(('grp', 'blk'))
- grad_key_weight: float32 [4096, 384], P(('grp', 'blk'))
- grad_value_weight: float32 [4096, 384], P(('grp', 'blk'))
- grad_mixer_weight: float32 [1536, 4096], P(('grp', 'blk'))
- grad_post_gain: float32 [4096], replicated
- grad_latent_gate: float32 [4096, 16384], P(None, 'blk')
- grad_latent_up: float32 [4096, 16384], P(None, 'blk')
- grad_latent_down: float32 [16384, 4096], P('blk')
Inputs may be any that keep to these rules, and one draw needn't show every extreme that they name: `segment_ids`: patches of one pack with equal ids belong to one image; ids are only compared within a pack. Each pack holds 4 images, each of one patch or more, at most 1024 patches each and one of exactly 1024. A pack is cut into blocks of 64 consecutive patches, placed on the pack's devices in a drawn order, two blocks a device, so the patches of one image may lie on many devices; in every pack some image has patches on the first and on the last device of blk.
All inputs are finite; a program needn't handle non-finite values.
Results may differ from a plain program's by a relative error of at most 0.028.
Values may be sent and summed in bfloat16 or wider, within the bound.
No kernel may reach another device: no remote copies, remote signals or barrier semaphores. Data moves between devices by JAX's collectives and lax.ppermute only.
A program may use at most 576 MiB of HBM per device.

v0:
```python
import jax
import jax.numpy as jnp
from jax import lax
from jax.sharding import PartitionSpec as P

HEADS = 16
HEAD = 72
LATENTS = 64
P_HEADS = 16
P_KV = 4
P_HEAD = 96


masked_score = -1e30
norm_eps = 1e-06
contract_last = (((1,), (1,)), ((), ()))


def merged(array, axis, combine):
    everything = jax.tree.map(
        lambda part, kind: lax.all_gather(part.astype(kind), axis),
        array,
        (jnp.bfloat16, jnp.bfloat16),
    )

    def take(k):
        return jax.tree.map(lambda part, own: part[k].astype(own.dtype), everything, array)

    return lax.fori_loop(
        1, lax.axis_size(axis), lambda k, so_far: combine(so_far, take(k)), take(0)
    )


def layer_norm(values, gain, bias):
    center = values - jnp.mean(values, axis=-1, keepdims=True)
    spread = jnp.mean(center * center, axis=-1, keepdims=True)
    return center * lax.rsqrt(spread + norm_eps) * gain + bias


def rms_norm(values, gain):
    return values * lax.rsqrt(jnp.mean(values * values, axis=-1, keepdims=True) + norm_eps) * gain


def smooth_gate(values):
    return jax.nn.gelu(values, approximate=True)


def swiglu(gate, up):
    return jax.nn.silu(gate) * up


def mat_times(left, right):
    return jnp.dot(left, right, preferred_element_type=jnp.float32)


def mat_times_t(left, right):
    return lax.dot_general(left, right, contract_last, preferred_element_type=jnp.float32)


def outer_sum(left, right):
    return jnp.einsum("td,te->de", left, right, preferred_element_type=jnp.float32)


def by_heads(matrix):
    return matrix.reshape(matrix.shape[0], HEADS, HEAD)


def query_heads(matrix):
    return matrix.reshape(matrix.shape[0], P_KV, P_HEADS // P_KV, P_HEAD)


def pair_heads(matrix):
    return matrix.reshape(matrix.shape[0], P_KV, P_HEAD)


def head_scores(query_rows, key_rows):
    raw = jnp.einsum(
        "thd,shd->hts", by_heads(query_rows), by_heads(key_rows), preferred_element_type=jnp.float32
    )
    return raw * HEAD ** (-0.5)


def same_image(row_ids, col_ids):
    return (row_ids[:, None] == col_ids[None, :])[None]


def rows_at(array, first, width, axis=0):
    return lax.dynamic_slice_in_dim(array, first, width, axis)


def over_blocks(total_rows, step_fn, carry):
    width = 512

    def inner(index, state):
        return step_fn(state, index * width, width)

    return lax.fori_loop(0, total_rows // width, inner, carry)


def attention_grads(query_rows, grad_rows, lse_rows, delta_rows, key_rows, value_rows, mask):
    scores = head_scores(query_rows, key_rows)
    probs = jnp.where(mask, jnp.exp(scores - lse_rows[:, :, None]), 0.0)
    dprob = jnp.einsum(
        "thd,shd->hts",
        by_heads(grad_rows),
        by_heads(value_rows),
        preferred_element_type=jnp.float32,
    )
    score_grad = (probs * (dprob - delta_rows[:, :, None])).astype(jnp.bfloat16)
    return (probs.astype(jnp.bfloat16), score_grad)


def combine_stats(first, second):
    top = jnp.maximum(first[0], second[0])
    return (top, first[1] * jnp.exp(first[0] - top) + second[1] * jnp.exp(second[0] - top))


def fetch_weights(
    qkv_weight,
    out_weight,
    fc1_weight,
    fc2_weight,
    query_weight,
    key_weight,
    value_weight,
    mixer_weight,
):
    return (
        lax.all_gather(qkv_weight, "blk", axis=0, tiled=True),
        lax.all_gather(out_weight, "blk", axis=0, tiled=True),
        lax.all_gather(fc1_weight, "blk", axis=0, tiled=True),
        lax.all_gather(fc2_weight, "blk", axis=0, tiled=True),
        lax.all_gather(query_weight, "blk", axis=0, tiled=True),
        lax.all_gather(key_weight, "blk", axis=0, tiled=True),
        lax.all_gather(value_weight, "blk", axis=0, tiled=True),
        lax.all_gather(mixer_weight, "blk", axis=0, tiled=True),
    )


def fetch_keys(keys, values, segment_ids):
    return (
        lax.all_gather(keys, "blk", axis=0, tiled=True),
        lax.all_gather(values, "blk", axis=0, tiled=True),
        lax.all_gather(segment_ids, "blk", axis=0, tiled=True),
    )


def on_device(
    tokens,
    segment_ids,
    ln1_gain,
    ln1_bias,
    qkv_weight,
    q_bias,
    v_bias,
    out_weight,
    out_bias,
    ln2_gain,
    ln2_bias,
    fc1_weight,
    fc1_bias,
    fc2_weight,
    fc2_bias,
    bridge_gate,
    bridge_up,
    bridge_down,
    context_gain,
    latents,
    latent_gain,
    query_weight,
    key_weight,
    value_weight,
    mixer_weight,
    post_gain,
    latent_gate,
    latent_up,
    latent_down,
    cotangent,
):
    local_rows = tokens.shape[0]
    features = tokens.shape[1]
    groups = P_HEADS // P_KV
    scale_latent = P_HEAD ** (-0.5)
    qkv_full, out_full, fc1_full, fc2_full, query_full, key_full, value_full, mixer_full = (
        fetch_weights(
            qkv_weight,
            out_weight,
            fc1_weight,
            fc2_weight,
            query_weight,
            key_weight,
            value_weight,
            mixer_weight,
        )
    )
    inputs = tokens.astype(jnp.float32)
    normed, first_norm_back = jax.vjp(layer_norm, inputs, ln1_gain, ln1_bias)
    first_in = normed.astype(jnp.bfloat16)
    projected = mat_times(first_in, qkv_full)
    queries = (projected[:, :features] + q_bias).astype(jnp.bfloat16)
    keys = projected[:, features : 2 * features].astype(jnp.bfloat16)
    values = (projected[:, 2 * features :] + v_bias).astype(jnp.bfloat16)
    all_keys, all_values, all_ids = fetch_keys(keys, values, segment_ids)
    group_rows = all_keys.shape[0]

    def stats_step(state, first, width):
        top, total = state
        mask = same_image(segment_ids, rows_at(all_ids, first, width))
        scores = jnp.where(
            mask, head_scores(queries, rows_at(all_keys, first, width)), masked_score
        )
        new_top = jnp.maximum(top, jnp.max(scores, axis=-1))
        weights = jnp.where(mask, jnp.exp(scores - new_top[:, :, None]), 0.0)
        return (new_top, total * jnp.exp(top - new_top) + jnp.sum(weights, axis=-1))

    start_top = jnp.full((HEADS, local_rows), masked_score, jnp.float32)
    start_total = jnp.zeros((HEADS, local_rows), jnp.float32)
    top, total = over_blocks(group_rows, stats_step, (start_top, start_total))
    lse = top + jnp.log(total)

    def value_step(state, first, width):
        mask = same_image(segment_ids, rows_at(all_ids, first, width))
        scores = head_scores(queries, rows_at(all_keys, first, width))
        probs = jnp.where(mask, jnp.exp(scores - lse[:, :, None]), 0.0).astype(jnp.bfloat16)
        mixed = jnp.einsum(
            "hts,shd->thd",
            probs,
            by_heads(rows_at(all_values, first, width)),
            preferred_element_type=jnp.float32,
        )
        return state + mixed.reshape(local_rows, features)

    zero_rows = jnp.zeros((local_rows, features), jnp.float32)
    attended = over_blocks(group_rows, value_step, zero_rows)
    attended_low = attended.astype(jnp.bfloat16)
    hidden_state = inputs + mat_times(attended_low, out_full) + out_bias
    second, second_norm_back = jax.vjp(layer_norm, hidden_state, ln2_gain, ln2_bias)
    second_in = second.astype(jnp.bfloat16)
    pre = mat_times(second_in, fc1_full) + fc1_bias
    act, gate_back = jax.vjp(smooth_gate, pre)
    act_low = act.astype(jnp.bfloat16)
    encoded = hidden_state + mat_times_t(act_low, fc2_full) + fc2_bias
    bridge_in = encoded.astype(jnp.bfloat16)
    bridge_rows = lax.all_gather(bridge_in, "blk", axis=0, tiled=True)
    bridge_act, bridge_act_back = jax.vjp(
        swiglu, mat_times(bridge_rows, bridge_gate), mat_times(bridge_rows, bridge_up)
    )
    bridge_hidden = bridge_act.astype(jnp.bfloat16)
    context = lax.psum_scatter(
        mat_times(
            rows_at(bridge_hidden, jnp.int32(0), local_rows * lax.axis_size("blk")), bridge_down
        ),
        "blk",
        scatter_dimension=0,
        tiled=True,
    )
    lat_rows = cotangent.shape[0]
    images = lat_rows // LATENTS
    lat_own = lat_rows // lax.axis_size("blk")
    own_start = lax.axis_index("blk") * lat_own
    own_mask = jnp.arange(lat_rows, dtype=jnp.int32) // lat_own == lax.axis_index("blk")
    image_index = jnp.arange(images, dtype=jnp.int32)
    image_mask = (image_index[:, None] == segment_ids[None, :])[:, None, None, None, :]
    row_mask = own_mask.reshape(images, LATENTS)[:, None, None, :, None]
    context_normed, context_norm_back = jax.vjp(rms_norm, context, context_gain)
    context_in = context_normed.astype(jnp.bfloat16)
    patch_keys = mat_times(context_in, key_full).astype(jnp.bfloat16)
    patch_values = mat_times(context_in, value_full).astype(jnp.bfloat16)
    latent_normed, latent_norm_back = jax.vjp(rms_norm, latents.astype(jnp.float32), latent_gain)
    latent_in = latent_normed.astype(jnp.bfloat16)
    latent_queries = mat_times(latent_in, query_full).astype(jnp.bfloat16)
    latent_keys = mat_times(latent_in, key_full).astype(jnp.bfloat16)
    latent_values = mat_times(latent_in, value_full).astype(jnp.bfloat16)
    latent_query_heads = query_heads(latent_queries)
    patch_key_heads = pair_heads(patch_keys)
    patch_value_heads = pair_heads(patch_values)
    latent_key_heads = pair_heads(latent_keys)
    latent_value_heads = pair_heads(latent_values)
    patch_scores = (
        jnp.einsum(
            "lgrd,tgd->grlt",
            latent_query_heads,
            patch_key_heads,
            preferred_element_type=jnp.float32,
        )
        * scale_latent
    )
    latent_scores = (
        jnp.einsum(
            "lgrd,kgd->grlk",
            latent_query_heads,
            latent_key_heads,
            preferred_element_type=jnp.float32,
        )
        * scale_latent
    )
    masked = jnp.where(image_mask, patch_scores[None], masked_score)
    part_top = jnp.max(masked, axis=-1)
    part_total = jnp.sum(jnp.where(image_mask, jnp.exp(masked - part_top[..., None]), 0.0), axis=-1)
    merged_top, merged_total = merged((part_top, part_total), "blk", combine_stats)
    self_top = jnp.max(latent_scores, axis=-1)
    self_total = jnp.sum(jnp.exp(latent_scores - self_top[..., None]), axis=-1)
    joint_top, joint_total = combine_stats(
        (merged_top, merged_total), (self_top[None], self_total[None])
    )
    latent_lse = joint_top + jnp.log(joint_total)
    patch_probs = jnp.where(
        image_mask, jnp.exp(patch_scores[None] - latent_lse[..., None]), 0.0
    ).astype(jnp.bfloat16)
    part_mix = jnp.einsum(
        "igrlt,tgd->ilgrd", patch_probs, patch_value_heads, preferred_element_type=jnp.float32
    ).reshape(lat_rows, P_HEADS * P_HEAD)
    patch_mix = lax.psum(part_mix, "blk")
    latent_probs = jnp.exp(latent_scores[None] - latent_lse[..., None]).astype(jnp.bfloat16)
    self_mix = jnp.einsum(
        "igrlk,kgd->ilgrd", latent_probs, latent_value_heads, preferred_element_type=jnp.float32
    ).reshape(lat_rows, P_HEADS * P_HEAD)
    mixed_latent = patch_mix + self_mix
    attended_latent = mixed_latent.astype(jnp.bfloat16)
    latent_state = jnp.tile(latents.astype(jnp.float32), (images, 1)) + mat_times(
        attended_latent, mixer_full
    )
    post_normed, post_norm_back = jax.vjp(rms_norm, latent_state, post_gain)
    post_unit = rms_norm(latent_state, 1.0)
    post_in = post_normed.astype(jnp.bfloat16)
    latent_act, latent_act_back = jax.vjp(
        swiglu, mat_times(post_in, latent_gate), mat_times(post_in, latent_up)
    )
    latent_hidden = latent_act.astype(jnp.bfloat16)
    latent_down_rows = lax.psum_scatter(
        mat_times(
            rows_at(latent_hidden, jnp.int32(0), lat_own * lax.axis_size("blk")), latent_down
        ),
        "blk",
        scatter_dimension=0,
        tiled=True,
    )
    latents_out = (rows_at(latent_state, own_start, lat_own) + latent_down_rows).astype(
        jnp.bfloat16
    )
    latent_gate_grad, latent_up_grad = latent_act_back(mat_times_t(cotangent, latent_down))
    latent_gate_low = latent_gate_grad.astype(jnp.bfloat16)
    latent_up_low = latent_up_grad.astype(jnp.bfloat16)
    grad_latent_down = jnp.einsum(
        "tf,td->fd", latent_hidden, cotangent, preferred_element_type=jnp.float32
    )
    grad_latent_gate = outer_sum(post_in, latent_gate_low)
    grad_latent_up = outer_sum(post_in, latent_up_low)
    post_part = mat_times_t(latent_gate_low, latent_gate) + mat_times_t(latent_up_low, latent_up)
    post_grad = lax.psum(post_part, "blk")
    state_norm_grad = post_norm_back(post_grad)[0]
    post_gain_part = jnp.sum(jnp.where(own_mask[:, None], post_grad * post_unit, 0.0), axis=0)
    state_grad = cotangent.astype(jnp.float32) + state_norm_grad
    state_low = state_grad.astype(jnp.bfloat16)
    zero_low = jnp.zeros((), jnp.bfloat16)
    grad_mixer_part = outer_sum(jnp.where(own_mask[:, None], attended_latent, zero_low), state_low)
    resid_part = jnp.sum(
        jnp.where(own_mask[:, None], state_grad, 0.0).reshape(images, LATENTS, -1), axis=0
    )
    latent_att_grad = mat_times_t(state_low, mixer_full).astype(jnp.bfloat16)
    grad_heads = latent_att_grad.reshape(images, LATENTS, P_KV, groups, P_HEAD)
    latent_delta = jnp.transpose(
        jnp.sum(
            (latent_att_grad.astype(jnp.float32) * mixed_latent).reshape(
                images, LATENTS, P_KV, groups, P_HEAD
            ),
            axis=-1,
        ),
        (0, 2, 3, 1),
    )
    patch_weights = jnp.where(image_mask, jnp.exp(patch_scores[None] - latent_lse[..., None]), 0.0)
    patch_dprob = jnp.einsum(
        "ilgrd,tgd->igrlt", grad_heads, patch_value_heads, preferred_element_type=jnp.float32
    )
    patch_sgrad = (patch_weights * (patch_dprob - latent_delta[..., None])).astype(jnp.bfloat16)
    query_part = jnp.einsum(
        "igrlt,tgd->lgrd", patch_sgrad, patch_key_heads, preferred_element_type=jnp.float32
    )
    patch_key_grad = (
        (
            jnp.einsum(
                "igrlt,lgrd->tgd",
                patch_sgrad,
                latent_query_heads,
                preferred_element_type=jnp.float32,
            )
            * scale_latent
        )
        .reshape(local_rows, P_KV * P_HEAD)
        .astype(jnp.bfloat16)
    )
    patch_value_grad = (
        jnp.einsum("igrlt,ilgrd->tgd", patch_probs, grad_heads, preferred_element_type=jnp.float32)
        .reshape(local_rows, P_KV * P_HEAD)
        .astype(jnp.bfloat16)
    )
    latent_weights = jnp.exp(latent_scores[None] - latent_lse[..., None])
    latent_dprob = jnp.einsum(
        "ilgrd,kgd->igrlk", grad_heads, latent_value_heads, preferred_element_type=jnp.float32
    )
    latent_sgrad = jnp.where(
        row_mask,
        (latent_weights * (latent_dprob - latent_delta[..., None])).astype(jnp.bfloat16),
        zero_low,
    )
    latent_probs_own = jnp.where(row_mask, latent_probs, zero_low)
    query_part = query_part + jnp.einsum(
        "igrlk,kgd->lgrd", latent_sgrad, latent_key_heads, preferred_element_type=jnp.float32
    )
    latent_key_part = jnp.einsum(
        "igrlk,lgrd->kgd", latent_sgrad, latent_query_heads, preferred_element_type=jnp.float32
    )
    latent_value_part = jnp.einsum(
        "igrlk,ilgrd->kgd", latent_probs_own, grad_heads, preferred_element_type=jnp.float32
    )
    context_in_grad = mat_times_t(patch_key_grad, key_full) + mat_times_t(
        patch_value_grad, value_full
    )
    context_grad, context_gain_part = context_norm_back(context_in_grad)
    grad_key_part = outer_sum(context_in, patch_key_grad)
    grad_value_part = outer_sum(context_in, patch_value_grad)
    context_rows = lax.all_gather(context_grad.astype(jnp.bfloat16), "blk", axis=0, tiled=True)
    bridge_gate_grad, bridge_up_grad = bridge_act_back(mat_times_t(context_rows, bridge_down))
    bridge_gate_low = bridge_gate_grad.astype(jnp.bfloat16)
    bridge_up_low = bridge_up_grad.astype(jnp.bfloat16)
    grad_bridge_down = jnp.einsum(
        "tf,td->fd", bridge_hidden, context_rows, preferred_element_type=jnp.float32
    )
    grad_bridge_gate = outer_sum(bridge_rows, bridge_gate_low)
    grad_bridge_up = outer_sum(bridge_rows, bridge_up_low)
    start = jnp.int32(0)
    encoded_grad = lax.psum_scatter(
        mat_times_t(rows_at(bridge_gate_low, start, local_rows * lax.axis_size("blk")), bridge_gate)
        + mat_times_t(rows_at(bridge_up_low, start, local_rows * lax.axis_size("blk")), bridge_up),
        "blk",
        scatter_dimension=0,
        tiled=True,
    )
    encoded_low = encoded_grad.astype(jnp.bfloat16)
    grad_fc2 = jnp.einsum("td,tf->df", encoded_low, act_low, preferred_element_type=jnp.float32)
    grad_fc2_bias = jnp.sum(encoded_grad, axis=0)
    pre_grad = gate_back(mat_times(encoded_low, fc2_full))[0].astype(jnp.bfloat16)
    grad_fc1 = outer_sum(second_in, pre_grad)
    grad_fc1_bias = jnp.sum(pre_grad.astype(jnp.float32), axis=0)
    second_grad = mat_times_t(pre_grad, fc1_full)
    hidden_norm_grad, grad_ln2_gain, grad_ln2_bias = second_norm_back(second_grad)
    hidden_grad = encoded_grad + hidden_norm_grad
    hidden_low = hidden_grad.astype(jnp.bfloat16)
    grad_out = outer_sum(attended_low, hidden_low)
    grad_out_bias = jnp.sum(hidden_grad, axis=0)
    attended_grad = mat_times_t(hidden_low, out_full).astype(jnp.bfloat16)
    delta = jnp.transpose(jnp.sum(by_heads(attended_grad.astype(jnp.float32) * attended), axis=-1))

    def query_step(state, first, width):
        key_rows = rows_at(all_keys, first, width)
        mask = same_image(segment_ids, rows_at(all_ids, first, width))
        probs_low, score_grad = attention_grads(
            queries, attended_grad, lse, delta, key_rows, rows_at(all_values, first, width), mask
        )
        change = jnp.einsum(
            "hts,shd->thd", score_grad, by_heads(key_rows), preferred_element_type=jnp.float32
        )
        return state + change.reshape(local_rows, features)

    vision_query_sum = over_blocks(group_rows, query_step, zero_rows)

    def step(state, first, width):
        key_rows = rows_at(all_keys, first, width)
        value_rows = rows_at(all_values, first, width)
        mask = same_image(segment_ids, rows_at(all_ids, first, width))
        probs_low, score_grad = attention_grads(
            queries, attended_grad, lse, delta, key_rows, value_rows, mask
        )
        key_change = jnp.einsum(
            "hts,thd->shd", score_grad, by_heads(queries), preferred_element_type=jnp.float32
        )
        value_change = jnp.einsum(
            "hts,thd->shd", probs_low, by_heads(attended_grad), preferred_element_type=jnp.float32
        )
        joined = jnp.concatenate(
            [key_change.reshape(width, features), value_change.reshape(width, features)], axis=1
        )
        return lax.dynamic_update_slice_in_dim(state, joined, first, 0)

    both_sums = lax.psum_scatter(
        over_blocks(
            local_rows * lax.axis_size("blk"),
            step,
            jnp.zeros((local_rows * lax.axis_size("blk"), 2 * features), jnp.float32),
        ),
        "blk",
        scatter_dimension=0,
        tiled=True,
    )
    scale = HEAD ** (-0.5)
    query_low = (vision_query_sum * scale).astype(jnp.bfloat16)
    key_low = (both_sums[:, :features] * scale).astype(jnp.bfloat16)
    value_low = both_sums[:, features:].astype(jnp.bfloat16)
    grad_q_bias = jnp.sum(query_low.astype(jnp.float32), axis=0)
    grad_v_bias = jnp.sum(value_low.astype(jnp.float32), axis=0)
    stacked = jnp.concatenate([query_low, key_low, value_low], axis=1)
    grad_qkv = outer_sum(first_in, stacked)
    first_grad = mat_times_t(stacked, qkv_full)
    input_norm_grad, grad_ln1_gain, grad_ln1_bias = first_norm_back(first_grad)
    grad_tokens = hidden_grad + input_norm_grad
    shares = (
        lax.psum_scatter(grad_qkv, ("grp", "blk"), scatter_dimension=0, tiled=True),
        lax.psum_scatter(grad_out, ("grp", "blk"), scatter_dimension=0, tiled=True),
        lax.psum_scatter(grad_fc1, ("grp", "blk"), scatter_dimension=0, tiled=True),
        lax.psum_scatter(grad_fc2, ("grp", "blk"), scatter_dimension=0, tiled=True),
        lax.psum_scatter(grad_key_part, ("grp", "blk"), scatter_dimension=0, tiled=True),
        lax.psum_scatter(grad_value_part, ("grp", "blk"), scatter_dimension=0, tiled=True),
        lax.psum_scatter(grad_mixer_part, ("grp", "blk"), scatter_dimension=0, tiled=True),
    )
    slices = (
        lax.psum(grad_bridge_gate.astype(jnp.bfloat16), "grp").astype(jnp.float32),
        lax.psum(grad_bridge_up.astype(jnp.bfloat16), "grp").astype(jnp.float32),
        lax.psum(grad_bridge_down.astype(jnp.bfloat16), "grp").astype(jnp.float32),
        lax.psum(grad_latent_gate.astype(jnp.bfloat16), "grp").astype(jnp.float32),
        lax.psum(grad_latent_up.astype(jnp.bfloat16), "grp").astype(jnp.float32),
        lax.psum(grad_latent_down.astype(jnp.bfloat16), "grp").astype(jnp.float32),
    )
    small = lax.psum(
        (
            grad_ln1_gain,
            grad_ln1_bias,
            grad_q_bias,
            grad_v_bias,
            grad_out_bias,
            grad_ln2_gain,
            grad_ln2_bias,
            grad_fc1_bias,
            grad_fc2_bias,
            context_gain_part,
            post_gain_part,
            resid_part,
            query_part,
            latent_key_part,
            latent_value_part,
        ),
        ("grp", "blk"),
    )
    latent_query_low = (
        (small[12] * scale_latent).reshape(LATENTS, P_HEADS * P_HEAD).astype(jnp.bfloat16)
    )
    latent_key_low = (small[13] * scale_latent).reshape(LATENTS, P_KV * P_HEAD).astype(jnp.bfloat16)
    latent_value_low = small[14].reshape(LATENTS, P_KV * P_HEAD).astype(jnp.bfloat16)
    latent_in_grad = (
        mat_times_t(latent_query_low, query_full)
        + mat_times_t(latent_key_low, key_full)
        + mat_times_t(latent_value_low, value_full)
    )
    latent_grad, grad_latent_gain = latent_norm_back(latent_in_grad)
    grad_latents = small[11] + latent_grad
    share_index = lax.axis_index(("grp", "blk"))
    model_rows = query_full.shape[0] // lax.axis_size(("grp", "blk"))
    share_start = share_index * model_rows
    grad_query = rows_at(outer_sum(latent_in, latent_query_low), share_start, model_rows)
    grad_key = shares[4] + rows_at(outer_sum(latent_in, latent_key_low), share_start, model_rows)
    grad_value = shares[5] + rows_at(
        outer_sum(latent_in, latent_value_low), share_start, model_rows
    )
    return (
        latents_out,
        grad_tokens,
        small[0],
        small[1],
        shares[0],
        small[2],
        small[3],
        shares[1],
        small[4],
        small[5],
        small[6],
        shares[2],
        small[7],
        shares[3],
        small[8],
        slices[0],
        slices[1],
        slices[2],
        small[9],
        grad_latents,
        grad_latent_gain,
        grad_query,
        grad_key,
        grad_value,
        shares[6],
        small[10],
        slices[3],
        slices[4],
        slices[5],
    )


def solution(mesh):
    in_specs = (
        P(("grp", "blk"), None),
        P(("grp", "blk")),
        P(),
        P(),
        P("blk", None),
        P(),
        P(),
        P("blk", None),
        P(),
        P(),
        P(),
        P("blk", None),
        P(),
        P("blk", None),
        P(),
        P(None, "blk"),
        P(None, "blk"),
        P("blk", None),
        P(),
        P(),
        P(),
        P("blk", None),
        P("blk", None),
        P("blk", None),
        P("blk", None),
        P(),
        P(None, "blk"),
        P(None, "blk"),
        P("blk", None),
        P("grp", None),
    )
    out_specs = (
        P(("grp", "blk"), None),
        P(("grp", "blk"), None),
        P(),
        P(),
        P(("grp", "blk"), None),
        P(),
        P(),
        P(("grp", "blk"), None),
        P(),
        P(),
        P(),
        P(("grp", "blk"), None),
        P(),
        P(("grp", "blk"), None),
        P(),
        P(None, "blk"),
        P(None, "blk"),
        P("blk", None),
        P(),
        P(),
        P(),
        P(("grp", "blk"), None),
        P(("grp", "blk"), None),
        P(("grp", "blk"), None),
        P(("grp", "blk"), None),
        P(),
        P(None, "blk"),
        P(None, "blk"),
        P("blk", None),
    )
    return jax.shard_map(
        on_device, mesh=mesh, in_specs=in_specs, out_specs=out_specs, check_vma=False
    )
```

profile of v0, /device:TPU:10, one launch (start us, length us, event | category | flops | bytes accessed | tf_op | source)
XLA Modules:
  0.0 4199.6 jit_solution(12883755450413090743)
XLA Ops:
  10.9 72.3 %all-gather.16.cloned.1.call-done = bf16[1152,3456]{1,0:T(8,128)(2,1)} async-done(((bf16[72,3456]{1,0:T(8,128)(2,1)}), bf16[1152,3456]{1,0:T(8,128)(2,1)}) %all-gather.16.cloned.1.call-update) | async-done | bytes 7962640 | tf_op jit(solution)/shard_map/all_gather | solution.py:129
  93.8 16.5 all-gather.2
  110.5 31.8 all-gather.18.cloned.1.call-done
  148.9 48.1 %all-gather.20.cloned.1.call-done = bf16[2048,1152]{1,0:T(8,128)(2,1)} async-done(((bf16[128,1152]{1,0:T(8,128)(2,1)}), bf16[2048,1152]{1,0:T(8,128)(2,1)}) %all-gather.20.cloned.1.call-update) | async-done | bytes 4718608 | tf_op jit(solution)/shard_map/all_gather | solution.py:142
  203.8 34.0 while.76
  237.7 32.7 while.77
  275.1 50.8 %all-gather.24.cloned.1.call-done = bf16[1152,4304]{1,0:T(8,128)(2,1)} async-done(((bf16[72,4304]{1,0:T(8,128)(2,1)}), bf16[1152,4304]{1,0:T(8,128)(2,1)}) %all-gather.24.cloned.1.call-update) | async-done | bytes 9916432 | tf_op jit(solution)/shard_map/all_gather | solution.py:131
  326.0 9.2 convolution_add_fusion.1
  335.2 76.1 %all-gather.26.cloned.1.call-done = bf16[1152,4304]{1,0:T(8,128)(2,1)} async-done(((bf16[72,4304]{1,0:T(8,128)(2,1)}), bf16[1152,4304]{1,0:T(8,128)(2,1)}) %all-gather.26.cloned.1.call-update) | async-done | bytes 9916432 | tf_op jit(solution)/shard_map/all_gather | solution.py:132
  411.3 8.6 fusion.37
  421.4 51.1 %all-gather.28.cloned.1.call-done = bf16[2048,1152]{1,0:T(8,128)(2,1)} async-done(((bf16[128,1152]{1,0:T(8,128)(2,1)}), bf16[2048,1152]{1,0:T(8,128)(2,1)}) %all-gather.28.cloned.1.call-update) | async-done | bytes 4718608 | tf_op jit(solution)/shard_map/all_gather | solution.py:244
  472.5 8.2 fusion.178
  480.8 7.8 multiply_convert_fusion.1
  490.4 21.9 fusion.179
  521.7 97.5 %all-gather.34.cloned.1.call-done = bf16[4096,1536]{1,0:T(8,128)(2,1)} async-done(((bf16[256,1536]{1,0:T(8,128)(2,1)}), bf16[4096,1536]{1,0:T(8,128)(2,1)}) %all-gather.34.cloned.1.call-update) | async-done | bytes 12582928 | tf_op jit(solution)/shard_map/all_gather | solution.py:133
  628.3 325.6 %reduce-scatter.16.cloned.1.call-done = f32[128,4096]{1,0:T(8,128)} async-done(((f32[2048,4096]{1,0:T(8,128)}), f32[128,4096]{1,0:T(8,128)}) %reduce-scatter.16.cloned.1.call-update) | async-done | bytes 2097168 | tf_op jit(solution)/shard_map/reduce_scatter | solution.py:249
  962.4 40.0 all-gather.30.cloned.1.call-done
  1007.6 16.8 all-gather
  1025.2 18.1 all-gather.1
  1044.0 12.0 while.74
  1080.3 82.1 %all-reduce.18.cloned.1.call-done = f32[256,1536]{1,0:T(8,128)} async-done(((f32[256,1536]{1,0:T(8,128)}), f32[256,1536]{1,0:T(8,128)}) %all-reduce.18.cloned.1.call-update) | async-done | bytes 1572880 | tf_op jit(solution)/shard_map/psum | solution.py:313
  1165.6 97.5 %all-gather.36.cloned.1.call-done = bf16[1536,4096]{1,0:T(8,128)(2,1)} async-done(((bf16[96,4096]{1,0:T(8,128)(2,1)}), bf16[1536,4096]{1,0:T(8,128)(2,1)}) %all-gather.36.cloned.1.call-update) | async-done | bytes 12582928 | tf_op jit(solution)/shard_map/all_gather | solution.py:136
  1302.9 110.6 %all-reduce.20.cloned.1.call-done = f32[256,4096]{1,0:T(8,128)} async-done(((f32[256,4096]{1,0:T(8,128)}), f32[256,4096]{1,0:T(8,128)}) %all-reduce.20.cloned.1.call-update) | async-done | bytes 4194320 | tf_op jit(solution)/shard_map/psum | solution.py:350
  1424.9 10.2 convert_multiply_fusion
  1455.6 124.4 %all-gather.38.cloned.1.call-done = bf16[2048,4096]{1,0:T(8,128)(2,1)} async-done(((bf16[128,4096]{1,0:T(8,128)(2,1)}), bf16[2048,4096]{1,0:T(8,128)(2,1)}) %all-gather.38.cloned.1.call-update) | async-done | bytes 16777232 | tf_op jit(solution)/shard_map/all_gather | solution.py:422
  1580.0 28.2 multiply_convert_fusion
  1616.0 8.1 convolution_add_fusion
  1631.4 8.7 fusion.182
  1678.6 21.3 convolution_convert_fusion.3
  1702.0 33.7 reduce-scatter.20.cloned.1.call-done
  1735.8 10.0 convert_reduce_fusion
  1745.8 8.5 multiply_reduce_fusion.8
  1757.7 8.8 broadcast_in_dim.320
  1766.5 74.6 %while.75 = (s32[]{:T(128)}, f32[2048,2304]{0,1:T(8,128)}, s32[128]{0:T(128)}, s32[2048]{0:T(1024)S(1)}, bf16[2048,1152]{0,1:T(8,128)(2,1)}, /*index=5*/bf16[128...) while((s32[]{:T(128)}, f32[2048,2304]{0,1:T(8,128)}, ...), condition=%wide.region_34.35_spmd, body=%wide.region_33.34_spmd.sunk | while | flops 615710720 | bytes 56720128 | solution.py:97
  1849.8 12.3 fusion.77
  1862.1 12.5 all-reduce.22.cloned.1.call-done
  1877.3 10.6 fusion.168
  1887.9 9.2 fusion.187
  1905.1 45.1 %reduce-scatter.18.cloned.1.call-done = f32[16,4096]{1,0:T(8,128)} async-done(((f32[256,4096]{1,0:T(8,128)}), f32[16,4096]{1,0:T(8,128)}) %reduce-scatter.18.cloned.1.call-update) | async-done | bytes 262160 | tf_op jit(solution)/shard_map/reduce_scatter | solution.py:330
  1951.9 118.2 %reduce-scatter.24.cloned.1.call-done = f32[128,384]{1,0:T(8,128)} async-done(((f32[4096,384]{1,0:T(8,128)}), f32[128,384]{1,0:T(8,128)}) %reduce-scatter.24.cloned.1.call-update) | async-done | bytes 196624 | tf_op jit(solution)/shard_map/reduce_scatter | solution.py:511
  2071.9 12.3 fusion.127
  2084.1 235.1 %fusion.3 = f32[40,4304]{1,0:T(8,128)} fusion(f32[1152,4304]{1,0:T(8,128)} %fusion.127), kind=kCustom, calls=%all-reduce-scatter.3 | all-reduce-scatter fusion | flops 5509121 | bytes 20521472
  2334.4 53.1 %while.78 = (s32[]{:T(128)}, f32[128,1152]{0,1:T(8,128)}, bf16[2048,1152]{0,1:T(8,128)(2,1)}, s32[128]{0:T(128)}, s32[2048]{0:T(1024)S(1)}, /*index=5*/bf16[128,...) while((s32[]{:T(128)}, f32[128,1152]{0,1:T(8,128)}, ...), condition=%wide.region_32.33_spmd.clone, body=%wide.region_31.32_spmd.clone.sunk | while | flops 459636736 | bytes 19749580 | solution.py:97
  2387.5 11.3 fusion.165
  2407.2 18.2 concatenate.14
  2427.5 612.5 %all-reduce.24.cloned.1.call-done = (bf16[1152,896]{1,0:T(8,128)(2,1)}, bf16[1152,896]{1,0:T(8,128)(2,1)}, bf16[896,4096]{1,0:T(8,128)(2,1)}, bf16[4096,1024]{1,...) async-done(((bf16[1152,896]{1,0:T(8,128)(2,1)}, bf16[1152,896]{1,0:T(8,128)(2,1)}, bf16[896,4096]{1,0:T(8,128)(2,1)}, bf16[4096,1024]{1,0:T(8,128)(2,1)}, ...) | async-done | bytes 36634640 | tf_op jit(solution)/shard_map/psum | solution.py:516
  3046.9 9.0 convert_element_type.370
  3055.9 16.6 convert_element_type.380
  3072.5 12.5 convert_element_type.382
  3085.0 11.9 convert_element_type.384
  3096.9 142.3 %reduce-scatter.22.cloned.1.call-done = f32[128,2304]{0,1:T(8,128)} async-done(((f32[2048,2304]{0,1:T(8,128)}), f32[128,2304]{0,1:T(8,128)}) %reduce-scatter.22.cloned.1.call-update) | async-done | bytes 1179664 | tf_op jit(solution)/shard_map/reduce_scatter | solution.py:485
  3242.2 7.9 fusion.118
  3250.0 615.3 %fusion.170 = (f32[48,3456]{1,0:T(8,128)S(1)}, f32[48,1152]{1,0:T(8,128)S(1)}, f32[40,4304]{1,0:T(8,128)S(1)}) fusion(f32[1152,3456]{1,0:T(8,128)} %fusion.118, f32[1152,1152]{1,0:T(8,128)} %fusion.124, f32[1152,4304]{1,0:T(8,128)} %fusion.165), kind=kCustom, calls=%all-reduce-scatter.4 | all-reduce-scatter fusion | flops 12587010 | bytes 42639872
  3866.2 11.9 collective-permute-start.6
  3900.4 72.9 %all-reduce.25 = (f32[1152]{0:T(1024)}, f32[1152]{0:T(1024)}, f32[1152]{0:T(1024)}, f32[1152]{0:T(1024)}, f32[1152]{0:T(1024)}, /*index=5*/f32[1152]{0:T(1024)},...) all-reduce(f32[1152]{0:T(1024)S(1)} %get-tuple-element.968, ...), channel_id=1, replica_groups=mesh['grp'=2,'blk'=16] {'grp','blk'}, use_global_device_ids=true, to_apply=%region_39.40 | all-reduce | flops 46288 | bytes 321152 | tf_op jit(solution)/shard_map/psum | solution.py:523
  3994.0 10.1 collective-permute-done.11
  4004.2 25.9 collective-permute-start.9
  4034.8 18.2 collective-permute-start.4
  4064.9 14.9 concatenate.12
  4086.9 22.9 collective-permute-start.16
  4111.5 10.9 collective-permute-done.1
  4124.3 10.8 collective-permute-done
  4135.1 36.1 concatenate.11
  4173.3 17.5 concatenate.13
  (665 shorter events, 564.4 us)
Async XLA Ops:
  7.2 473.5 %copy-start = (bf16[1152,896]{1,0:T(8,128)(2,1)S(1)}, bf16[1152,896]{1,0:T(8,128)(2,1)}, u32[]{:S(2)}) copy-start(bf16[1152,896]{1,0:T(8,128)(2,1)} %param.56) | copy-start | bytes 6193156
  7.2 75.9 %all-gather.16.cloned.1.call-start = ((), (), s32[]{:S(2)}) async-start(), calls=%async_computation.7 | async-start | bytes 8460288 | tf_op jit(solution)/shard_map/all_gather | solution.py:129
  8.0 134.3 %all-gather.18.cloned.1.call-start = ((), (), s32[]{:S(2)}) async-start(), calls=%async_computation.8 | async-start | bytes 5013504 | tf_op jit(solution)/shard_map/all_gather | solution.py:143
  90.1 107.0 %all-gather.20.cloned.1.call-start = ((), (), s32[]{:S(2)}) async-start(), calls=%async_computation.9 | async-start | bytes 5013504 | tf_op jit(solution)/shard_map/all_gather | solution.py:142
  91.9 178.6 %all-gather.22.cloned.1.call-start = ((), (), s32[]{:S(2)}) async-start(), calls=%async_computation.10 | async-start | bytes 2820096 | tf_op jit(solution)/shard_map/all_gather | solution.py:130
  92.5 233.4 %all-gather.24.cloned.1.call-start = ((), (), s32[]{:S(2)}) async-start(), calls=%async_computation.11 | async-start | bytes 10653696 | tf_op jit(solution)/shard_map/all_gather | solution.py:131
  93.1 318.2 %all-gather.26.cloned.1.call-start = ((), (), s32[]{:S(2)}) async-start(), calls=%async_computation.12 | async-start | bytes 10653696 | tf_op jit(solution)/shard_map/all_gather | solution.py:132
  93.7 378.8 %all-gather.28.cloned.1.call-start = ((), (), s32[]{:S(2)}) async-start(), calls=%async_computation.13 | async-start | bytes 5013504 | tf_op jit(solution)/shard_map/all_gather | solution.py:244
  273.3 138.0 %copy-start.22 = (f32[128,1152]{1,0:T(8,128)}, f32[128,1152]{1,0:T(8,128)S(1)}, u32[]{:S(2)}) copy-start(f32[128,1152]{1,0:T(8,128)S(1)} %get-tuple-element.1110) | copy-start | bytes 1769476
  419.9 99.1 %all-gather.32.cloned.1.call-start = ((), (), s32[]{:S(2)}) async-start(), calls=%async_computation.16 | async-start | bytes 3342336 | tf_op jit(solution)/shard_map/all_gather | solution.py:134
  420.6 198.5 %all-gather.34.cloned.1.call-start = ((), (), s32[]{:S(2)}) async-start(), calls=%async_computation.17 | async-start | bytes 13369344 | tf_op jit(solution)/shard_map/all_gather | solution.py:133
  421.4 532.5 %reduce-scatter.16.cloned.1.call-start = ((), (), s32[]{:S(2)}) async-start(), calls=%async_computation.14 | async-start | bytes 35651584 | tf_op jit(solution)/shard_map/reduce_scatter | solution.py:249
  512.4 490.0 %all-gather.30.cloned.1.call-start = ((), (), s32[]{:S(2)}) async-start(), calls=%async_computation.15 | async-start | bytes 3342336 | tf_op jit(solution)/shard_map/all_gather | solution.py:135
  513.1 649.2 %all-reduce.18.cloned.1.call-start = ((), (), s32[]{:S(2)}) async-start(), calls=%async_computation.18 | async-start | bytes 3145728 | tf_op jit(solution)/shard_map/psum | solution.py:313
  513.6 112.5 %copy-start.127 = (f32[64]{0:T(128)}, f32[64]{0:T(128)S(1)}, u32[]{:S(2)}) copy-start(f32[64]{0:T(128)S(1)} %multiply_reduce_fusion.7) | copy-start | bytes 772
  514.3 446.2 %copy-start.122 = (pred[4,128]{1,0:T(4,128)(4,1)}, pred[4,128]{1,0:T(4,128)(4,1)S(1)}, u32[]{:S(2)}) copy-start(pred[4,128]{1,0:T(4,128)(4,1)S(1)} %iota_compare_fusion) | copy-start | bytes 1540
  514.3 104.9 %copy-start.92 = (f32[64]{0:T(128)}, f32[64]{0:T(128)S(1)}, u32[]{:S(2)}) copy-start(f32[64]{0:T(128)S(1)} %fusion.154) | copy-start | bytes 772
  626.1 329.8 %copy-start.88 = (f32[4096]{0:T(1024)S(1)}, f32[4096]{0:T(1024)}, u32[]{:S(2)}) copy-start(f32[4096]{0:T(1024)} %param.58) | copy-start | bytes 49156
  626.8 329.1 %copy-start.91 = (f32[4,4,64]{2,1,0:T(4,128)}, f32[4,4,64]{2,1,0:T(4,128)S(1)}, u32[]{:S(2)}) copy-start(f32[4,4,64]{2,1,0:T(4,128)S(1)} %get-tuple-element.1113) | copy-start | bytes 12292
  1065.9 197.2 %all-gather.36.cloned.1.call-start = ((), (), s32[]{:S(2)}) async-start(), calls=%async_computation.19 | async-start | bytes 13369344 | tf_op jit(solution)/shard_map/all_gather | solution.py:136
  1066.6 346.8 %all-reduce.20.cloned.1.call-start = ((), (), s32[]{:S(2)}) async-start(), calls=%async_computation.21 | async-start | bytes 8388608 | tf_op jit(solution)/shard_map/psum | solution.py:350
  1302.6 277.4 %all-gather.38.cloned.1.call-start = ((), (), s32[]{:S(2)}) async-start(), calls=%async_computation.22 | async-start | bytes 17825792 | tf_op jit(solution)/shard_map/all_gather | solution.py:422
  1302.9 116.1 %copy-start.112 = (pred[256]{0:T(512)(128)(4,1)}, pred[256]{0:T(512)(128)(4,1)S(1)}, u32[]{:S(2)}) copy-start(pred[256]{0:T(512)(128)(4,1)S(1)} %fusion.149) | copy-start | bytes 772
  1455.6 280.2 %reduce-scatter.20.cloned.1.call-start = ((), (), s32[]{:S(2)}) async-start(), calls=%async_computation.23 | async-start | bytes 10027008 | tf_op jit(solution)/shard_map/reduce_scatter | solution.py:432
  1624.1 250.4 %all-reduce.22.cloned.1.call-start = ((), (), s32[]{:S(2)}) async-start(), calls=%async_computation.28 | async-start | bytes 3407872 | tf_op jit(solution)/shard_map/psum | solution.py:523
  1631.3 318.9 %reduce-scatter.18.cloned.1.call-start = ((), (), s32[]{:S(2)}) async-start(), calls=%async_computation.20 | async-start | bytes 4456448 | tf_op jit(solution)/shard_map/reduce_scatter | solution.py:330
  1640.1 430.0 %reduce-scatter.24.cloned.1.call-start = ((), (), s32[]{:S(2)}) async-start(), calls=%async_computation.25 | async-start | bytes 6488064 | tf_op jit(solution)/shard_map/reduce_scatter | solution.py:511
  1645.3 1394.7 %all-reduce.24.cloned.1.call-start = ((), (), s32[]{:S(2)}) async-start(), calls=%async_computation.29 | async-start | bytes 73269248 | tf_op jit(solution)/shard_map/psum | solution.py:516
  1699.9 1539.3 %reduce-scatter.22.cloned.1.call-start = ((), (), s32[]{:S(2)}) async-start(), calls=%async_computation.24 | async-start | bytes 20054016 | tf_op jit(solution)/shard_map/reduce_scatter | solution.py:485
  1841.7 2191.0 %reduce-scatter.26.cloned.1.call-start = ((), (), s32[]{:S(2)}) async-start(), calls=%async_computation.26 | async-start | bytes 6488064 | tf_op jit(solution)/shard_map/reduce_scatter | solution.py:512
  1846.2 2346.7 %reduce-scatter.28.cloned.1.call-start = ((), (), s32[]{:S(2)}) async-start(), calls=%async_computation.27 | async-start | bytes 25952256 | tf_op jit(solution)/shard_map/reduce_scatter | solution.py:513
  1901.3 170.6 %copy-start.47 = (f32[128,1152]{1,0:T(8,128)S(1)}, f32[128,1152]{1,0:T(8,128)}, u32[]{:S(2)}) copy-start(f32[128,1152]{1,0:T(8,128)} %reduce-scatter.20.cloned.1.call-done) | copy-start | bytes 1769476
  2084.1 250.2 %copy-start.117 = (f32[16,128]{1,0:T(8,128)S(1)}, f32[16,128]{1,0:T(8,128)}, u32[]{:S(2)}) copy-start(f32[16,128]{1,0:T(8,128)} %copy-done.116) | copy-start | bytes 24580
  2319.3 87.9 %collective-permute-start.22 = (f32[40,4304]{1,0:T(8,128)}, f32[40,4304]{1,0:T(8,128)}, u32[]{:S(2)}, u32[]{:S(2)}) collective-permute-start(f32[40,4304]{1,0:T(8,128)} %fusion.3), channel_id=1, source_target_pairs={{0,3},{1,4},{2,5},{3,6},{4,7},{5,8},{6,9},{7,10},{8,11},{9,12},{10... | collective-permute-start | bytes 2065928
  2325.1 82.1 %collective-permute-start.21 = (f32[40,4304]{1,0:T(8,128)}, f32[40,4304]{1,0:T(8,128)}, u32[]{:S(2)}, u32[]{:S(2)}) collective-permute-start(f32[40,4304]{1,0:T(8,128)} %fusion.3), channel_id=1, source_target_pairs={{0,2},{1,3},{2,4},{3,5},{4,6},{5,7},{6,8},{7,9},{8,10},{9,11},{10,... | collective-permute-start | bytes 2065928
  2331.8 75.4 %collective-permute-start.20 = (f32[40,4304]{1,0:T(8,128)}, f32[40,4304]{1,0:T(8,128)}, u32[]{:S(2)}, u32[]{:S(2)}) collective-permute-start(f32[40,4304]{1,0:T(8,128)} %fusion.3), channel_id=1, source_target_pairs={{0,1},{1,2},{2,3},{3,4},{4,5},{5,6},{6,7},{7,8},{8,9},{9,10},{10,1... | collective-permute-start | bytes 2065928
  2399.8 7.4 collective-permute-start.23
  2407.2 834.2 %copy-start.49 = (bf16[128,1152]{0,1:T(8,128)(2,1)}, bf16[128,1152]{0,1:T(8,128)(2,1)S(1)}, u32[]{:S(2)}) copy-start(bf16[128,1152]{0,1:T(8,128)(2,1)S(1)} %get-tuple-element.1089) | copy-start | bytes 884740
  3085.0 157.1 %copy-start.25 = (bf16[128,1152]{1,0:T(8,128)(2,1)S(1)}, bf16[128,1152]{1,0:T(8,128)(2,1)}, u32[]{:S(2)}) copy-start(bf16[128,1152]{1,0:T(8,128)(2,1)} %param.40) | copy-start | bytes 884740
  3085.0 157.1 %copy-start.65 = (f32[1152]{0:T(1024)S(1)}, f32[1152]{0:T(1024)}, u32[]{:S(2)}) copy-start(f32[1152]{0:T(1024)} %param.42) | copy-start | bytes 13828
  3085.0 157.1 %copy-start.86 = (f32[1152]{0:T(1024)S(1)}, f32[1152]{0:T(1024)}, u32[]{:S(2)}) copy-start(f32[1152]{0:T(1024)} %param.43) | copy-start | bytes 13828
  3085.0 157.1 %copy-start.100 = (f32[128]{0:T(128)S(1)}, f32[128]{0:T(128)}, u32[]{:S(2)}) copy-start(f32[128]{0:T(128)} %copy-done.99) | copy-start | bytes 1540
  3085.0 157.1 %copy-start.106 = (f32[128]{0:T(128)S(1)}, f32[128]{0:T(128)}, u32[]{:S(2)}) copy-start(f32[128]{0:T(128)} %copy-done.105) | copy-start | bytes 1540
  3250.0 641.9 %copy-start.50 = (bf16[128,1152]{0,1:T(8,128)(2,1)S(1)}, bf16[128,1152]{0,1:T(8,128)(2,1)}, u32[]{:S(2)}) copy-start(bf16[128,1152]{0,1:T(8,128)(2,1)} %copy-done.49) | copy-start | bytes 884740
  3866.2 192.5 %collective-permute-start.6 = (f32[48,3456]{1,0:T(8,128)S(1)}, f32[48,3456]{1,0:T(8,128)}, u32[]{:S(2)}, u32[]{:S(2)}) collective-permute-start(f32[48,3456]{1,0:T(8,128)S(1)} %get-tuple-element.1077), channel_id=1, source_target_pairs={{0,7},{1,8},{2,9},{3,10},{4,11},{5,12},{6,13},{7,14},{8,15},{9,16}... | collective-permute-start | bytes 1990664
  3878.1 104.3 %collective-permute-start.14 = (f32[48,1152]{1,0:T(8,128)S(1)}, f32[48,1152]{1,0:T(8,128)}, u32[]{:S(2)}, u32[]{:S(2)}) collective-permute-start(f32[48,1152]{1,0:T(8,128)S(1)} %get-tuple-element.1078), channel_id=1, source_target_pairs={{0,7},{1,8},{2,9},{3,10},{4,11},{5,12},{6,13},{7,14},{8,15},{9,16}... | collective-permute-start | bytes 663560
  3880.1 106.4 %collective-permute-start.13 = (f32[48,1152]{1,0:T(8,128)S(1)}, f32[48,1152]{1,0:T(8,128)}, u32[]{:S(2)}, u32[]{:S(2)}) collective-permute-start(f32[48,1152]{1,0:T(8,128)S(1)} %get-tuple-element.1078), channel_id=1, source_target_pairs={{0,6},{1,7},{2,8},{3,9},{4,10},{5,11},{6,12},{7,13},{8,14},{9,15},... | collective-permute-start | bytes 663560
  3887.9 100.5 %collective-permute-start.12 = (f32[48,1152]{1,0:T(8,128)S(1)}, f32[48,1152]{1,0:T(8,128)}, u32[]{:S(2)}, u32[]{:S(2)}) collective-permute-start(f32[48,1152]{1,0:T(8,128)S(1)} %get-tuple-element.1078), channel_id=1, source_target_pairs={{0,5},{1,6},{2,7},{3,8},{4,9},{5,10},{6,11},{7,12},{8,13},{9,14},{... | collective-permute-start | bytes 663560
  3889.8 89.7 %collective-permute-start.15 = (f32[36,1152]{1,0:T(8,128)S(1)}, f32[36,1152]{1,0:T(8,128)}, u32[]{:S(2)}, u32[]{:S(2)}) collective-permute-start(f32[36,1152]{1,0:T(8,128)S(1)} %slice.40), channel_id=1, source_target_pairs={{0,8},{1,9},{2,10},{3,11},{4,12},{5,13},{6,14},{7,15},{8,16},{9,17... | collective-permute-start | bytes 497672
  3979.5 81.2 %collective-permute-start.5 = (f32[48,3456]{1,0:T(8,128)S(1)}, f32[48,3456]{1,0:T(8,128)}, u32[]{:S(2)}, u32[]{:S(2)}) collective-permute-start(f32[48,3456]{1,0:T(8,128)S(1)} %get-tuple-element.1077), channel_id=1, source_target_pairs={{0,6},{1,7},{2,8},{3,9},{4,10},{5,11},{6,12},{7,13},{8,14},{9,15},... | collective-permute-start | bytes 1990664
  3982.4 21.8 collective-permute-start.11
  3986.5 43.6 %collective-permute-start.10 = (f32[48,1152]{1,0:T(8,128)S(1)}, f32[48,1152]{1,0:T(8,128)S(1)}, u32[]{:S(2)}, u32[]{:S(2)}) collective-permute-start(f32[48,1152]{1,0:T(8,128)S(1)} %get-tuple-element.1078), channel_id=1, source_target_pairs={{0,3},{1,4},{2,5},{3,6},{4,7},{5,8},{6,9},{7,10},{8,11},{9,12},{10... | collective-permute-start | bytes 663560
  3988.4 67.3 %collective-permute-start.7 = (f32[36,3456]{1,0:T(8,128)}, f32[36,3456]{1,0:T(8,128)}, u32[]{:S(2)}, u32[]{:S(2)}) collective-permute-start(f32[36,3456]{1,0:T(8,128)} %slice.39), channel_id=1, source_target_pairs={{0,8},{1,9},{2,10},{3,11},{4,12},{5,13},{6,14},{7,15},{8,16},{9,17... | collective-permute-start | bytes 1493000
  4004.2 30.6 collective-permute-start.9
  4030.8 22.2 collective-permute-start.8
  4034.8 45.0 %collective-permute-start.4 = (f32[48,3456]{1,0:T(8,128)S(1)}, f32[48,3456]{1,0:T(8,128)S(1)}, u32[]{:S(2)}, u32[]{:S(2)}) collective-permute-start(f32[48,3456]{1,0:T(8,128)S(1)} %get-tuple-element.1077), channel_id=1, source_target_pairs={{0,5},{1,6},{2,7},{3,8},{4,9},{5,10},{6,11},{7,12},{8,13},{9,14},{... | collective-permute-start | bytes 1990664
  4053.0 29.6 collective-permute-start.3
  4055.8 31.2 collective-permute-start.2
  4058.6 63.7 %collective-permute-start.1 = (f32[48,3456]{1,0:T(8,128)S(1)}, f32[48,3456]{1,0:T(8,128)}, u32[]{:S(2)}, u32[]{:S(2)}) collective-permute-start(f32[48,3456]{1,0:T(8,128)S(1)} %get-tuple-element.1077), channel_id=1, source_target_pairs={{0,2},{1,3},{2,4},{3,5},{4,6},{5,7},{6,8},{7,9},{8,10},{9,11},{10,... | collective-permute-start | bytes 1990664
  4060.7 74.4 %collective-permute-start = (f32[48,3456]{1,0:T(8,128)S(1)}, f32[48,3456]{1,0:T(8,128)}, u32[]{:S(2)}, u32[]{:S(2)}) collective-permute-start(f32[48,3456]{1,0:T(8,128)S(1)} %get-tuple-element.1077), channel_id=1, source_target_pairs={{0,1},{1,2},{2,3},{3,4},{4,5},{5,6},{6,7},{7,8},{8,9},{9,10},{10,1... | collective-permute-start | bytes 1990664
  4079.9 93.4 %collective-permute-start.18 = (f32[40,4304]{1,0:T(8,128)S(1)}, f32[40,4304]{1,0:T(8,128)}, u32[]{:S(2)}, u32[]{:S(2)}) collective-permute-start(f32[40,4304]{1,0:T(8,128)S(1)} %get-tuple-element.1079), channel_id=1, source_target_pairs={{0,3},{1,4},{2,5},{3,6},{4,7},{5,8},{6,9},{7,10},{8,11},{9,12},{10... | collective-permute-start | bytes 2065928
  4082.6 90.8 %collective-permute-start.17 = (f32[40,4304]{1,0:T(8,128)S(1)}, f32[40,4304]{1,0:T(8,128)}, u32[]{:S(2)}, u32[]{:S(2)}) collective-permute-start(f32[40,4304]{1,0:T(8,128)S(1)} %get-tuple-element.1079), channel_id=1, source_target_pairs={{0,2},{1,3},{2,4},{3,5},{4,6},{5,7},{6,8},{7,9},{8,10},{9,11},{10,... | collective-permute-start | bytes 2065928
  4086.9 86.4 %collective-permute-start.16 = (f32[40,4304]{1,0:T(8,128)S(1)}, f32[40,4304]{1,0:T(8,128)}, u32[]{:S(2)}, u32[]{:S(2)}) collective-permute-start(f32[40,4304]{1,0:T(8,128)S(1)} %get-tuple-element.1079), channel_id=1, source_target_pairs={{0,1},{1,2},{2,3},{3,4},{4,5},{5,6},{6,7},{7,8},{8,9},{9,10},{10,1... | collective-permute-start | bytes 2065928
  4122.4 51.0 %collective-permute-start.19 = (f32[4,4304]{1,0:T(4,128)S(1)}, f32[4,4304]{1,0:T(4,128)S(1)}, u32[]{:S(2)}, u32[]{:S(2)}) collective-permute-start(f32[4,4304]{1,0:T(4,128)S(1)} %copy-done.96), channel_id=1, source_target_pairs={{0,4},{1,5},{2,6},{3,7},{4,8},{5,9},{6,10},{7,11},{8,12},{9,13},{1... | collective-permute-start | bytes 206600
  (140 other events, 2297.3 us)
Sparse Core Ops, SparseCore 0:
  10.2 72.8 all-gather.15
  90.2 52.0 all-gather.17
  145.1 51.9 all-gather.19
  199.1 41.7 all-gather.21
  242.9 83.0 all-gather.23
  328.0 83.2 all-gather.25
  420.0 52.4 all-gather.27
  474.8 44.1 all-gather.31
  521.3 97.8 all-gather.33
  623.2 330.5 reduce-scatter.15
  956.1 46.2 all-gather.29
  1066.0 96.2 all-reduce.17
  1164.6 98.4 all-gather.35
  1302.7 110.7 all-reduce.19
  1455.7 124.2 all-gather.37
  1624.2 111.4 reduce-scatter.19
  1741.8 132.7 all-reduce.21
  1878.8 71.3 reduce-scatter.17
  1955.9 114.2 reduce-scatter.23
  2073.8 966.1 all-reduce.23
  3044.7 194.5 reduce-scatter.21
  3245.8 159.6 reduce-scatter.25
  3412.5 374.4 reduce-scatter.27
where the time goes:
time: 4210 us; the launch traced here: 4200 us
  waiting for transfers between devices  2220 us (53%)
  blocking collectives  975 us (23%)
  matrix products  458 us (11%)
  local copies, waits for them, and re-layouts  211 us (5%)
  other arithmetic  179 us (4%)
  starting transfers between devices  144 us (3%)
    unnamed x2, blocking collectives  850 us
    psum x1, waiting for transfers between devices, on_device(): lax.psum(grad_bridge_gate.astype(jnp.bfloat16), 'grp').astype(jnp.float32)  613 us
    reduce_scatter x1, waiting for transfers between devices, on_device(): lax.psum_scatter(mat_times(rows_at(bridge_hidden, jnp.int32(0), local_row...  326 us
    reduce_scatter x1, waiting for transfers between devices, on_device(): lax.psum_scatter(over_blocks(local_rows * lax.axis_size('blk'), step, jnp...  142 us
    unnamed x24, starting transfers between devices  142 us
    unnamed x314, local copies, waits for them, and re-layouts  132 us
    all_gather x1, waiting for transfers between devices, on_device(): lax.all_gather(context_grad.astype(jnp.bfloat16), 'blk', axis=0, tiled=True)  124 us
    reduce_scatter x1, waiting for transfers between devices, on_device(): lax.psum_scatter(grad_key_part, ('grp', 'blk'), scatter_dimension=0, tile...  118 us
  transfers between devices with their start and end apart: 47, of which 25 were waited for; matrix products, arithmetic and copies ran while one was open for 36% of the time, Pallas kernels for 0%

commit v1 on v0

v1 whole, which is shorter than its diff:
```python
import functools

import jax
import jax.numpy as jnp
from jax import lax
from jax.experimental import pallas as pl
from jax.experimental.pallas import tpu as pltpu
from jax.sharding import PartitionSpec as P

HEADS = 16
HEAD = 72
LATENTS = 64
P_HEADS = 16
P_KV = 4
P_HEAD = 96
LANES = 128

masked_score = -1e30
norm_eps = 1e-06
vmem_bytes = 56 * 2**20
low = jnp.bfloat16
wide = jnp.float32


def layer_norm(values, gain, bias):
    center = values - jnp.mean(values, axis=-1, keepdims=True)
    spread = jnp.mean(center * center, axis=-1, keepdims=True)
    return center * lax.rsqrt(spread + norm_eps) * gain + bias


def rms_norm(values, gain):
    return values * lax.rsqrt(jnp.mean(values * values, axis=-1, keepdims=True) + norm_eps) * gain


def smooth_gate(values):
    return jax.nn.gelu(values, approximate=True)


def swiglu(gate, up):
    return jax.nn.silu(gate) * up


def mat_times(left, right):
    return jnp.dot(left, right, preferred_element_type=wide)


def contract(left, right, left_dim, right_dim):
    return lax.dot_general(
        left, right, (((left_dim,), (right_dim,)), ((), ())), preferred_element_type=wide
    )


def mat_times_t(left, right):
    return contract(left, right, 1, 1)


def outer_sum(left, right):
    return contract(left, right, 0, 0)


def rows_at(array, first, width, axis=0):
    return lax.dynamic_slice_in_dim(array, first, width, axis)


def gather(array):
    return lax.all_gather(array, "blk", axis=0, tiled=True)


def scatter_sum(array):
    return lax.psum_scatter(array.astype(low), "blk", scatter_dimension=0, tiled=True).astype(wide)


def swap_pieces(pieces):
    flat = pieces.reshape((-1,) + pieces.shape[2:])
    return lax.all_to_all(flat, "blk", 0, 0, tiled=True)


def attend_kernel(query_ref, key_ref, value_ref, row_ids_ref, col_ids_ref, out_ref):
    scores = mat_times_t(query_ref[...], key_ref[...]) * HEAD ** (-0.5)
    mask = row_ids_ref[...] == col_ids_ref[...]
    scores = jnp.where(mask, scores, masked_score)
    top = jnp.max(scores, axis=-1, keepdims=True)
    weights = jnp.exp(scores - top)
    total = jnp.sum(weights, axis=-1, keepdims=True)
    probs = (weights * (1.0 / total)).astype(low)
    out_ref[...] = mat_times(probs, value_ref[...]).astype(low)


def query_rows_for(rows):
    return 256 if rows <= 2048 else 64


def attend(heads, row_ids, col_ids):
    rows = heads.shape[0]
    width = query_rows_for(rows)
    return pl.pallas_call(
        attend_kernel,
        out_shape=jax.ShapeDtypeStruct((rows, LANES), low),
        grid=(rows // width,),
        in_specs=[
            pl.BlockSpec((width, LANES), lambda i: (i, 0)),
            pl.BlockSpec((rows, LANES), lambda i: (0, 1)),
            pl.BlockSpec((rows, LANES), lambda i: (0, 2)),
            pl.BlockSpec((width, 1), lambda i: (i, 0)),
            pl.BlockSpec((1, rows), lambda i: (0, 0)),
        ],
        out_specs=pl.BlockSpec((width, LANES), lambda i: (i, 0)),
        compiler_params=pltpu.CompilerParams(vmem_limit_bytes=vmem_bytes),
        name="vision_attend",
    )(heads, heads, heads, row_ids, col_ids)


def attend_back_kernel(
    query_ref, key_ref, value_ref, grad_ref, row_ids_ref, col_ids_ref,
    query_grad_ref, key_grad_ref, value_grad_ref, key_sum, value_sum,
):
    step = pl.program_id(0)

    @pl.when(step == 0)
    def _():
        key_sum[...] = jnp.zeros_like(key_sum)
        value_sum[...] = jnp.zeros_like(value_sum)

    queries = query_ref[...]
    grads = grad_ref[...]
    scores = mat_times_t(key_ref[...], queries) * HEAD ** (-0.5)
    mask = row_ids_ref[...] == col_ids_ref[...]
    scores = jnp.where(mask, scores, masked_score)
    top = jnp.max(scores, axis=0, keepdims=True)
    weights = jnp.exp(scores - top)
    total = jnp.sum(weights, axis=0, keepdims=True)
    probs = weights * (1.0 / total)
    dprob = mat_times_t(value_ref[...], grads)
    delta = jnp.sum(probs * dprob, axis=0, keepdims=True)
    score_grad = (probs * (dprob - delta)).astype(low)
    key_sum[...] += mat_times(score_grad, queries)
    value_sum[...] += mat_times(probs.astype(low), grads)
    query_grad_ref[...] = (outer_sum(score_grad, key_ref[...]) * HEAD ** (-0.5)).astype(low)

    @pl.when(step == pl.num_programs(0) - 1)
    def _():
        key_grad_ref[...] = (key_sum[...] * HEAD ** (-0.5)).astype(low)
        value_grad_ref[...] = value_sum[...].astype(low)


def attend_back(heads, grads, row_ids, col_ids):
    rows = heads.shape[0]
    width = query_rows_for(rows)
    return pl.pallas_call(
        attend_back_kernel,
        out_shape=[jax.ShapeDtypeStruct((rows, LANES), low)] * 3,
        grid=(rows // width,),
        in_specs=[
            pl.BlockSpec((width, LANES), lambda i: (i, 0)),
            pl.BlockSpec((rows, LANES), lambda i: (0, 1)),
            pl.BlockSpec((rows, LANES), lambda i: (0, 2)),
            pl.BlockSpec((width, LANES), lambda i: (i, 0)),
            pl.BlockSpec((rows, 1), lambda i: (0, 0)),
            pl.BlockSpec((1, width), lambda i: (0, i)) if width % LANES == 0
            else pl.BlockSpec((None, 1, width), lambda i: (i, 0, 0)),
        ],
        out_specs=[
            pl.BlockSpec((width, LANES), lambda i: (i, 0)),
            pl.BlockSpec((rows, LANES), lambda i: (0, 0)),
            pl.BlockSpec((rows, LANES), lambda i: (0, 0)),
        ],
        scratch_shapes=[pltpu.VMEM((rows, LANES), wide)] * 2,
        compiler_params=pltpu.CompilerParams(vmem_limit_bytes=vmem_bytes),
        name="vision_attend_back",
    )(
        heads, heads, heads, grads, row_ids,
        col_ids if width % LANES == 0 else col_ids.reshape(rows // width, 1, width),
    )


def image_probs(scores, self_scores, mask):
    scores = jnp.where(mask, scores, masked_score)
    top = jnp.maximum(
        jnp.max(scores, axis=-1, keepdims=True), jnp.max(self_scores, axis=-1, keepdims=True)
    )
    weights = jnp.where(mask, jnp.exp(scores - top), 0.0)
    self_weights = jnp.exp(self_scores - top)
    total = jnp.sum(weights, axis=-1, keepdims=True) + jnp.sum(
        self_weights, axis=-1, keepdims=True
    )
    scale = 1.0 / total
    return weights * scale, self_weights * scale


def resample_kernel(
    query_ref, key_ref, value_ref, self_key_ref, self_value_ref, ids_ref, out_ref, *, images
):
    queries = query_ref[...]
    scores = mat_times_t(queries, key_ref[...]) * P_HEAD ** (-0.5)
    self_scores = mat_times_t(queries, self_key_ref[...]) * P_HEAD ** (-0.5)
    for image in range(images):
        probs, self_probs = image_probs(scores, self_scores, ids_ref[...] == image)
        mixed = mat_times(probs.astype(low), value_ref[...])
        mixed += mat_times(self_probs.astype(low), self_value_ref[...])
        out_ref[pl.ds(image * LATENTS, LATENTS), :] = mixed.astype(low)


def resample(queries, keys, values, self_keys, self_values, ids, images):
    return pl.pallas_call(
        functools.partial(resample_kernel, images=images),
        out_shape=jax.ShapeDtypeStruct((images * LATENTS, LANES), low),
        compiler_params=pltpu.CompilerParams(vmem_limit_bytes=vmem_bytes),
        name="resampler_attend",
    )(queries, keys, values, self_keys, self_values, ids)


def resample_back_kernel(
    query_ref, key_ref, value_ref, self_key_ref, self_value_ref, ids_ref, grad_ref,
    query_grad_ref, key_grad_ref, value_grad_ref, self_key_grad_ref, self_value_grad_ref,
    *, images,
):
    queries = query_ref[...]
    scale = P_HEAD ** (-0.5)
    scores = mat_times_t(queries, key_ref[...]) * scale
    self_scores = mat_times_t(queries, self_key_ref[...]) * scale
    for image in range(images):
        probs, self_probs = image_probs(scores, self_scores, ids_ref[...] == image)
        grads = grad_ref[pl.ds(image * LATENTS, LATENTS), :]
        dprob = mat_times_t(grads, value_ref[...])
        self_dprob = mat_times_t(grads, self_value_ref[...])
        delta = jnp.sum(probs * dprob, axis=-1, keepdims=True) + jnp.sum(
            self_probs * self_dprob, axis=-1, keepdims=True
        )
        score_grad = (probs * (dprob - delta)).astype(low)
        self_score_grad = (self_probs * (self_dprob - delta)).astype(low)
        terms = (
            mat_times(score_grad, key_ref[...]) + mat_times(self_score_grad, self_key_ref[...]),
            outer_sum(score_grad, queries),
            outer_sum(probs.astype(low), grads),
            outer_sum(self_score_grad, queries),
            outer_sum(self_probs.astype(low), grads),
        )
        refs = (
            query_grad_ref, key_grad_ref, value_grad_ref, self_key_grad_ref, self_value_grad_ref
        )
        for ref, term in zip(refs, terms):
            if image == 0:
                ref[...] = term
            else:
                ref[...] += term


def resample_back(queries, keys, values, self_keys, self_values, ids, grads, images):
    rows = keys.shape[0]
    shapes = [(LATENTS, LANES), (rows, LANES), (rows, LANES), (LATENTS, LANES), (LATENTS, LANES)]
    return pl.pallas_call(
        functools.partial(resample_back_kernel, images=images),
        out_shape=[jax.ShapeDtypeStruct(shape, wide) for shape in shapes],
        compiler_params=pltpu.CompilerParams(vmem_limit_bytes=vmem_bytes),
        name="resampler_attend_back",
    )(queries, keys, values, self_keys, self_values, ids, grads)


def lane_pad(array):
    gap = [(0, 0)] * (array.ndim - 1) + [(0, LANES - array.shape[-1])]
    return jnp.pad(array, gap)


def on_device(
    tokens, segment_ids, ln1_gain, ln1_bias, qkv_weight, q_bias, v_bias, out_weight, out_bias,
    ln2_gain, ln2_bias, fc1_weight, fc1_bias, fc2_weight, fc2_bias, bridge_gate, bridge_up,
    bridge_down, context_gain, latents, latent_gain, query_weight, key_weight, value_weight,
    mixer_weight, post_gain, latent_gate, latent_up, latent_down, cotangent,
):
    blocks = lax.axis_size("blk")
    planes = lax.axis_size("grp")
    me = lax.axis_index("blk")
    plane = lax.axis_index("grp")
    rows, features = tokens.shape
    pack_rows = rows * blocks
    hidden_units = fc1_weight.shape[1]
    unit_share = -(-hidden_units // blocks)
    model = latents.shape[1]
    model_share = query_weight.shape[0]
    lat_rows = cotangent.shape[0]
    lat_own = lat_rows // blocks
    images = lat_rows // LATENTS
    copies = blocks // HEADS
    head = me // copies
    part = me % copies
    kv_head = head // (P_HEADS // P_KV)

    def other_plane(array, step=1):
        return lax.ppermute(array, "grp", [(k, (k + step) % planes) for k in range(planes)])

    def both_planes(array):
        pieces = [array] + [other_plane(array, step) for step in range(1, planes)]
        return jnp.concatenate(
            [
                functools.reduce(
                    lambda held, step: jnp.where((plane - step) % planes == k, pieces[step], held),
                    range(1, planes),
                    pieces[0],
                )
                for k in range(planes)
            ],
            axis=0,
        )

    def plane_sum(array):
        mine = array.astype(low)
        total = mine.astype(wide)
        for step in range(1, planes):
            total = total + other_plane(mine, step).astype(wide)
        return total

    def to_columns(weight):
        padded = jnp.pad(weight, ((0, 0), (0, unit_share * blocks - weight.shape[1])))
        pieces = padded.reshape(weight.shape[0], blocks, unit_share)
        return swap_pieces(jnp.transpose(pieces, (1, 0, 2)))

    def share_rows(matrix):
        width = matrix.shape[0] // planes
        total = None
        for step in range(planes):
            piece = rows_at(matrix, (plane + step) % planes * width, width).astype(low)
            pairs = [
                (k * blocks + j, planes * j + (k + step) % planes)
                for k in range(planes)
                for j in range(blocks)
            ]
            arrived = lax.ppermute(piece, ("grp", "blk"), pairs).astype(wide)
            total = arrived if total is None else total + arrived
        return total

    def share_columns(matrix):
        width = matrix.shape[0] // planes
        total = rows_at(matrix, plane * width, width)
        for step in range(1, planes):
            piece = rows_at(matrix, (plane + step) % planes * width, width)
            total = total + other_plane(piece.astype(low), step).astype(wide)
        arrived = swap_pieces(total.astype(low).reshape(blocks, width // blocks, -1))
        return arrived.reshape(blocks, width // blocks, -1).astype(wide)

    head_pieces = lane_pad(qkv_weight.reshape(-1, 3, HEADS, HEAD))
    head_pieces = jnp.transpose(head_pieces, (2, 0, 1, 3)).reshape(HEADS, -1, 3 * LANES)
    head_weight = swap_pieces(jnp.repeat(head_pieces, copies, axis=0))
    fc1_own = to_columns(fc1_weight)
    fc2_own = to_columns(fc2_weight)
    mixer_pieces = jnp.transpose(
        mixer_weight.reshape(-1, blocks, model // blocks), (1, 0, 2)
    )
    mixer_own = swap_pieces(mixer_pieces)
    out_full = gather(out_weight)
    pair_weight = gather(jnp.concatenate([key_weight, value_weight], axis=1))
    fc1_bias_own = rows_at(
        jnp.pad(fc1_bias, (0, unit_share * blocks - hidden_units)), me * unit_share, unit_share
    )
    head_bias = jnp.concatenate(
        [
            lane_pad(rows_at(q_bias, head * HEAD, HEAD)),
            jnp.zeros((LANES,), wide),
            lane_pad(rows_at(v_bias, head * HEAD, HEAD)),
        ]
    )

    inputs = tokens.astype(wide)
    normed, first_norm_back = jax.vjp(layer_norm, inputs, ln1_gain, ln1_bias)
    first_rows = gather(normed.astype(low))
    all_ids = gather(segment_ids)
    row_ids = all_ids[:, None]
    col_ids = all_ids[None, :]
    heads = (mat_times(first_rows, head_weight) + head_bias).astype(low)
    attended_head = attend(heads, row_ids, col_ids)
    attended_pieces = swap_pieces(attended_head[:, :HEAD].reshape(blocks, rows, HEAD))
    attended_pieces = attended_pieces.reshape(blocks, rows, HEAD)[::copies]
    attended = jnp.transpose(attended_pieces, (1, 0, 2)).reshape(rows, features)
    hidden_state = inputs + mat_times(attended, out_full) + out_bias

    second, second_norm_back = jax.vjp(layer_norm, hidden_state, ln2_gain, ln2_bias)
    second_rows = gather(second.astype(low))
    pre = mat_times(second_rows, fc1_own) + fc1_bias_own
    act, gate_back = jax.vjp(smooth_gate, pre)
    act_low = act.astype(low)
    encoded = hidden_state + scatter_sum(mat_times_t(act_low, fc2_own)) + fc2_bias

    bridge_rows = gather(encoded.astype(low))
    bridge_act, bridge_act_back = jax.vjp(
        swiglu, mat_times(bridge_rows, bridge_gate), mat_times(bridge_rows, bridge_up)
    )
    bridge_hidden = bridge_act.astype(low)
    context = scatter_sum(mat_times(bridge_hidden, bridge_down))

    context_normed, context_norm_back = jax.vjp(rms_norm, context, context_gain)
    context_in = context_normed.astype(low)
    patch_pairs = gather(mat_times(context_in, pair_weight).astype(low))
    latent_normed, latent_norm_back = jax.vjp(rms_norm, latents.astype(wide), latent_gain)
    latent_in = latent_normed.astype(low)
    latent_in_own = rows_at(latent_in, me * model_share, model_share, 1)
    latent_proj = lax.psum(
        jnp.concatenate(
            [
                mat_times(latent_in_own, query_weight),
                mat_times(latent_in_own, key_weight),
                mat_times(latent_in_own, value_weight),
            ],
            axis=1,
        ),
        "blk",
    ).astype(low)
    query_width = P_HEADS * P_HEAD
    pair_width = P_KV * P_HEAD

    def head_of(matrix, first, index):
        return lane_pad(rows_at(matrix, first + index * P_HEAD, P_HEAD, 1))

    latent_query = head_of(latent_proj, 0, head)
    latent_key = head_of(latent_proj, query_width, kv_head)
    latent_value = head_of(latent_proj, query_width + pair_width, kv_head)
    patch_key = head_of(patch_pairs, 0, kv_head)
    patch_value = head_of(patch_pairs, pair_width, kv_head)
    attended_latent_head = resample(
        latent_query, patch_key, patch_value, latent_key, latent_value, col_ids, images
    )[:, :P_HEAD]
    attended_latent = gather(attended_latent_head).reshape(blocks, lat_rows, P_HEAD)[::copies]
    attended_latent = jnp.transpose(attended_latent, (1, 0, 2)).reshape(lat_rows, query_width)
    mixed = gather(mat_times(attended_latent, mixer_own).astype(low))
    mixed = jnp.transpose(mixed.reshape(blocks, lat_rows, -1), (1, 0, 2)).reshape(lat_rows, model)
    latent_state = jnp.tile(latents.astype(wide), (images, 1)) + mixed.astype(wide)

    post_in = rms_norm(latent_state, post_gain).astype(low)
    latent_act, latent_act_back = jax.vjp(
        swiglu, mat_times(post_in, latent_gate), mat_times(post_in, latent_up)
    )
    latent_hidden = latent_act.astype(low)
    own_start = me * lat_own
    state_own = rows_at(latent_state, own_start, lat_own)
    latent_gate_grad, latent_up_grad = latent_act_back(mat_times_t(cotangent, latent_down))
    latent_gate_low = latent_gate_grad.astype(low)
    latent_up_low = latent_up_grad.astype(low)
    post_grad = scatter_sum(
        mat_times_t(latent_gate_low, latent_gate) + mat_times_t(latent_up_low, latent_up)
    )
    _, post_norm_back = jax.vjp(rms_norm, state_own, post_gain)
    state_norm_grad, post_gain_part = post_norm_back(post_grad)
    state_grad = rows_at(cotangent, own_start, lat_own).astype(wide) + state_norm_grad
    state_low = gather(state_grad.astype(low))
    resid_part = lax.dynamic_update_slice_in_dim(
        jnp.zeros((LATENTS, model), wide), state_grad, own_start % LATENTS, 0
    )
    latents_out = (state_own + scatter_sum(mat_times(latent_hidden, latent_down))).astype(low)

    latent_att_grad = mat_times_t(state_low, mixer_weight).astype(low)
    if copies > 1:
        latent_att_grad = gather(latent_att_grad).reshape(blocks, lat_rows, -1)
        latent_att_grad = jnp.transpose(latent_att_grad, (1, 0, 2)).reshape(lat_rows, query_width)
        latent_att_grad = rows_at(latent_att_grad, head * P_HEAD, P_HEAD, 1)
    query_part, patch_key_part, patch_value_part, latent_key_part, latent_value_part = (
        resample_back(
            latent_query, patch_key, patch_value, latent_key, latent_value, col_ids,
            lane_pad(latent_att_grad), images,
        )
    )
    scale_latent = P_HEAD ** (-0.5)
    patch_part = jnp.concatenate(
        [patch_key_part[:, :P_HEAD] * scale_latent, patch_value_part[:, :P_HEAD]], axis=1
    ).astype(low)
    patch_part = swap_pieces(patch_part.reshape(blocks, rows, 2 * P_HEAD))
    patch_part = patch_part.reshape(blocks, rows, 2, P_HEAD)[::copies].astype(wide)
    patch_grad = jnp.sum(
        patch_part.reshape(P_KV, P_HEADS // P_KV, rows, 2, P_HEAD), axis=1
    )
    patch_grad = jnp.transpose(patch_grad, (1, 2, 0, 3)).reshape(rows, 2 * pair_width).astype(low)
    context_grad, context_gain_part = context_norm_back(mat_times_t(patch_grad, pair_weight))

    context_rows = gather(context_grad.astype(low))
    bridge_gate_grad, bridge_up_grad = bridge_act_back(mat_times_t(context_rows, bridge_down))
    bridge_gate_low = bridge_gate_grad.astype(low)
    bridge_up_low = bridge_up_grad.astype(low)
    grad_bridge_down = plane_sum(outer_sum(bridge_hidden, context_rows))
    encoded_grad = scatter_sum(
        mat_times_t(bridge_gate_low, bridge_gate) + mat_times_t(bridge_up_low, bridge_up)
    )
    grad_bridge_gate = plane_sum(outer_sum(bridge_rows, bridge_gate_low))
    grad_bridge_up = plane_sum(outer_sum(bridge_rows, bridge_up_low))

    encoded_rows = gather(encoded_grad.astype(low))
    grad_fc2_bias = jnp.sum(encoded_grad, axis=0)
    pre_grad = gate_back(mat_times(encoded_rows, fc2_own))[0].astype(low)
    second_grad = scatter_sum(mat_times_t(pre_grad, fc1_own))
    grad_fc1_bias = jnp.sum(pre_grad.astype(wide), axis=0)
    hidden_norm_grad, grad_ln2_gain, grad_ln2_bias = second_norm_back(second_grad)
    hidden_grad = encoded_grad + hidden_norm_grad
    grad_out_bias = jnp.sum(hidden_grad, axis=0)
    hidden_low = hidden_grad.astype(low)

    attended_grad = mat_times_t(hidden_low, out_full).astype(low)
    attended_grad = jnp.transpose(attended_grad.reshape(rows, HEADS, HEAD), (1, 0, 2))
    attended_grad = swap_pieces(jnp.repeat(lane_pad(attended_grad), copies, axis=0))
    query_low, key_low, value_low = attend_back(heads, attended_grad, row_ids, col_ids)
    head_grad = jnp.concatenate([query_low, key_low, value_low], axis=1)
    first_part = mat_times_t(head_grad, head_weight)
    if copies > 1:
        first_part = jnp.where(part == 0, first_part, 0.0)
    first_grad = scatter_sum(first_part)
    input_norm_grad, grad_ln1_gain, grad_ln1_bias = first_norm_back(first_grad)
    grad_tokens = hidden_grad + input_norm_grad

    hidden_rows = gather(hidden_low)
    out_width = out_weight.shape[0]
    grad_out = share_rows(
        outer_sum(rows_at(attended_head, part * out_width, out_width, 1), hidden_rows)
    )
    mixer_width = mixer_weight.shape[0]
    grad_mixer = share_rows(
        outer_sum(rows_at(attended_latent_head, part * mixer_width, mixer_width, 1), state_low)
    )
    grad_fc1 = outer_sum(second_rows, pre_grad)
    grad_fc2 = outer_sum(encoded_rows, act_low)
    units = share_columns(jnp.concatenate([grad_fc1, grad_fc2], axis=1))
    units = jnp.transpose(
        units.reshape(blocks, units.shape[1], 2, unit_share), (2, 1, 0, 3)
    ).reshape(2, units.shape[1], -1)[:, :, :hidden_units]
    grad_qkv = share_columns(outer_sum(first_rows, head_grad))[::copies]
    grad_qkv = grad_qkv.reshape(HEADS, grad_qkv.shape[1], 3, LANES)[..., :HEAD]
    grad_qkv = jnp.transpose(grad_qkv, (1, 2, 0, 3)).reshape(-1, 3 * features)
    context_in_columns = swap_pieces(
        jnp.transpose(context_in.reshape(rows, blocks, model_share), (1, 0, 2))
    )
    grad_pair = share_rows(outer_sum(context_in_columns, gather(patch_grad)))

    post_both = both_planes(post_in)
    grad_latent_gate = outer_sum(post_both, both_planes(latent_gate_low))
    grad_latent_up = outer_sum(post_both, both_planes(latent_up_low))
    grad_latent_down = outer_sum(both_planes(latent_hidden), both_planes(cotangent))

    once = (part == 0).astype(wide)

    def placed(width, pieces):
        base = jnp.zeros((LATENTS, width), wide)
        return lax.dynamic_update_slice_in_dim(base, pieces[0][:, :P_HEAD] * once, pieces[1], 1)

    def spread(width, piece, first):
        return lax.dynamic_update_slice_in_dim(jnp.zeros((width,), wide), piece, first, 0)

    latent_sums = lax.psum(
        (
            placed(query_width, (query_part, head * P_HEAD)),
            placed(pair_width, (latent_key_part, kv_head * P_HEAD)),
            placed(pair_width, (latent_value_part, kv_head * P_HEAD)),
            resid_part,
            context_gain_part,
            post_gain_part,
        ),
        ("grp", "blk"),
    )
    query_bias_part = jnp.sum(query_low[:, :HEAD].astype(wide), axis=0) * once
    value_bias_part = jnp.sum(value_low[:, :HEAD].astype(wide), axis=0) * once
    small = lax.psum(
        (
            grad_ln1_gain,
            grad_ln1_bias,
            spread(features, query_bias_part, head * HEAD),
            spread(features, value_bias_part, head * HEAD),
            grad_out_bias,
            grad_ln2_gain,
            grad_ln2_bias,
            spread(unit_share * blocks, grad_fc1_bias, me * unit_share),
            grad_fc2_bias,
        ),
        ("grp", "blk"),
    )

    query_grad = (latent_sums[0] * scale_latent).astype(low)
    pair_grad = jnp.concatenate([latent_sums[1] * scale_latent, latent_sums[2]], axis=1)
    pair_grad = pair_grad.astype(low)
    latent_in_grad = (
        mat_times_t(query_grad, query_weight)
        + mat_times_t(pair_grad[:, :pair_width], key_weight)
        + mat_times_t(pair_grad[:, pair_width:], value_weight)
    )
    latent_in_grad = gather(latent_in_grad).reshape(blocks, LATENTS, model_share)
    latent_in_grad = jnp.transpose(latent_in_grad, (1, 0, 2)).reshape(LATENTS, model)
    latent_grad, grad_latent_gain = latent_norm_back(latent_in_grad)
    grad_latents = latent_sums[3] + latent_grad
    share = model // (planes * blocks)
    latent_in_share = rows_at(latent_in, (plane * blocks + me) * share, share, 1)
    grad_query = outer_sum(latent_in_share, query_grad)
    grad_pair = grad_pair + outer_sum(latent_in_share, pair_grad)
    return (
        latents_out,
        grad_tokens,
        small[0],
        small[1],
        grad_qkv,
        small[2],
        small[3],
        grad_out,
        small[4],
        small[5],
        small[6],
        units[0],
        small[7][:hidden_units],
        units[1],
        small[8],
        grad_bridge_gate,
        grad_bridge_up,
        grad_bridge_down,
        latent_sums[4],
        grad_latents,
        grad_latent_gain,
        grad_query,
        grad_pair[:, :pair_width],
        grad_pair[:, pair_width:],
        grad_mixer,
        latent_sums[5],
        grad_latent_gate,
        grad_latent_up,
        grad_latent_down,
    )


def solution(mesh):
    in_specs = (
        P(("grp", "blk"), None),
        P(("grp", "blk")),
        P(),
        P(),
        P("blk", None),
        P(),
        P(),
        P("blk", None),
        P(),
        P(),
        P(),
        P("blk", None),
        P(),
        P("blk", None),
        P(),
        P(None, "blk"),
        P(None, "blk"),
        P("blk", None),
        P(),
        P(),
        P(),
        P("blk", None),
        P("blk", None),
        P("blk", None),
        P("blk", None),
        P(),
        P(None, "blk"),
        P(None, "blk"),
        P("blk", None),
        P("grp", None),
    )
    out_specs = (
        P(("grp", "blk"), None),
        P(("grp", "blk"), None),
        P(),
        P(),
        P(("grp", "blk"), None),
        P(),
        P(),
        P(("grp", "blk"), None),
        P(),
        P(),
        P(),
        P(("grp", "blk"), None),
        P(),
        P(("grp", "blk"), None),
        P(),
        P(None, "blk"),
        P(None, "blk"),
        P("blk", None),
        P(),
        P(),
        P(),
        P(("grp", "blk"), None),
        P(("grp", "blk"), None),
        P(("grp", "blk"), None),
        P(("grp", "blk"), None),
        P(),
        P(None, "blk"),
        P(None, "blk"),
        P("blk", None),
    )
    return jax.shard_map(
        on_device, mesh=mesh, in_specs=in_specs, out_specs=out_specs, check_vma=False
    )
```

time: 4210 us -> 2040 us (0.48)
  waiting for transfers between devices: 2220 us -> 1250 us
  blocking collectives: 975 us -> 204 us
  matrix products: 458 us -> 263 us
  local copies, waits for them, and re-layouts: 211 us -> 79.5 us
  other arithmetic: 179 us -> 81.4 us
  starting transfers between devices: 144 us -> 80.6 us
  Pallas kernels: 0 us -> 47.6 us
    unnamed x2 -> x0, blocking collectives: 850 us -> none
    psum x4 -> x1, waiting for transfers between devices: 818 us -> 0.01 us  [on_device(): lax.psum((placed(query_width, (query_part, head * P_HEAD)), placed(pair_w...]
    ppermute x0 -> x16, waiting for transfers between devices: none -> 293 us  [the longest x10 290 us: other_plane(): lax.ppermute(array, 'grp', [(k, (k + step) % planes) for k in range(plane...]
    reduce_scatter x7, waiting for transfers between devices: 665 us -> 442 us  [scatter_sum(): lax.psum_scatter(array.astype(low), 'blk', scatter_dimension=0, tiled=True)]
    all_gather x12 -> x13, waiting for transfers between devices: 694 us -> 486 us  [gather(): return lax.all_gather(array, 'blk', axis=0, tiled=True)]
    dot_general x88 -> x44, matrix products: 458 us -> 263 us  [the longest x29 179 us: contract(): lax.dot_general(left, right, (((left_dim,), (right_dim,)), ((), ())), pre...]
    unnamed x24 -> x0, starting transfers between devices: 142 us -> none
    unnamed x314 -> x222, local copies, waits for them, and re-layouts: 132 us -> 19.5 us
  transfers between devices with their start and end apart: 47 -> 46, of which waited for: 25 -> 27; matrix products, arithmetic and copies ran while one was open for 36% -> 11% of each run, Pallas kernels for 0% -> 2%
where the time goes in v1:
time: 2040 us; the launch traced here: 2020 us
  waiting for transfers between devices  1250 us (61%)
  matrix products  263 us (13%)
  blocking collectives  204 us (10%)
  other arithmetic  81.4 us (4%)
  starting transfers between devices  80.6 us (4%)
  local copies, waits for them, and re-layouts  79.5 us (4%)
  Pallas kernels  47.6 us (2%)
    all_gather x13, waiting for transfers between devices, gather(): return lax.all_gather(array, 'blk', axis=0, tiled=True)  486 us
    reduce_scatter x7, waiting for transfers between devices, scatter_sum(): lax.psum_scatter(array.astype(low), 'blk', scatter_dimension=0, tiled=True)  442 us
    ppermute x10, waiting for transfers between devices, other_plane(): lax.ppermute(array, 'grp', [(k, (k + step) % planes) for k in range(plane...  290 us
    dot_general x29, matrix products, contract(): lax.dot_general(left, right, (((left_dim,), (right_dim,)), ((), ())), pre...  179 us
    dot_general x15, matrix products, mat_times(): return jnp.dot(left, right, preferred_element_type=wide)  83.3 us
    psum x1, blocking collectives, on_device(): lax.psum(jnp.concatenate([mat_times(latent_in_own, query_weight), mat_tim...  69.3 us
    all_gather x2, blocking collectives, gather(): return lax.all_gather(array, 'blk', axis=0, tiled=True)  64.4 us
    all_to_all x9, starting transfers between devices, swap_pieces(): return lax.all_to_all(flat, 'blk', 0, 0, tiled=True)  53.3 us
  transfers between devices with their start and end apart: 46, of which 27 were waited for; matrix products, arithmetic and copies ran while one was open for 11% of the time, Pallas kernels for 2%

profile of v1, /device:TPU:10, one launch (start us, length us, event | category | flops | bytes accessed | tf_op | source)
XLA Modules:
  0.0 2021.5 jit_solution(15044495228168093176)
XLA Ops:
  19.2 6.3 all-to-all-start
  27.1 36.4 %all-gather = s32[16,1,128]{2,1,0:T(1,128)S(1)} all-gather(s32[1,1,128]{2,1,0:T(1,128)S(1)} %bitcast.194), channel_id=1, replica_groups=mesh['grp'=2,'blk'=16] {'blk'}, dimensions={0}, use_global_device_ids=true | all-gather | bytes 8704 | tf_op jit(solution)/shard_map/all_gather | solution.py:66
  64.9 14.4 all-gather.15.cloned.1.call-done
  79.3 6.3 add_convert_fusion.1.query_ref.key_ref.value_ref
  85.6 12.7 vision_attend.1
  104.3 21.5 %all-gather.17.cloned.1.call-done = bf16[1152,1152]{1,0:T(8,128)(2,1)} async-done(((bf16[72,1152]{1,0:T(8,128)(2,1)}), bf16[1152,1152]{1,0:T(8,128)(2,1)}) %all-gather.17.cloned.1.call-update) | async-done | bytes 2654224 | tf_op jit(solution)/shard_map/all_gather | solution.py:66
  133.0 5.4 all-to-all-start.2
  142.0 26.8 %all-to-all-done.2 = bf16[16,72,269]{2,1,0:T(8,128)(2,1)} async-done(((bf16[16,72,269]{2,1,0:T(8,128)(2,1)}), bf16[16,72,269]{2,1,0:T(8,128)(2,1)}, u32[]{:S(2)}, u32[]{:S(2)}) %all-to-all-start.2) | async-done | bytes 619808 | tf_op jit(solution)/shard_map/all_to_all | solution.py:75
  168.8 5.3 all-to-all-start.3
  174.9 32.3 %all-gather.19.cloned.1.call-done = bf16[2048,1152]{1,0:T(8,128)(2,1)} async-done(((bf16[128,1152]{1,0:T(8,128)(2,1)}), bf16[2048,1152]{1,0:T(8,128)(2,1)}) %all-gather.19.cloned.1.call-update) | async-done | bytes 4718608 | tf_op jit(solution)/shard_map/all_gather | solution.py:66
  207.2 5.6 convolution_add_fusion.1
  212.8 7.1 convolution_convert_fusion.3
  219.9 77.1 %reduce-scatter.8.cloned.1.call-done = bf16[128,1152]{1,0:T(8,128)(2,1)} async-done(((bf16[2048,1152]{1,0:T(8,128)(2,1)}), bf16[128,1152]{1,0:T(8,128)(2,1)}) %reduce-scatter.8.cloned.1.call-update) | async-done | bytes 294928 | tf_op jit(solution)/shard_map/reduce_scatter | solution.py:70
  299.1 54.0 %all-gather.21.cloned.1.call-done = bf16[2048,1152]{1,0:T(8,128)(2,1)} async-done(((bf16[128,1152]{1,0:T(8,128)(2,1)}), bf16[2048,1152]{1,0:T(8,128)(2,1)}) %all-gather.21.cloned.1.call-update) | async-done | bytes 4718608 | tf_op jit(solution)/shard_map/all_gather | solution.py:66
  353.1 8.1 fusion.115
  361.2 7.9 multiply_convert_fusion.1
  370.9 20.5 %convolution_convert_fusion = bf16[2048,4096]{1,0:T(8,128)(2,1)} fusion(bf16[2048,896]{1,0:T(8,128)(2,1)S(1)} %get-tuple-element.117, bf16[896,4096]{1,0:T(8,128)(2,1)S(1)} %bitcast.200), kind=kOutput, calls=%fused_computation | convolution fusion | flops 15040774144 | bytes 27787264 | tf_op jit(solution)/shard_map/dot_general | solution.py:44
  393.2 174.1 %reduce-scatter.10.cloned.1.call-done = bf16[128,4096]{1,0:T(8,128)(2,1)} async-done(((bf16[2048,4096]{1,0:T(8,128)(2,1)}), bf16[128,4096]{1,0:T(8,128)(2,1)}) %reduce-scatter.10.cloned.1.call-update) | async-done | bytes 1048592 | tf_op jit(solution)/shard_map/reduce_scatter | solution.py:70
  570.4 62.3 %all-gather.23.cloned.1.call-done = bf16[4096,768]{1,0:T(8,128)(2,1)} async-done(((bf16[256,768]{1,0:T(8,128)(2,1)}), bf16[4096,768]{1,0:T(8,128)(2,1)}) %all-gather.23.cloned.1.call-update) | async-done | bytes 6291472 | tf_op jit(solution)/shard_map/all_gather | solution.py:66
  649.1 69.3 %all-reduce.17 = bf16[64,2304]{1,0:T(8,128)(2,1)S(1)} all-reduce(f32[64,2304]{1,0:T(8,128)S(1)} %pad_maximum_fusion.4), channel_id=1, replica_groups=mesh['grp'=2,'blk'=16] {'blk'}, use_global_device_ids=true, to_apply=%region_1.2 | all-reduce | flops 147456 | bytes 884736 | tf_op jit(solution)/shard_map/psum | solution.py:395
  727.4 28.1 %all_gather.52 = bf16[4096,96]{1,0:T(8,128)(2,1)} all-gather(bf16[256,96]{1,0:T(8,128)(2,1)} %bitcast.185), channel_id=1, replica_groups=mesh['grp'=2,'blk'=16] {'blk'}, dimensions={0}, use_global_device_ids=true | all-gather | bytes 835584 | tf_op jit(solution)/shard_map/all_gather | solution.py:66
  764.5 38.4 %all-gather.27.cloned.1.call-done = bf16[4096,256]{1,0:T(8,128)(2,1)} async-done(((bf16[256,256]{1,0:T(8,128)(2,1)}), bf16[4096,256]{1,0:T(8,128)(2,1)}) %all-gather.27.cloned.1.call-update) | async-done | bytes 2097168 | tf_op jit(solution)/shard_map/all_gather | solution.py:66
  815.1 5.1 fusion.117
  820.2 5.1 fusion.116
  825.4 6.7 multiply_convert_fusion.5
  836.6 6.2 fusion.4
  842.8 7.0 convolution_convert_fusion.5
  851.1 53.0 %reduce-scatter.14.cloned.1.call-done = bf16[16,4096]{1,0:T(8,128)(2,1)} async-done(((bf16[256,4096]{1,0:T(8,128)(2,1)}), bf16[16,4096]{1,0:T(8,128)(2,1)}) %reduce-scatter.14.cloned.1.call-update) | async-done | bytes 131088 | tf_op jit(solution)/shard_map/reduce_scatter | solution.py:70
  905.9 63.2 %reduce-scatter.12.cloned.1.call-done = bf16[16,4096]{1,0:T(8,128)(2,1)} async-done(((bf16[256,4096]{1,0:T(8,128)(2,1)}), bf16[16,4096]{1,0:T(8,128)(2,1)}) %reduce-scatter.12.cloned.1.call-update) | async-done | bytes 131088 | tf_op jit(solution)/shard_map/reduce_scatter | solution.py:70
  972.2 39.7 %all-gather.29.cloned.1.call-done = bf16[256,4096]{1,0:T(8,128)(2,1)} async-done(((bf16[16,4096]{1,0:T(8,128)(2,1)}), bf16[256,4096]{1,0:T(8,128)(2,1)}) %all-gather.29.cloned.1.call-update) | async-done | bytes 2097168 | tf_op jit(solution)/shard_map/all_gather | solution.py:66
  1015.0 6.2 resampler_attend_back.1
  1028.0 24.4 %all_to_all.86 = bf16[16,128,192]{1,2,0:T(8,128)(2,1)} all-to-all(bf16[16,128,192]{1,2,0:T(8,128)(2,1)S(1)} %pad_maximum_fusion.3), channel_id=1, replica_groups=mesh['grp'=2,'blk'=16] {'blk'}, dimensions={0} | all-to-all | bytes 1572864 | tf_op jit(solution)/shard_map/all_to_all | solution.py:75
  1053.7 5.8 fusion.24
  1061.1 124.6 %all-gather.31.cloned.1.call-done = bf16[2048,4096]{1,0:T(8,128)(2,1)} async-done(((bf16[128,4096]{1,0:T(8,128)(2,1)}), bf16[2048,4096]{1,0:T(8,128)(2,1)}) %all-gather.31.cloned.1.call-update) | async-done | bytes 16777232 | tf_op jit(solution)/shard_map/all_gather | solution.py:66
  1185.7 27.9 %multiply_convert_fusion = (bf16[2048,896]{1,0:T(8,128)(2,1)}, bf16[2048,896]{1,0:T(8,128)(2,1)}) fusion(f32[2048,896]{1,0:T(8,128)} %copy-done.97, f32[2048,896]{1,0:T(8,128)} %get-tuple-element.118, bf16[2048,4096]{1,0:T(8,128)(2,1)} %all-gather.31.cloned.1.call-done, bf16[896,4096]{1,0:T(8,128)(2,1)} %param.47), kind=kOutput, calls=%fused_computation.10 | convolution fusion | flops 15058075648 | bytes 46137344 | tf_op jit(solution)/shard_map/dot_general | solution.py:48
  1213.6 7.7 fusion.119
  1221.4 7.5 add_convert_fusion
  1229.0 75.2 %reduce-scatter.16.cloned.1.call-done = bf16[128,1152]{1,0:T(8,128)(2,1)} async-done(((bf16[2048,1152]{1,0:T(8,128)(2,1)}), bf16[128,1152]{1,0:T(8,128)(2,1)}) %reduce-scatter.16.cloned.1.call-update) | async-done | bytes 294928 | tf_op jit(solution)/shard_map/reduce_scatter | solution.py:70
  1304.2 55.1 %all-gather.33.cloned.1.call-done = bf16[2048,1152]{1,0:T(8,128)(2,1)} async-done(((bf16[128,1152]{1,0:T(8,128)(2,1)}), bf16[2048,1152]{1,0:T(8,128)(2,1)}) %all-gather.33.cloned.1.call-update) | async-done | bytes 4718608 | tf_op jit(solution)/shard_map/all_gather | solution.py:66
  1359.3 6.1 convert_reduce_fusion
  1365.4 6.1 convolution_convert_fusion.2
  1375.9 44.6 %collective-permute-done.15 = bf16[256,4096]{1,0:T(8,128)(2,1)} collective-permute-done((bf16[256,4096]{1,0:T(8,128)(2,1)}, bf16[256,4096]{1,0:T(8,128)(2,1)}, u32[]{:S(2)}, u32[]{:S(2)}) %collective-permute-start.15) | collective-permute-done | bytes 2097184 | tf_op jit(solution)/shard_map/ppermute | solution.py:289
  1426.7 4.9 collective-permute-done.14
  1431.7 8.6 fusion.7
  1443.9 10.2 collective-permute-done.12
  1466.2 36.5 %collective-permute-done.11 = bf16[256,4096]{1,0:T(8,128)(2,1)} collective-permute-done((bf16[256,4096]{1,0:T(8,128)(2,1)}, bf16[256,4096]{1,0:T(8,128)(2,1)}, u32[]{:S(2)}, u32[]{:S(2)}) %collective-permute-start.11) | collective-permute-done | bytes 2097184 | tf_op jit(solution)/shard_map/ppermute | solution.py:289
  1512.3 25.3 %vision_attend_back.1 = (bf16[2048,128]{1,0:T(8,128)(2,1)}, bf16[2048,128]{1,0:T(8,128)(2,1)}, bf16[2048,128]{1,0:T(8,128)(2,1)}) custom-call(bf16[2048,384]{1,0:T(8,128)(2,1)} %add_convert_fusion.1.query_ref.key_ref.value_ref, bf16[2048,384]{1,0:T(8,128)(2,1)} %add_convert_fusion.1.query_ref.key_ref.value_ref, ...), custom_call_target="tpu_custom_call" | custom-call | tf_op jit(solution)/shard_map/vision_attend_back/pallas_call | solution.py:149
  1547.8 11.0 fusion.11
  1558.9 8.6 fusion.12
  1574.9 22.3 %convolution_convert_fusion.4 = bf16[896,4096]{1,0:T(8,128)(2,1)} fusion(bf16[2048,896]{1,0:T(8,128)(2,1)} %copy-done.98, bf16[2048,4096]{1,0:T(8,128)(2,1)} %all-gather.31.cloned.1.call-done), kind=kOutput, calls=%fused_computation.14 | convolution fusion | flops 15036055552 | bytes 27787264 | tf_op jit(solution)/shard_map/dot_general | solution.py:48
  1601.2 8.6 convolution_convert_fusion.7
  1613.2 32.2 %all-gather.39.cloned.1.call-done = bf16[2048,768]{0,1:T(8,128)(2,1)} async-done(((bf16[128,768]{0,1:T(8,128)(2,1)}), bf16[2048,768]{0,1:T(8,128)(2,1)}) %all-gather.39.cloned.1.call-update) | async-done | bytes 3145744 | tf_op jit(solution)/shard_map/all_gather | solution.py:66
  1648.4 8.6 convolution_convert_fusion.6
  1665.2 137.2 %collective-permute-done.4 = bf16[1152,896]{1,0:T(8,128)(2,1)} collective-permute-done((bf16[1152,896]{1,0:T(8,128)(2,1)S(1)}, bf16[1152,896]{1,0:T(8,128)(2,1)}, u32[]{:S(2)}, u32[]{:S(2)}) %collective-permute-start.4) | collective-permute-done | bytes 2064416 | tf_op jit(solution)/shard_map/ppermute | solution.py:289
  1812.5 34.0 %collective-permute-done.5 = bf16[1152,896]{1,0:T(8,128)(2,1)S(1)} collective-permute-done((bf16[1152,896]{1,0:T(8,128)(2,1)S(1)}, bf16[1152,896]{1,0:T(8,128)(2,1)S(1)}, u32[]{:S(2)}, u32[]{:S(2)}) %collective-permute-start.5) | collective-permute-done | bytes 2064416 | tf_op jit(solution)/shard_map/ppermute | solution.py:289
  1848.8 12.5 collective-permute-done.3
  1863.3 13.8 all-to-all-start.8
  1877.2 14.1 convert_add_fusion
  1891.5 5.5 fusion.120
  1903.3 7.6 collective-permute-done
  1913.2 6.0 all-to-all-start.7
  1925.8 45.6 %all-reduce.18 = (f32[1152]{0:T(1024)}, f32[1152]{0:T(1024)}, f32[1152]{0:T(1024)}, f32[1152]{0:T(1024)}, f32[1152]{0:T(1024)}, /*index=5*/f32[1152]{0:T(1024)},...) all-reduce(f32[1152]{0:T(1024)} %get-tuple-element.55, ...), channel_id=1, replica_groups=mesh['grp'=2,'blk'=16] {'grp','blk'}, use_global_device_ids=true, to_apply=%region_24.25 | all-reduce | flops 46288 | bytes 321152 | tf_op jit(solution)/shard_map/psum | solution.py:554
  1973.2 4.7 slice_reduce_fusion
  1997.7 11.8 all-gather.37.cloned.1.call-done
  (459 shorter events, 238.9 us)
Async XLA Ops:
  7.2 353.9 %copy-start = (bf16[1152,896]{1,0:T(8,128)(2,1)S(1)}, bf16[1152,896]{1,0:T(8,128)(2,1)}, u32[]{:S(2)}) copy-start(bf16[1152,896]{1,0:T(8,128)(2,1)} %param.46) | copy-start | bytes 6193156
  7.2 72.1 %all-gather.15.cloned.1.call-start = ((), (), s32[]{:S(2)}) async-start(), calls=%async_computation.17 | async-start | bytes 5013504 | tf_op jit(solution)/shard_map/all_gather | solution.py:66
  12.7 113.2 %all-gather.17.cloned.1.call-start = ((), (), s32[]{:S(2)}) async-start(), calls=%async_computation.18 | async-start | bytes 2820096 | tf_op jit(solution)/shard_map/all_gather | solution.py:66
  19.2 45.6 %all-to-all-start = ((bf16[16,72,384]{2,1,0:T(8,128)(2,1)}), bf16[16,72,384]{2,1,0:T(8,128)(2,1)S(1)}, u32[]{:S(2)}, u32[]{:S(2)}) async-start(bf16[16,72,384]{2,1,0:T(8,128)(2,1)} %all_to_all.57), calls=%async_computation | async-start | bytes 1769472 | tf_op jit(solution)/shard_map/all_to_all | solution.py:75
  85.6 40.3 %copy-start.8 = (bf16[128,1152]{1,0:T(8,128)(2,1)S(1)}, bf16[128,1152]{1,0:T(8,128)(2,1)}, u32[]{:S(2)}) copy-start(bf16[128,1152]{1,0:T(8,128)(2,1)} %param.30) | copy-start | bytes 884740
  85.6 40.3 %copy-start.73 = (f32[1152]{0:T(1024)S(1)}, f32[1152]{0:T(1024)}, u32[]{:S(2)}) copy-start(f32[1152]{0:T(1024)} %param.38) | copy-start | bytes 13828
  100.2 28.4 %copy-start.74 = (f32[1152]{0:T(1024)S(1)}, f32[1152]{0:T(1024)}, u32[]{:S(2)}) copy-start(f32[1152]{0:T(1024)} %param.40) | copy-start | bytes 13828
  100.2 25.6 %all-to-all-start.1 = ((bf16[16,128,72]{1,2,0:T(8,128)(2,1)}), bf16[16,128,72]{1,2,0:T(8,128)(2,1)S(1)}, u32[]{:S(2)}, u32[]{:S(2)}) async-start(bf16[16,128,72]{1,2,0:T(8,128)(2,1)} %copy.150), calls=%async_computation.1 | async-start | bytes 589824 | tf_op jit(solution)/shard_map/all_to_all | solution.py:75
  104.3 102.9 %all-gather.19.cloned.1.call-start = ((), (), s32[]{:S(2)}) async-start(), calls=%async_computation.19 | async-start | bytes 5013504 | tf_op jit(solution)/shard_map/all_gather | solution.py:66
  128.3 168.7 %copy-start.2 = (f32[128,1152]{1,0:T(8,128)}, f32[128,1152]{1,0:T(8,128)S(1)}, u32[]{:S(2)}) copy-start(f32[128,1152]{1,0:T(8,128)S(1)} %get-tuple-element.116) | copy-start | bytes 1769476
  133.0 35.8 %all-to-all-start.2 = ((bf16[16,72,269]{2,1,0:T(8,128)(2,1)}), bf16[16,72,269]{2,1,0:T(8,128)(2,1)}, u32[]{:S(2)}, u32[]{:S(2)}) async-start(bf16[16,72,269]{2,1,0:T(8,128)(2,1)} %bitcast.152), calls=%async_computation.2 | async-start | bytes 1769472 | tf_op jit(solution)/shard_map/all_to_all | solution.py:75
  168.8 44.0 %all-to-all-start.3 = ((bf16[16,72,269]{2,1,0:T(8,128)(2,1)}), bf16[16,72,269]{2,1,0:T(8,128)(2,1)S(1)}, u32[]{:S(2)}, u32[]{:S(2)}) async-start(bf16[16,72,269]{2,1,0:T(8,128)(2,1)} %bitcast.151), calls=%async_computation.3 | async-start | bytes 1769472 | tf_op jit(solution)/shard_map/all_to_all | solution.py:75
  174.1 122.9 %reduce-scatter.8.cloned.1.call-start = ((), (), s32[]{:S(2)}) async-start(), calls=%async_computation.20 | async-start | bytes 5013504 | tf_op jit(solution)/shard_map/reduce_scatter | solution.py:70
  219.9 77.2 %copy-start.75 = (f32[1152]{0:T(1024)S(1)}, f32[1152]{0:T(1024)}, u32[]{:S(2)}) copy-start(f32[1152]{0:T(1024)} %param.44) | copy-start | bytes 13828
  219.9 133.2 %all-gather.21.cloned.1.call-start = ((), (), s32[]{:S(2)}) async-start(), calls=%async_computation.21 | async-start | bytes 5013504 | tf_op jit(solution)/shard_map/all_gather | solution.py:66
  298.8 268.5 %reduce-scatter.10.cloned.1.call-start = ((), (), s32[]{:S(2)}) async-start(), calls=%async_computation.22 | async-start | bytes 17825792 | tf_op jit(solution)/shard_map/reduce_scatter | solution.py:70
  391.4 177.5 %copy-start.57 = (f32[4096]{0:T(1024)S(1)}, f32[4096]{0:T(1024)}, u32[]{:S(2)}) copy-start(f32[4096]{0:T(1024)} %param.48) | copy-start | bytes 49156
  391.4 241.3 %all-gather.23.cloned.1.call-start = ((), (), s32[]{:S(2)}) async-start(), calls=%async_computation.23 | async-start | bytes 6684672 | tf_op jit(solution)/shard_map/all_gather | solution.py:66
  393.2 327.2 %all-gather.25.cloned.1.call-start = ((), (), s32[]{:S(2)}) async-start(), calls=%async_computation.24 | async-start | bytes 3342336 | tf_op jit(solution)/shard_map/all_gather | solution.py:66
  570.4 62.3 %copy-start.10 = (bf16[128,4096]{1,0:T(8,128)(2,1)}, bf16[128,4096]{1,0:T(8,128)(2,1)S(1)}, u32[]{:S(2)}) copy-start(bf16[128,4096]{1,0:T(8,128)(2,1)S(1)} %fusion.23) | copy-start | bytes 3145732
  639.3 117.6 %all-to-all-start.4 = ((bf16[16,96,256]{2,1,0:T(8,128)(2,1)}), bf16[16,96,256]{2,1,0:T(8,128)(2,1)}, u32[]{:S(2)}, u32[]{:S(2)}) async-start(bf16[16,96,256]{2,1,0:T(8,128)(2,1)} %bitcast.168), calls=%async_computation.6 | async-start | bytes 1572864 | tf_op jit(solution)/shard_map/all_to_all | solution.py:75
  643.9 158.9 %all-gather.27.cloned.1.call-start = ((), (), s32[]{:S(2)}) async-start(), calls=%async_computation.25 | async-start | bytes 2228224 | tf_op jit(solution)/shard_map/all_gather | solution.py:66
  759.2 144.9 %reduce-scatter.14.cloned.1.call-start = ((), (), s32[]{:S(2)}) async-start(), calls=%async_computation.27 | async-start | bytes 2228224 | tf_op jit(solution)/shard_map/reduce_scatter | solution.py:70
  842.7 126.3 %reduce-scatter.12.cloned.1.call-start = ((), (), s32[]{:S(2)}) async-start(), calls=%async_computation.26 | async-start | bytes 2228224 | tf_op jit(solution)/shard_map/reduce_scatter | solution.py:70
  849.8 162.0 %copy-start.20 = (bf16[96,4096]{1,0:T(8,128)(2,1)S(1)}, bf16[96,4096]{1,0:T(8,128)(2,1)}, u32[]{:S(2)}) copy-start(bf16[96,4096]{1,0:T(8,128)(2,1)} %param.54) | copy-start | bytes 2359300
  849.9 162.0 %all-gather.29.cloned.1.call-start = ((), (), s32[]{:S(2)}) async-start(), calls=%async_computation.28 | async-start | bytes 2228224 | tf_op jit(solution)/shard_map/all_gather | solution.py:66
  972.1 213.6 %all-gather.31.cloned.1.call-start = ((), (), s32[]{:S(2)}) async-start(), calls=%async_computation.29 | async-start | bytes 17825792 | tf_op jit(solution)/shard_map/all_gather | solution.py:66
  1024.8 28.8 %copy-start.6 = (bf16[128,4096]{1,0:T(8,128)(2,1)S(1)}, bf16[128,4096]{1,0:T(8,128)(2,1)}, u32[]{:S(2)}) copy-start(bf16[128,4096]{1,0:T(8,128)(2,1)} %reduce-scatter.10.cloned.1.call-done) | copy-start | bytes 3145732
  1061.1 243.1 %reduce-scatter.16.cloned.1.call-start = ((), (), s32[]{:S(2)}) async-start(), calls=%async_computation.30 | async-start | bytes 5013504 | tf_op jit(solution)/shard_map/reduce_scatter | solution.py:70
  1228.9 130.4 %copy-start.38 = (bf16[16,72,269]{2,1,0:T(8,128)(2,1)S(1)}, bf16[16,72,269]{2,1,0:T(8,128)(2,1)}, u32[]{:S(2)}) copy-start(bf16[16,72,269]{2,1,0:T(8,128)(2,1)} %copy-done.37) | copy-start | bytes 1859332
  1229.0 130.4 %all-gather.33.cloned.1.call-start = ((), (), s32[]{:S(2)}) async-start(), calls=%async_computation.31 | async-start | bytes 5013504 | tf_op jit(solution)/shard_map/all_gather | solution.py:66
  1304.2 150.9 %reduce-scatter.18.cloned.1.call-start = ((), (), s32[]{:S(2)}) async-start(), calls=%async_computation.32 | async-start | bytes 5013504 | tf_op jit(solution)/shard_map/reduce_scatter | solution.py:70
  1371.6 228.2 %all-reduce.16.cloned.1.call-start = ((), (), s32[]{:S(2)}) async-start(), calls=%async_computation.37 | async-start | bytes 3080192 | tf_op jit(solution)/shard_map/psum | solution.py:541
  1371.6 48.8 %collective-permute-start.15 = (bf16[256,4096]{1,0:T(8,128)(2,1)}, bf16[256,4096]{1,0:T(8,128)(2,1)}, u32[]{:S(2)}, u32[]{:S(2)}) collective-permute-start(bf16[256,4096]{1,0:T(8,128)(2,1)} %param.59), channel_id=1, source_target_pairs={{0,16},{16,0},{1,17},{17,1},{2,18},{18,2},{3,19},{19,3},{4,20},{20... | collective-permute-start | bytes 6291464 | tf_op jit(solution)/shard_map/ppermute | solution.py:289
  1374.2 271.2 %all-gather.39.cloned.1.call-start = ((), (), s32[]{:S(2)}) async-start(), calls=%async_computation.36 | async-start | bytes 3342336 | tf_op jit(solution)/shard_map/all_gather | solution.py:66
  1374.3 57.3 %collective-permute-start.14 = (bf16[256,1024]{1,0:T(8,128)(2,1)S(1)}, bf16[256,1024]{1,0:T(8,128)(2,1)S(1)}, u32[]{:S(2)}, u32[]{:S(2)}) collective-permute-start(bf16[256,1024]{1,0:T(8,128)(2,1)S(1)} %copy-done.46), channel_id=1, source_target_pairs={{0,16},{16,0},{1,17},{17,1},{2,18},{18,2},{3,19},{19,3},{4,20},{20... | collective-permute-start | bytes 1572872 | tf_op jit(solution)/shard_map/ppermute | solution.py:289
  1375.9 47.1 %copy-start.11 = (bf16[128,4096]{1,0:T(8,128)(2,1)S(1)}, bf16[128,4096]{1,0:T(8,128)(2,1)}, u32[]{:S(2)}) copy-start(bf16[128,4096]{1,0:T(8,128)(2,1)} %copy-done.10) | copy-start | bytes 3145732
  1375.9 48.2 %copy-start.44 = (bf16[256,1024]{1,0:T(8,128)(2,1)S(1)}, bf16[256,1024]{1,0:T(8,128)(2,1)}, u32[]{:S(2)}) copy-start(bf16[256,1024]{1,0:T(8,128)(2,1)} %copy-done.43) | copy-start | bytes 1572868
  1375.9 48.8 %copy-start.42 = (bf16[256,1024]{1,0:T(8,128)(2,1)S(1)}, bf16[256,1024]{1,0:T(8,128)(2,1)}, u32[]{:S(2)}) copy-start(bf16[256,1024]{1,0:T(8,128)(2,1)} %copy-done.41) | copy-start | bytes 1572868
  1424.1 18.7 collective-permute-start.13
  1424.7 29.4 %collective-permute-start.12 = (bf16[256,1024]{1,0:T(8,128)(2,1)S(1)}, bf16[256,1024]{1,0:T(8,128)(2,1)S(1)}, u32[]{:S(2)}, u32[]{:S(2)}) collective-permute-start(bf16[256,1024]{1,0:T(8,128)(2,1)S(1)} %copy-done.42), channel_id=1, source_target_pairs={{0,16},{16,0},{1,17},{17,1},{2,18},{18,2},{3,19},{19,3},{4,20},{20... | collective-permute-start | bytes 1572872 | tf_op jit(solution)/shard_map/ppermute | solution.py:289
  1426.1 76.6 %collective-permute-start.11 = (bf16[256,4096]{1,0:T(8,128)(2,1)}, bf16[256,4096]{1,0:T(8,128)(2,1)}, u32[]{:S(2)}, u32[]{:S(2)}) collective-permute-start(bf16[256,4096]{1,0:T(8,128)(2,1)} %get-tuple-element.81), channel_id=1, source_target_pairs={{0,16},{16,0},{1,17},{17,1},{2,18},{18,2},{3,19},{19,3},{4,20},{20... | collective-permute-start | bytes 6291464 | tf_op jit(solution)/shard_map/ppermute | solution.py:289
  1462.4 44.9 %all-to-all-start.6 = ((bf16[16,128,128]{1,2,0:T(8,128)(2,1)}), bf16[16,128,128]{1,2,0:T(8,128)(2,1)S(1)}, u32[]{:S(2)}, u32[]{:S(2)}) async-start(bf16[16,128,128]{1,2,0:T(8,128)(2,1)} %pad.45), calls=%async_computation.12 | async-start | bytes 1048576 | tf_op jit(solution)/shard_map/all_to_all | solution.py:75
  1507.2 105.9 %all-to-all-start.9 = ((bf16[16,128,256]{2,1,0:T(8,128)(2,1)}), bf16[16,128,256]{2,1,0:T(8,128)(2,1)S(1)}, u32[]{:S(2)}, u32[]{:S(2)}) async-start(bf16[16,128,256]{2,1,0:T(8,128)(2,1)} %bitcast.150), calls=%async_computation.16 | async-start | bytes 2097152 | tf_op jit(solution)/shard_map/all_to_all | solution.py:75
  1511.2 408.1 %reduce-scatter.20.cloned.1.call-start = ((), (), s32[]{:S(2)}) async-start(), calls=%async_computation.33 | async-start | bytes 5013504 | tf_op jit(solution)/shard_map/reduce_scatter | solution.py:70
  1546.6 438.0 %all-gather.35.cloned.1.call-start = ((), (), s32[]{:S(2)}) async-start(), calls=%async_computation.34 | async-start | bytes 5013504 | tf_op jit(solution)/shard_map/all_gather | solution.py:66
  1568.0 30.8 %collective-permute-start.9 = (bf16[48,4096]{1,0:T(8,128)(2,1)S(1)}, bf16[48,4096]{1,0:T(8,128)(2,1)S(1)}, u32[]{:S(2)}, u32[]{:S(2)}) collective-permute-start(bf16[48,4096]{1,0:T(8,128)(2,1)S(1)} %get-tuple-element.104), channel_id=1, source_target_pairs={{0,0},{1,2},{2,4},{3,6},{4,8},{5,10},{6,12},{7,14},{8,16},{9,18},{... | collective-permute-start | bytes 1179656 | tf_op jit(solution)/shard_map/ppermute | solution.py:327
  1571.2 27.6 %collective-permute-start.10 = (bf16[48,4096]{1,0:T(8,128)(2,1)S(1)}, bf16[48,4096]{1,0:T(8,128)(2,1)S(1)}, u32[]{:S(2)}, u32[]{:S(2)}) collective-permute-start(bf16[48,4096]{1,0:T(8,128)(2,1)S(1)} %get-tuple-element.105), channel_id=1, source_target_pairs={{0,1},{1,3},{2,5},{3,7},{4,9},{5,11},{6,13},{7,15},{8,17},{9,19},{... | collective-permute-start | bytes 1179656 | tf_op jit(solution)/shard_map/ppermute | solution.py:327
  1597.2 280.0 %collective-permute-start.6 = (bf16[896,4096]{1,0:T(8,128)(2,1)}, bf16[896,4096]{1,0:T(8,128)(2,1)}, u32[]{:S(2)}, u32[]{:S(2)}) collective-permute-start(bf16[896,4096]{1,0:T(8,128)(2,1)} %convolution_convert_fusion.4), channel_id=1, source_target_pairs={{0,16},{16,0},{1,17},{17,1},{2,18},{18,2},{3,19},{19,3},{4,20},{20... | collective-permute-start | bytes 22020104 | tf_op jit(solution)/shard_map/ppermute | solution.py:289
  1609.8 192.5 %collective-permute-start.4 = (bf16[1152,896]{1,0:T(8,128)(2,1)S(1)}, bf16[1152,896]{1,0:T(8,128)(2,1)}, u32[]{:S(2)}, u32[]{:S(2)}) collective-permute-start(bf16[1152,896]{1,0:T(8,128)(2,1)S(1)} %convolution_convert_fusion.7), channel_id=1, source_target_pairs={{0,16},{16,0},{1,17},{17,1},{2,18},{18,2},{3,19},{19,3},{4,20},{20... | collective-permute-start | bytes 6193160 | tf_op jit(solution)/shard_map/ppermute | solution.py:289
  1645.4 161.1 %slice-start.6 = ((s8[4718592]{0:T(1024)(128)(4,1)}), s8[4194304]{0:T(1024)(128)(4,1)S(1)}, s32[]{:S(2)}) async-start(s8[4718592]{0:T(1024)(128)(4,1)} %bitcast.201), calls=%async_computation.44 | async-start | bytes 8388608
  1648.4 158.0 %slice-start.7 = ((s8[4718592]{0:T(1024)(128)(4,1)}), s8[524288]{0:T(1024)(128)(4,1)S(1)}, s32[]{:S(2)}) async-start(s8[4718592]{0:T(1024)(128)(4,1)} %bitcast.201), calls=%async_computation.45 | async-start | bytes 1048576
  1657.1 189.4 %collective-permute-start.5 = (bf16[1152,896]{1,0:T(8,128)(2,1)S(1)}, bf16[1152,896]{1,0:T(8,128)(2,1)S(1)}, u32[]{:S(2)}, u32[]{:S(2)}) collective-permute-start(bf16[1152,896]{1,0:T(8,128)(2,1)S(1)} %convolution_convert_fusion.6), channel_id=1, source_target_pairs={{0,16},{16,0},{1,17},{17,1},{2,18},{18,2},{3,19},{19,3},{4,20},{20... | collective-permute-start | bytes 6193160 | tf_op jit(solution)/shard_map/ppermute | solution.py:289
  1658.5 324.8 %collective-permute-start.7 = (bf16[128,768]{1,0:T(8,128)(2,1)}, bf16[128,768]{1,0:T(8,128)(2,1)}, u32[]{:S(2)}, u32[]{:S(2)}) collective-permute-start(bf16[128,768]{1,0:T(8,128)(2,1)} %get-tuple-element.108), channel_id=1, source_target_pairs={{0,0},{1,2},{2,4},{3,6},{4,8},{5,10},{6,12},{7,14},{8,16},{9,18},{... | collective-permute-start | bytes 589832 | tf_op jit(solution)/shard_map/ppermute | solution.py:327
  1662.8 143.7 %copy-start.94 = (bf16[2048,269]{0,1:T(8,128)(2,1)S(1)}, bf16[2048,269]{0,1:T(8,128)(2,1)}, u32[]{:S(2)}) copy-start(bf16[2048,269]{0,1:T(8,128)(2,1)} %copy-done.93) | copy-start | bytes 3305476
  1662.8 320.5 %collective-permute-start.8 = (bf16[128,768]{1,0:T(8,128)(2,1)}, bf16[128,768]{1,0:T(8,128)(2,1)}, u32[]{:S(2)}, u32[]{:S(2)}) collective-permute-start(bf16[128,768]{1,0:T(8,128)(2,1)} %get-tuple-element.109), channel_id=1, source_target_pairs={{0,1},{1,3},{2,5},{3,7},{4,9},{5,11},{6,13},{7,15},{8,17},{9,19},{... | collective-permute-start | bytes 589832 | tf_op jit(solution)/shard_map/ppermute | solution.py:327
  1810.5 50.8 %collective-permute-start.3 = (bf16[576,538]{0,1:T(8,128)(2,1)S(1)}, bf16[576,538]{0,1:T(8,128)(2,1)S(1)}, u32[]{:S(2)}, u32[]{:S(2)}) collective-permute-start(bf16[576,538]{0,1:T(8,128)(2,1)S(1)} %fusion.29), channel_id=1, source_target_pairs={{0,16},{16,0},{1,17},{17,1},{2,18},{18,2},{3,19},{19,3},{4,20},{20... | collective-permute-start | bytes 1859336 | tf_op jit(solution)/shard_map/ppermute | solution.py:289
  1863.3 35.3 %all-to-all-start.8 = ((bf16[16,36,538]{2,1,0:T(8,128)(2,1)}), bf16[16,36,538]{2,1,0:T(8,128)(2,1)S(1)}, u32[]{:S(2)}, u32[]{:S(2)}) async-start(bf16[16,36,538]{2,1,0:T(8,128)(2,1)} %all_to_all.72), calls=%async_computation.15 | async-start | bytes 1638400 | tf_op jit(solution)/shard_map/all_to_all | solution.py:75
  1898.4 12.5 collective-permute-start
  1912.3 59.1 %copy-start.55 = (f32[64,256]{1,0:T(8,128)S(1)}, f32[64,256]{1,0:T(8,128)}, u32[]{:S(2)}) copy-start(f32[64,256]{1,0:T(8,128)} %convolution_add_fusion.4) | copy-start | bytes 196612
  1913.2 68.4 %all-to-all-start.7 = ((bf16[16,36,384]{2,1,0:T(8,128)(2,1)}), bf16[16,36,384]{2,1,0:T(8,128)(2,1)S(1)}, u32[]{:S(2)}, u32[]{:S(2)}) async-start(bf16[16,36,384]{2,1,0:T(8,128)(2,1)} %all_to_all.70), calls=%async_computation.14 | async-start | bytes 983040 | tf_op jit(solution)/shard_map/all_to_all | solution.py:75
  1919.2 90.3 %all-gather.37.cloned.1.call-start = ((), (), s32[]{:S(2)}) async-start(), calls=%async_computation.35 | async-start | bytes 1114112 | tf_op jit(solution)/shard_map/all_gather | solution.py:66
  1988.0 9.1 collective-permute-start.1
  1990.3 6.8 collective-permute-start.2
  (91 other events, 779.8 us)
Sparse Core Ops, SparseCore 0:
  12.8 66.4 all-gather.14
  81.4 44.3 all-gather.16
  129.7 77.4 all-gather.18
  220.0 76.9 reduce-scatter.7
  300.0 53.0 all-gather.20
  391.5 175.7 reduce-scatter.9
  570.4 62.2 all-gather.22
  637.3 54.7 all-gather.24
  759.3 43.5 all-gather.26
  842.9 61.1 reduce-scatter.13
  908.4 60.5 reduce-scatter.11
  972.3 39.5 all-gather.28
  1061.2 124.4 all-gather.30
  1229.1 75.0 reduce-scatter.15
  1306.3 52.9 all-gather.32
  1371.7 73.4 reduce-scatter.17
  1452.2 143.9 all-reduce.15
  1599.0 46.2 all-gather.38
  1649.7 74.5 reduce-scatter.19
  1726.4 53.0 all-gather.34
  1973.3 36.1 all-gather.36

commit v2 on v1

--- a/solution.py
+++ b/solution.py
@@ -66,6 +66,12 @@
     return lax.all_gather(array, "blk", axis=0, tiled=True)
 
 
+def swiglu_back(gate, up, grad):
+    share = jax.nn.sigmoid(gate)
+    gated = gate * share
+    return grad * up * (share + gated * (1.0 - share)), grad * gated
+
+
 def scatter_sum(array):
     return lax.psum_scatter(array.astype(low), "blk", scatter_dimension=0, tiled=True).astype(wide)
 
@@ -73,6 +79,129 @@
 def swap_pieces(pieces):
     flat = pieces.reshape((-1,) + pieces.shape[2:])
     return lax.all_to_all(flat, "blk", 0, 0, tiled=True)
+
+
+def after(value, *others):
+    return lax.optimization_barrier((value,) + others)[0]
+
+
+def chip_walk(chips):
+    return list(range(0, chips, 2)) + list(range(chips - 1, 0, -2))
+
+
+class Walk:
+    def __init__(self, blocks):
+        self.blocks = blocks
+        self.chips = blocks // 2
+        self.short = blocks % 4 == 0 and self.chips <= 8
+        self.far = self.chips // 2
+        self.order = chip_walk(self.chips)
+        me = lax.axis_index("blk")
+        self.core = me % 2
+        place = jnp.array([self.order.index(chip) for chip in range(self.chips)], jnp.int32)[me // 2]
+        steps = jnp.arange(self.chips, dtype=jnp.int32) * (1 - 2 * self.core)
+        self.ahead = jnp.array(self.order, jnp.int32)[(place + steps) % self.chips]
+        places = [0]
+        for step in range(1, self.far):
+            places += [-step, step]
+        self.places = places + [self.far]
+
+    def advance(self, array):
+        pairs = []
+        for k in range(self.chips):
+            pairs.append((2 * self.order[k], 2 * self.order[(k + 1) % self.chips]))
+            pairs.append((2 * self.order[k] + 1, 2 * self.order[(k - 1) % self.chips] + 1))
+        return lax.ppermute(array, "blk", pairs)
+
+    def swap(self, array):
+        return lax.ppermute(array, "blk", [(k, k ^ 1) for k in range(self.blocks)])
+
+    def first_rows(self, index, rows):
+        place = self.places[index]
+        sibling_first = place > 0 and place != self.far
+        cores = (1 - self.core, self.core) if sibling_first else (self.core, 1 - self.core)
+        chip = self.ahead[place % self.chips]
+        return [(2 * chip + core) * rows for core in cores]
+
+    def spread(self, array):
+        if not self.short:
+            return [lax.all_gather(array, "blk", axis=0, tiled=True)]
+        rows = array.shape[0]
+        chain = jnp.concatenate([array, self.swap(array)], axis=0)
+        found = [chain]
+        for _ in range(1, self.far):
+            chain = self.advance(chain)
+            found += [chain, self.swap(chain)]
+        end = self.advance(chain[:rows])
+        return found + [jnp.concatenate([end, self.swap(end)], axis=0)]
+
+    def gather(self, array):
+        if not self.short:
+            return lax.all_gather(array, "blk", axis=0, tiled=True)
+        rows = array.shape[0]
+        whole = jnp.zeros((self.blocks * rows,) + array.shape[1:], array.dtype)
+        for index, block in enumerate(self.spread(array)):
+            for half, first in enumerate(self.first_rows(index, rows)):
+                piece = block[half * rows : (half + 1) * rows]
+                whole = lax.dynamic_update_slice_in_dim(whole, piece, first, 0)
+        return whole
+
+    def collect(self, part, chunks=1):
+        if not self.short:
+            return scatter_sum(part(0))
+
+        def total(kept, given):
+            return kept.astype(wide) + self.swap(given.astype(low)).astype(wide)
+
+        def split(block):
+            width = block.shape[1] // chunks
+            return [block[:, k * width : (k + 1) * width] for k in range(chunks)]
+
+        block = part(2 * self.far - 1)
+        rows = block.shape[0] // 2
+        chains = [
+            self.advance(total(piece[rows:], piece[:rows]).astype(low)) for piece in split(block)
+        ]
+        for step in range(self.far - 1, 0, -1):
+            ahead, behind = split(part(2 * step)), split(part(2 * step - 1))
+            for k in range(chunks):
+                terms = total(ahead[k], behind[k])
+                arrived = chains[k].astype(wide)
+                if step == self.far - 1:
+                    terms = jnp.concatenate([terms[:rows] + arrived, terms[rows:]], axis=0)
+                else:
+                    terms = terms + arrived
+                chains[k] = self.advance(terms.astype(low))
+        sums = [
+            total(own[:rows] + chain[rows:].astype(wide), own[rows:] + chain[:rows].astype(wide))
+            for own, chain in zip(split(part(0)), chains)
+        ]
+        return sums[0] if chunks == 1 else jnp.concatenate(sums, axis=1)
+
+    def collect_rows(self, part, pack_rows):
+        if not self.short:
+            return scatter_sum(part(lambda array: array))
+        rows = pack_rows // self.blocks
+
+        def of_block(index):
+            firsts = self.first_rows(index, rows)
+            return part(
+                lambda array: jnp.concatenate(
+                    [rows_at(array, first, rows) for first in firsts], axis=0
+                )
+            )
+
+        return self.collect(of_block)
+
+
+def sum_over_all(array, axes):
+    for axis in axes:
+        size = lax.axis_size(axis)
+        step = 1
+        while step < size:
+            array = array + lax.ppermute(array, axis, [(k, k ^ step) for k in range(size)])
+            step *= 2
+    return array
 
 
 def attend_kernel(query_ref, key_ref, value_ref, row_ids_ref, col_ids_ref, out_ref):
@@ -284,6 +413,7 @@
     head = me // copies
     part = me % copies
     kv_head = head // (P_HEADS // P_KV)
+    walk = Walk(blocks)
 
     def other_plane(array, step=1):
         return lax.ppermute(array, "grp", [(k, (k + step) % planes) for k in range(planes)])
@@ -302,17 +432,12 @@
             axis=0,
         )
 
-    def plane_sum(array):
-        mine = array.astype(low)
-        total = mine.astype(wide)
-        for step in range(1, planes):
-            total = total + other_plane(mine, step).astype(wide)
-        return total
+    def joined(blocks):
+        return blocks[0] if len(blocks) == 1 else jnp.concatenate(blocks, axis=0)
 
     def to_columns(weight):
         padded = jnp.pad(weight, ((0, 0), (0, unit_share * blocks - weight.shape[1])))
-        pieces = padded.reshape(weight.shape[0], blocks, unit_share)
-        return swap_pieces(jnp.transpose(pieces, (1, 0, 2)))
+        return jnp.transpose(padded.reshape(weight.shape[0], blocks, unit_share), (1, 0, 2))
 
     def share_rows(matrix):
         width = matrix.shape[0] // planes
@@ -328,26 +453,23 @@
             total = arrived if total is None else total + arrived
         return total
 
-    def share_columns(matrix):
-        width = matrix.shape[0] // planes
-        total = rows_at(matrix, plane * width, width)
+    def share_columns(matrix, last):
+        width = matrix.shape[0] // (planes * blocks)
+        pieces = matrix.astype(low).reshape(planes, blocks, width, -1)
+        arrived = swap_pieces(jnp.transpose(pieces, (1, 0, 2, 3)))
+        arrived = arrived.reshape(blocks, planes, width, -1)
+        arrived = after(arrived, last)
+        total = lax.dynamic_index_in_dim(arrived, plane, 1, keepdims=False).astype(wide)
         for step in range(1, planes):
-            piece = rows_at(matrix, (plane + step) % planes * width, width)
-            total = total + other_plane(piece.astype(low), step).astype(wide)
-        arrived = swap_pieces(total.astype(low).reshape(blocks, width // blocks, -1))
-        return arrived.reshape(blocks, width // blocks, -1).astype(wide)
+            piece = lax.dynamic_index_in_dim(
+                arrived, (plane + step) % planes, 1, keepdims=False
+            )
+            total = total + other_plane(piece, step).astype(wide)
+        return total
 
     head_pieces = lane_pad(qkv_weight.reshape(-1, 3, HEADS, HEAD))
     head_pieces = jnp.transpose(head_pieces, (2, 0, 1, 3)).reshape(HEADS, -1, 3 * LANES)
     head_weight = swap_pieces(jnp.repeat(head_pieces, copies, axis=0))
-    fc1_own = to_columns(fc1_weight)
-    fc2_own = to_columns(fc2_weight)
-    mixer_pieces = jnp.transpose(
-        mixer_weight.reshape(-1, blocks, model // blocks), (1, 0, 2)
-    )
-    mixer_own = swap_pieces(mixer_pieces)
-    out_full = gather(out_weight)
-    pair_weight = gather(jnp.concatenate([key_weight, value_weight], axis=1))
     fc1_bias_own = rows_at(
         jnp.pad(fc1_bias, (0, unit_share * blocks - hidden_units)), me * unit_share, unit_share
     )
@@ -361,11 +483,22 @@
 
     inputs = tokens.astype(wide)
     normed, first_norm_back = jax.vjp(layer_norm, inputs, ln1_gain, ln1_bias)
-    first_rows = gather(normed.astype(low))
-    all_ids = gather(segment_ids)
+    first_rows = walk.gather(normed.astype(low))
+    all_ids = swap_pieces(jnp.tile(segment_ids[None, None], (blocks, 1, 1))).reshape(-1)
+    cotangent_both = both_planes(after(cotangent, first_rows))
+    out_full = gather(after(out_weight, first_rows))
+    pair_weight = gather(
+        after(jnp.concatenate([key_weight, value_weight], axis=1), first_rows)
+    )
     row_ids = all_ids[:, None]
     col_ids = all_ids[None, :]
     heads = (mat_times(first_rows, head_weight) + head_bias).astype(low)
+    fc1_weight, fc2_weight = lax.optimization_barrier((fc1_weight, fc2_weight, first_rows))[:2]
+    unit_weights = swap_pieces(
+        jnp.concatenate([to_columns(fc1_weight), to_columns(fc2_weight)], axis=2)
+    )
+    fc1_own = unit_weights[:, :unit_share]
+    fc2_own = unit_weights[:, unit_share:]
     attended_head = attend(heads, row_ids, col_ids)
     attended_pieces = swap_pieces(attended_head[:, :HEAD].reshape(blocks, rows, HEAD))
     attended_pieces = attended_pieces.reshape(blocks, rows, HEAD)[::copies]
@@ -373,77 +506,88 @@
     hidden_state = inputs + mat_times(attended, out_full) + out_bias
 
     second, second_norm_back = jax.vjp(layer_norm, hidden_state, ln2_gain, ln2_bias)
-    second_rows = gather(second.astype(low))
-    pre = mat_times(second_rows, fc1_own) + fc1_bias_own
-    act, gate_back = jax.vjp(smooth_gate, pre)
-    act_low = act.astype(low)
-    encoded = hidden_state + scatter_sum(mat_times_t(act_low, fc2_own)) + fc2_bias
-
-    bridge_rows = gather(encoded.astype(low))
-    bridge_act, bridge_act_back = jax.vjp(
-        swiglu, mat_times(bridge_rows, bridge_gate), mat_times(bridge_rows, bridge_up)
-    )
-    bridge_hidden = bridge_act.astype(low)
-    context = scatter_sum(mat_times(bridge_hidden, bridge_down))
+    second_blocks = walk.spread(second.astype(low))
+    pre_blocks = [mat_times(block, fc1_own) + fc1_bias_own for block in second_blocks]
+    act_blocks = [smooth_gate(pre).astype(low) for pre in pre_blocks]
+    encoded = walk.collect(lambda i: mat_times_t(act_blocks[i], fc2_own))
+    encoded = after(hidden_state + encoded + fc2_bias, pair_weight, cotangent_both)
+
+    bridge_blocks = walk.spread(encoded.astype(low))
+    gate_blocks = [mat_times(block, bridge_gate) for block in bridge_blocks]
+    up_blocks = [mat_times(block, bridge_up) for block in bridge_blocks]
+    hidden_blocks = [swiglu(gate, up).astype(low) for gate, up in zip(gate_blocks, up_blocks)]
+    context = walk.collect(lambda i: mat_times(hidden_blocks[i], bridge_down), 2)
 
     context_normed, context_norm_back = jax.vjp(rms_norm, context, context_gain)
     context_in = context_normed.astype(low)
-    patch_pairs = gather(mat_times(context_in, pair_weight).astype(low))
+    patch_pairs = walk.gather(mat_times(context_in, pair_weight).astype(low))
     latent_normed, latent_norm_back = jax.vjp(rms_norm, latents.astype(wide), latent_gain)
     latent_in = latent_normed.astype(low)
     latent_in_own = rows_at(latent_in, me * model_share, model_share, 1)
-    latent_proj = lax.psum(
-        jnp.concatenate(
-            [
-                mat_times(latent_in_own, query_weight),
-                mat_times(latent_in_own, key_weight),
-                mat_times(latent_in_own, value_weight),
-            ],
-            axis=1,
-        ),
-        "blk",
-    ).astype(low)
     query_width = P_HEADS * P_HEAD
     pair_width = P_KV * P_HEAD
 
+
+    def heads_of(matrix, count):
+        split = lane_pad(matrix.reshape(LATENTS, count, P_HEAD))
+        split = jnp.transpose(split, (1, 0, 2))
+        return jnp.repeat(split, blocks // count, axis=0)
+
+    latent_pieces = jnp.concatenate(
+        [
+            heads_of(mat_times(latent_in_own, query_weight), P_HEADS),
+            heads_of(mat_times(latent_in_own, key_weight), P_KV),
+            heads_of(mat_times(latent_in_own, value_weight), P_KV),
+        ],
+        axis=2,
+    ).astype(low)
+    mixer_pieces = jnp.transpose(mixer_weight.reshape(-1, blocks, model // blocks), (1, 0, 2))
+    latent_pieces, mixer_pieces = lax.optimization_barrier(
+        (latent_pieces, mixer_pieces, second_blocks[-1])
+    )[:2]
+    latent_proj = swap_pieces(latent_pieces).reshape(blocks, LATENTS, 3 * LANES)
+    latent_proj = jnp.sum(latent_proj.astype(wide), axis=0).astype(low)
+    mixer_own = swap_pieces(mixer_pieces)
+    latent_query = latent_proj[:, :LANES]
+    latent_key = latent_proj[:, LANES : 2 * LANES]
+    latent_value = latent_proj[:, 2 * LANES :]
+
     def head_of(matrix, first, index):
         return lane_pad(rows_at(matrix, first + index * P_HEAD, P_HEAD, 1))
 
-    latent_query = head_of(latent_proj, 0, head)
-    latent_key = head_of(latent_proj, query_width, kv_head)
-    latent_value = head_of(latent_proj, query_width + pair_width, kv_head)
     patch_key = head_of(patch_pairs, 0, kv_head)
     patch_value = head_of(patch_pairs, pair_width, kv_head)
     attended_latent_head = resample(
         latent_query, patch_key, patch_value, latent_key, latent_value, col_ids, images
     )[:, :P_HEAD]
-    attended_latent = gather(attended_latent_head).reshape(blocks, lat_rows, P_HEAD)[::copies]
+    attended_latent = walk.gather(attended_latent_head).reshape(blocks, lat_rows, P_HEAD)[::copies]
     attended_latent = jnp.transpose(attended_latent, (1, 0, 2)).reshape(lat_rows, query_width)
-    mixed = gather(mat_times(attended_latent, mixer_own).astype(low))
+    mixed = walk.gather(mat_times(attended_latent, mixer_own).astype(low))
     mixed = jnp.transpose(mixed.reshape(blocks, lat_rows, -1), (1, 0, 2)).reshape(lat_rows, model)
     latent_state = jnp.tile(latents.astype(wide), (images, 1)) + mixed.astype(wide)
 
     post_in = rms_norm(latent_state, post_gain).astype(low)
-    latent_act, latent_act_back = jax.vjp(
-        swiglu, mat_times(post_in, latent_gate), mat_times(post_in, latent_up)
-    )
-    latent_hidden = latent_act.astype(low)
+    latent_gate_pre = mat_times(post_in, latent_gate)
+    latent_up_pre = mat_times(post_in, latent_up)
+    latent_hidden = swiglu(latent_gate_pre, latent_up_pre).astype(low)
     own_start = me * lat_own
     state_own = rows_at(latent_state, own_start, lat_own)
-    latent_gate_grad, latent_up_grad = latent_act_back(mat_times_t(cotangent, latent_down))
+    latent_gate_grad, latent_up_grad = swiglu_back(
+        latent_gate_pre, latent_up_pre, mat_times_t(cotangent, latent_down)
+    )
     latent_gate_low = latent_gate_grad.astype(low)
     latent_up_low = latent_up_grad.astype(low)
-    post_grad = scatter_sum(
-        mat_times_t(latent_gate_low, latent_gate) + mat_times_t(latent_up_low, latent_up)
-    )
+    post_part = mat_times_t(latent_gate_low, latent_gate) + mat_times_t(latent_up_low, latent_up)
+    post_part = post_part.astype(low)
+    post_grad = walk.collect_rows(lambda take: take(post_part), lat_rows)
     _, post_norm_back = jax.vjp(rms_norm, state_own, post_gain)
     state_norm_grad, post_gain_part = post_norm_back(post_grad)
     state_grad = rows_at(cotangent, own_start, lat_own).astype(wide) + state_norm_grad
-    state_low = gather(state_grad.astype(low))
-    resid_part = lax.dynamic_update_slice_in_dim(
-        jnp.zeros((LATENTS, model), wide), state_grad, own_start % LATENTS, 0
-    )
-    latents_out = (state_own + scatter_sum(mat_times(latent_hidden, latent_down))).astype(low)
+    state_low = walk.gather(state_grad.astype(low))
+    resid = jnp.sum(state_low.astype(wide).reshape(images, LATENTS, model), axis=0)
+    resid_low = resid.astype(low)
+    resid_others = [other_plane(resid_low, step) for step in range(1, planes)]
+    latent_down_rows = scatter_sum(mat_times(latent_hidden, latent_down))
 
     latent_att_grad = mat_times_t(state_low, mixer_weight).astype(low)
     if copies > 1:
@@ -468,21 +612,60 @@
     patch_grad = jnp.transpose(patch_grad, (1, 2, 0, 3)).reshape(rows, 2 * pair_width).astype(low)
     context_grad, context_gain_part = context_norm_back(mat_times_t(patch_grad, pair_weight))
 
-    context_rows = gather(context_grad.astype(low))
-    bridge_gate_grad, bridge_up_grad = bridge_act_back(mat_times_t(context_rows, bridge_down))
-    bridge_gate_low = bridge_gate_grad.astype(low)
-    bridge_up_low = bridge_up_grad.astype(low)
-    grad_bridge_down = plane_sum(outer_sum(bridge_hidden, context_rows))
-    encoded_grad = scatter_sum(
-        mat_times_t(bridge_gate_low, bridge_gate) + mat_times_t(bridge_up_low, bridge_up)
-    )
-    grad_bridge_gate = plane_sum(outer_sum(bridge_rows, bridge_gate_low))
-    grad_bridge_up = plane_sum(outer_sum(bridge_rows, bridge_up_low))
-
-    encoded_rows = gather(encoded_grad.astype(low))
+    units_both = both_planes(
+        jnp.concatenate([latent_gate_low, latent_up_low, latent_hidden], axis=1)
+    )
+    post_both = both_planes(post_in)
+    lat_units = latent_hidden.shape[1]
+    mixer_width = mixer_weight.shape[0]
+    grad_mixer = share_rows(
+        outer_sum(rows_at(attended_latent_head, part * mixer_width, mixer_width, 1), state_low)
+    )
+
+    context_blocks = walk.spread(context_grad.astype(low))
+    units_both = after(units_both, context_blocks[len(context_blocks) // 2])
+    grad_latent_gate = outer_sum(post_both, units_both[:, :lat_units])
+    grad_latent_up = outer_sum(post_both, units_both[:, lat_units : 2 * lat_units])
+    grad_latent_down = outer_sum(units_both[:, 2 * lat_units :], cotangent_both)
+    context_in_columns = swap_pieces(
+        jnp.transpose(context_in.reshape(rows, blocks, model_share), (1, 0, 2))
+    )
+    patch_grad_rows = gather(patch_grad)
+    grad_pair = share_rows(outer_sum(context_in_columns, patch_grad_rows))
+    latent_table = jnp.concatenate(
+        [query_part * scale_latent, latent_key_part * scale_latent, latent_value_part], axis=1
+    )
+    latent_total = latent_table
+    for step in range(1, planes):
+        latent_total = latent_total + other_plane(latent_table, step)
+    part_bridge_down = outer_sum(joined(hidden_blocks), joined(context_blocks)).astype(low)
+    part_bridge_down = after(part_bridge_down, grad_pair, grad_mixer, latent_total, resid_others)
+    down_others = [other_plane(part_bridge_down, step) for step in range(1, planes)]
+    context_blocks[-1] = after(context_blocks[-1], part_bridge_down)
+    bridge_grads = [
+        swiglu_back(gate, up, mat_times_t(block, bridge_down))
+        for gate, up, block in zip(gate_blocks, up_blocks, context_blocks)
+    ]
+    gate_low_blocks = [gate.astype(low) for gate, _ in bridge_grads]
+    up_low_blocks = [up.astype(low) for _, up in bridge_grads]
+    encoded_grad = walk.collect(
+        lambda i: mat_times_t(gate_low_blocks[i], bridge_gate)
+        + mat_times_t(up_low_blocks[i], bridge_up)
+    )
+    bridge_rows = joined(bridge_blocks)
+    part_bridge_gate = outer_sum(bridge_rows, joined(gate_low_blocks)).astype(low)
+    part_bridge_up = outer_sum(bridge_rows, joined(up_low_blocks)).astype(low)
+    part_bridge_pair = jnp.concatenate([part_bridge_gate, part_bridge_up], axis=1)
+    pair_others = [other_plane(part_bridge_pair, step) for step in range(1, planes)]
+
+    encoded_blocks = walk.spread(encoded_grad.astype(low))
     grad_fc2_bias = jnp.sum(encoded_grad, axis=0)
-    pre_grad = gate_back(mat_times(encoded_rows, fc2_own))[0].astype(low)
-    second_grad = scatter_sum(mat_times_t(pre_grad, fc1_own))
+    pre_grad_blocks = [
+        jax.vjp(smooth_gate, pre)[1](mat_times(block, fc2_own))[0].astype(low)
+        for pre, block in zip(pre_blocks, encoded_blocks)
+    ]
+    second_grad = walk.collect(lambda i: mat_times_t(pre_grad_blocks[i], fc1_own))
+    pre_grad = joined(pre_grad_blocks)
     grad_fc1_bias = jnp.sum(pre_grad.astype(wide), axis=0)
     hidden_norm_grad, grad_ln2_gain, grad_ln2_bias = second_norm_back(second_grad)
     hidden_grad = encoded_grad + hidden_norm_grad
@@ -494,90 +677,97 @@
     attended_grad = swap_pieces(jnp.repeat(lane_pad(attended_grad), copies, axis=0))
     query_low, key_low, value_low = attend_back(heads, attended_grad, row_ids, col_ids)
     head_grad = jnp.concatenate([query_low, key_low, value_low], axis=1)
-    first_part = mat_times_t(head_grad, head_weight)
+    first_weight = head_weight
     if copies > 1:
-        first_part = jnp.where(part == 0, first_part, 0.0)
-    first_grad = scatter_sum(first_part)
+        first_weight = jnp.where(part == 0, head_weight, jnp.zeros((), low))
+    first_grad = walk.collect_rows(
+        lambda take: mat_times_t(take(head_grad), first_weight), pack_rows
+    )
     input_norm_grad, grad_ln1_gain, grad_ln1_bias = first_norm_back(first_grad)
     grad_tokens = hidden_grad + input_norm_grad
 
     hidden_rows = gather(hidden_low)
     out_width = out_weight.shape[0]
-    grad_out = share_rows(
-        outer_sum(rows_at(attended_head, part * out_width, out_width, 1), hidden_rows)
-    )
-    mixer_width = mixer_weight.shape[0]
-    grad_mixer = share_rows(
-        outer_sum(rows_at(attended_latent_head, part * mixer_width, mixer_width, 1), state_low)
-    )
-    grad_fc1 = outer_sum(second_rows, pre_grad)
-    grad_fc2 = outer_sum(encoded_rows, act_low)
-    units = share_columns(jnp.concatenate([grad_fc1, grad_fc2], axis=1))
+    grad_out = outer_sum(rows_at(attended_head, part * out_width, out_width, 1), hidden_rows)
+    grad_out = share_rows(after(grad_out, first_grad))
+    grad_fc1 = outer_sum(joined(second_blocks), pre_grad)
+    grad_fc2 = outer_sum(joined(encoded_blocks), joined(act_blocks))
+    units = share_columns(jnp.concatenate([grad_fc1, grad_fc2], axis=1), first_grad)
     units = jnp.transpose(
         units.reshape(blocks, units.shape[1], 2, unit_share), (2, 1, 0, 3)
     ).reshape(2, units.shape[1], -1)[:, :, :hidden_units]
-    grad_qkv = share_columns(outer_sum(first_rows, head_grad))[::copies]
+    grad_qkv = share_columns(outer_sum(first_rows, head_grad), first_grad)[::copies]
     grad_qkv = grad_qkv.reshape(HEADS, grad_qkv.shape[1], 3, LANES)[..., :HEAD]
     grad_qkv = jnp.transpose(grad_qkv, (1, 2, 0, 3)).reshape(-1, 3 * features)
-    context_in_columns = swap_pieces(
-        jnp.transpose(context_in.reshape(rows, blocks, model_share), (1, 0, 2))
-    )
-    grad_pair = share_rows(outer_sum(context_in_columns, gather(patch_grad)))
-
-    post_both = both_planes(post_in)
-    grad_latent_gate = outer_sum(post_both, both_planes(latent_gate_low))
-    grad_latent_up = outer_sum(post_both, both_planes(latent_up_low))
-    grad_latent_down = outer_sum(both_planes(latent_hidden), both_planes(cotangent))
-
     once = (part == 0).astype(wide)
-
-    def placed(width, pieces):
-        base = jnp.zeros((LATENTS, width), wide)
-        return lax.dynamic_update_slice_in_dim(base, pieces[0][:, :P_HEAD] * once, pieces[1], 1)
 
     def spread(width, piece, first):
         return lax.dynamic_update_slice_in_dim(jnp.zeros((width,), wide), piece, first, 0)
 
-    latent_sums = lax.psum(
-        (
-            placed(query_width, (query_part, head * P_HEAD)),
-            placed(pair_width, (latent_key_part, kv_head * P_HEAD)),
-            placed(pair_width, (latent_value_part, kv_head * P_HEAD)),
-            resid_part,
-            context_gain_part,
-            post_gain_part,
-        ),
-        ("grp", "blk"),
-    )
+    def packed(arrays):
+        flat = jnp.concatenate([array.reshape(-1) for array in arrays])
+        gap = -flat.shape[0] % (8 * LANES)
+        return jnp.pad(flat, (0, gap)).reshape(-1, LANES)
+
+    def unpacked(table, arrays):
+        flat = table.reshape(-1)
+        first = 0
+        pieces = []
+        for array in arrays:
+            pieces.append(flat[first : first + array.size].reshape(array.shape))
+            first += array.size
+        return pieces
+
     query_bias_part = jnp.sum(query_low[:, :HEAD].astype(wide), axis=0) * once
     value_bias_part = jnp.sum(value_low[:, :HEAD].astype(wide), axis=0) * once
-    small = lax.psum(
-        (
-            grad_ln1_gain,
-            grad_ln1_bias,
-            spread(features, query_bias_part, head * HEAD),
-            spread(features, value_bias_part, head * HEAD),
-            grad_out_bias,
-            grad_ln2_gain,
-            grad_ln2_bias,
-            spread(unit_share * blocks, grad_fc1_bias, me * unit_share),
-            grad_fc2_bias,
-        ),
-        ("grp", "blk"),
-    )
-
-    query_grad = (latent_sums[0] * scale_latent).astype(low)
-    pair_grad = jnp.concatenate([latent_sums[1] * scale_latent, latent_sums[2]], axis=1)
+    small_terms = (
+        grad_ln1_gain,
+        grad_ln1_bias,
+        spread(features, query_bias_part, head * HEAD),
+        spread(features, value_bias_part, head * HEAD),
+        grad_out_bias,
+        grad_ln2_gain,
+        grad_ln2_bias,
+        spread(unit_share * blocks, grad_fc1_bias, me * unit_share),
+        grad_fc2_bias,
+        context_gain_part,
+        post_gain_part,
+    )
+    small = unpacked(sum_over_all(packed(small_terms), ("grp", "blk")), small_terms)
+    def plane_sum(mine, others):
+        others = lax.optimization_barrier((others, first_grad))[0]
+        return functools.reduce(
+            lambda total, other: total + other.astype(wide), others, mine.astype(wide)
+        )
+
+    bridge_units = bridge_gate.shape[1]
+    grad_bridge_down = plane_sum(part_bridge_down, down_others)
+    grad_bridge_gate = plane_sum(
+        part_bridge_gate, [other[:, :bridge_units] for other in pair_others]
+    )
+    grad_bridge_up = plane_sum(part_bridge_up, [other[:, bridge_units:] for other in pair_others])
+    latents_out = (state_own + after(latent_down_rows, first_grad)).astype(low)
+
+    latent_tables = walk.gather(after(latent_total, encoded_grad).astype(low))
+    latent_tables = latent_tables.reshape(blocks, LATENTS, 3, LANES)[::copies, :, :, :P_HEAD]
+    query_grad = jnp.transpose(latent_tables[:, :, 0], (1, 0, 2)).reshape(LATENTS, query_width)
+    pair_grad = jnp.sum(
+        latent_tables[:, :, 1:]
+        .astype(wide)
+        .reshape(P_KV, P_HEADS // P_KV, LATENTS, 2, P_HEAD),
+        axis=1,
+    )
+    pair_grad = jnp.transpose(pair_grad, (1, 2, 0, 3)).reshape(LATENTS, 2 * pair_width)
     pair_grad = pair_grad.astype(low)
     latent_in_grad = (
         mat_times_t(query_grad, query_weight)
         + mat_times_t(pair_grad[:, :pair_width], key_weight)
         + mat_times_t(pair_grad[:, pair_width:], value_weight)
     )
-    latent_in_grad = gather(latent_in_grad).reshape(blocks, LATENTS, model_share)
+    latent_in_grad = walk.gather(latent_in_grad).reshape(blocks, LATENTS, model_share)
     latent_in_grad = jnp.transpose(latent_in_grad, (1, 0, 2)).reshape(LATENTS, model)
     latent_grad, grad_latent_gain = latent_norm_back(latent_in_grad)
-    grad_latents = latent_sums[3] + latent_grad
+    grad_latents = latent_grad + plane_sum(resid_low, resid_others)
     share = model // (planes * blocks)
     latent_in_share = rows_at(latent_in, (plane * blocks + me) * share, share, 1)
     grad_query = outer_sum(latent_in_share, query_grad)
@@ -601,14 +791,14 @@
         grad_bridge_gate,
         grad_bridge_up,
         grad_bridge_down,
-        latent_sums[4],
+        small[9],
         grad_latents,
         grad_latent_gain,
         grad_query,
         grad_pair[:, :pair_width],
         grad_pair[:, pair_width:],
         grad_mixer,
-        latent_sums[5],
+        small[10],
         grad_latent_gate,
         grad_latent_up,
         grad_latent_down,

time: 2040 us -> 1520 us (0.75)
  waiting for transfers between devices: 1250 us -> 537 us
  blocking collectives: 204 us -> 0 us
  local copies, waits for them, and re-layouts: 79.5 us -> 264 us
  starting transfers between devices: 80.6 us -> 199 us
  other arithmetic: 81.4 us -> 143 us
  matrix products: 263 us -> 295 us
    all_gather x13 -> x4, waiting for transfers between devices: 486 us -> 0.04 us  [gather(): return lax.all_gather(array, 'blk', axis=0, tiled=True)]
    reduce_scatter x7 -> x1, waiting for transfers between devices: 442 us -> 0.01 us  [scatter_sum(): lax.psum_scatter(array.astype(low), 'blk', scatter_dimension=0, tiled=True)]
    ppermute x0 -> x167, waiting for transfers between devices: none -> 376 us  [the longest x72 361 us: advance(): return lax.ppermute(array, 'blk', pairs)]
    ppermute x10 -> x9, waiting for transfers between devices: 290 us -> 49 us  [other_plane(): lax.ppermute(array, 'grp', [(k, (k + step) % planes) for k in range(plane...]
    psum x2 -> x0, blocking collectives: 115 us -> none  [the longest x1 69.3 us: on_device(): lax.psum(jnp.concatenate([mat_times(latent_in_own, query_weight), mat_tim...]
    ppermute x0 -> x167, starting transfers between devices: none -> 115 us  [the longest x72 82 us: advance(): return lax.ppermute(array, 'blk', pairs)]
    all_to_all x9 -> x11, waiting for transfers between devices: 26.9 us -> 97.5 us  [swap_pieces(): return lax.all_to_all(flat, 'blk', 0, 0, tiled=True)]
    all_gather x2 -> x0, blocking collectives: 64.4 us -> none  [gather(): return lax.all_gather(array, 'blk', axis=0, tiled=True)]
  transfers between devices with their start and end apart: 46 -> 198, of which waited for: 27 -> 82; matrix products, arithmetic and copies ran while one was open for 11% -> 43% of each run, Pallas kernels for 2% -> 3%
where the time goes in v2:
time: 1520 us; the launch traced here: 1510 us
  waiting for transfers between devices  537 us (35%)
  matrix products  295 us (19%)
  local copies, waits for them, and re-layouts  264 us (17%)
  starting transfers between devices  199 us (13%)
  other arithmetic  143 us (9%)
  Pallas kernels  47.5 us (3%)
  between operations  23.4 us (2%)
    ppermute x72, waiting for transfers between devices, advance(): return lax.ppermute(array, 'blk', pairs)  361 us
    dot_general x71, matrix products, contract(): lax.dot_general(left, right, (((left_dim,), (right_dim,)), ((), ())), pre...  198 us
    all_to_all x11, waiting for transfers between devices, swap_pieces(): return lax.all_to_all(flat, 'blk', 0, 0, tiled=True)  97.5 us
    dot_general x50, matrix products, mat_times(): return jnp.dot(left, right, preferred_element_type=wide)  96.2 us
    ppermute x72, starting transfers between devices, advance(): return lax.ppermute(array, 'blk', pairs)  82 us
    unnamed x460, local copies, waits for them, and re-layouts  80.5 us
    all_to_all x11, starting transfers between devices, swap_pieces(): return lax.all_to_all(flat, 'blk', 0, 0, tiled=True)  62.1 us
    dynamic_update_slice x101, local copies, waits for them, and re-layouts, gather(): whole = lax.dynamic_update_slice_in_dim(whole, piece, first, 0)  59.9 us
  transfers between devices with their start and end apart: 198, of which 82 were waited for; matrix products, arithmetic and copies ran while one was open for 43% of the time, Pallas kernels for 3%

profile of v2, /device:TPU:10, one launch (start us, length us, event | category | flops | bytes accessed | tf_op | source)
XLA Modules:
  0.0 1508.8 jit_solution(9147454474262165894)
XLA Ops:
  32.9 6.8 collective-permute-done.3
  44.2 5.4 collective-permute-done.5
  62.2 6.4 all-to-all-start.1
  73.5 5.7 all-to-all-start
  82.1 27.9 %all-to-all-done = bf16[16,72,384]{2,1,0:T(8,128)(2,1)S(1)} async-done(((bf16[16,72,384]{2,1,0:T(8,128)(2,1)}), bf16[16,72,384]{2,1,0:T(8,128)(2,1)S(1)}, u32[]{:S(2)}, u32[]{:S(2)}) %all-to-all-start) | async-done | bytes 884768 | tf_op jit(solution)/shard_map/all_to_all | solution.py:81
  110.1 6.6 add_convert_fusion.query_ref.key_ref.value_ref
  116.7 12.7 vision_attend.1
  131.3 6.8 all-to-all-start.2
  147.6 5.9 all-to-all-start.4
  164.1 34.8 %all-to-all-done.4 = bf16[16,72,538]{2,1,0:T(8,128)(2,1)S(1)} async-done(((bf16[16,72,538]{2,1,0:T(8,128)(2,1)}), bf16[16,72,538]{2,1,0:T(8,128)(2,1)S(1)}, u32[]{:S(2)}, u32[]{:S(2)}) %all-to-all-start.4) | async-done | bytes 1239584 | tf_op jit(solution)/shard_map/all_to_all | solution.py:81
  201.0 12.7 collective-permute-done.10
  222.6 13.1 collective-permute-done.11
  240.8 7.1 collective-permute-done.12
  263.5 5.4 collective-permute-done.22
  270.8 8.2 collective-permute-done.23
  280.0 9.1 collective-permute-done.24
  290.2 9.1 collective-permute-done.25
  307.7 5.5 collective-permute-done.29
  333.7 7.9 collective-permute-done.35
  373.8 6.2 collective-permute-done.41
  380.3 5.3 collective-permute-done.50
  389.1 7.7 collective-permute-done.42
  396.8 11.2 collective-permute-done.51
  414.5 9.8 collective-permute-done.43
  424.3 11.2 collective-permute-done.52
  438.6 5.6 fusion.305
  446.1 6.6 collective-permute-done.44
  456.8 7.1 collective-permute-done.53
  497.0 5.4 all-to-all-start.5
  509.8 14.7 collective-permute-done.58
  642.0 6.1 multiply_convert_fusion.4
  652.7 6.9 fusion
  667.9 5.5 collective-permute-done.87
  683.5 7.0 convolution_convert_fusion.1
  711.0 49.0 %collective-permute-done.181 = bf16[256,3072]{1,0:T(8,128)(2,1)S(1)} collective-permute-done((bf16[256,3072]{1,0:T(8,128)(2,1)}, bf16[256,3072]{1,0:T(8,128)(2,1)S(1)}, u32[]{:S(2)}, u32[]{:S(2)}) %collective-permute-start.181) | collective-permute-done | bytes 1572896 | tf_op jit(solution)/shard_map/ppermute | solution.py:419
  782.2 6.2 resampler_attend_back.1
  807.8 14.4 all-to-all-done.6
  822.1 5.3 all-to-all-start.7
  830.4 6.1 multiply_reduce_fusion
  856.5 6.0 collective-permute-done.115
  862.5 9.0 collective-permute-done.114
  875.2 6.5 constant_dynamic-update-slice_fusion.86
  883.7 12.7 collective-permute-done.101
  900.1 6.8 constant_dynamic-update-slice_fusion.85
  916.1 22.2 %collective-permute-done.104 = bf16[256,4096]{1,0:T(8,128)(2,1)} collective-permute-done((bf16[256,4096]{1,0:T(8,128)(2,1)}, bf16[256,4096]{1,0:T(8,128)(2,1)}, u32[]{:S(2)}, u32[]{:S(2)}) %collective-permute-start.104) | collective-permute-done | bytes 2097184 | tf_op jit(solution)/shard_map/ppermute | solution.py:114
  959.1 10.3 fusion.5
  969.4 8.5 fusion.4
  983.2 5.5 constant_dynamic-update-slice_fusion.82
  998.6 8.5 fusion.32
  1015.8 22.2 %convolution_convert_fusion = bf16[896,4096]{1,0:T(8,128)(2,1)} fusion(bf16[2048,896]{1,0:T(8,128)(2,1)} %get-tuple-element.319, bf16[2048,4096]{1,0:T(8,128)(2,1)} %constant_dynamic-update-slice_fusion.12), kind=kOutput, calls=%fused_computation.2 | convolution fusion | flops 15036055552 | bytes 27787264 | tf_op jit(solution)/shard_map/dot_general | solution.py:48
  1168.6 8.3 collective-permute-done.128
  1179.4 7.4 collective-permute-done.131
  1210.0 7.3 collective-permute-done.138
  1220.6 6.8 collective-permute-done.139
  1231.3 6.3 collective-permute-done.140
  1246.2 6.4 all-to-all-start.8
  1267.1 25.3 %vision_attend_back.1 = (bf16[2048,128]{1,0:T(8,128)(2,1)}, bf16[2048,128]{1,0:T(8,128)(2,1)}, bf16[2048,128]{1,0:T(8,128)(2,1)}) custom-call(bf16[2048,384]{1,0:T(8,128)(2,1)} %add_convert_fusion.query_ref.key_ref.value_ref, bf16[2048,384]{1,0:T(8,128)(2,1)} %add_convert_fusion.query_ref.key_ref.value_ref, ...), custom_call_target="tpu_custom_call" | custom-call | tf_op jit(solution)/shard_map/vision_attend_back/pallas_call | solution.py:278
  1340.1 5.9 convolution_convert_fusion.7
  1351.8 22.7 %collective-permute-done.148 = bf16[256,1152]{1,0:T(8,128)(2,1)} collective-permute-done((bf16[256,1152]{1,0:T(8,128)(2,1)}, bf16[256,1152]{1,0:T(8,128)(2,1)}, u32[]{:S(2)}, u32[]{:S(2)}) %collective-permute-start.148) | collective-permute-done | bytes 589856 | tf_op jit(solution)/shard_map/ppermute | solution.py:114
  1398.2 9.9 all-to-all-done.9
  1427.1 14.5 convert_add_fusion
  1452.9 5.6 copy.299
  1458.5 5.9 copy.300
  1492.1 5.7 slice_reduce_fusion
  (1320 shorter events, 834.8 us)
Async XLA Ops:
  7.2 146.3 %all-gather.5.cloned.1.call-start = ((), (), s32[]{:S(2)}) async-start(), calls=%async_computation.12 | async-start | bytes 2820096 | tf_op jit(solution)/shard_map/all_gather | solution.py:66
  73.5 36.6 %all-to-all-start = ((bf16[16,72,384]{2,1,0:T(8,128)(2,1)}), bf16[16,72,384]{2,1,0:T(8,128)(2,1)S(1)}, u32[]{:S(2)}, u32[]{:S(2)}) async-start(bf16[16,72,384]{2,1,0:T(8,128)(2,1)} %all_to_all.53), calls=%async_computation | async-start | bytes 1769472 | tf_op jit(solution)/shard_map/all_to_all | solution.py:81
  131.3 15.5 %all-to-all-start.2 = ((bf16[16,128,72]{1,2,0:T(8,128)(2,1)}), bf16[16,128,72]{1,2,0:T(8,128)(2,1)S(1)}, u32[]{:S(2)}, u32[]{:S(2)}) async-start(bf16[16,128,72]{1,2,0:T(8,128)(2,1)} %copy.255), calls=%async_computation.2 | async-start | bytes 589824 | tf_op jit(solution)/shard_map/all_to_all | solution.py:81
  147.6 51.4 %all-to-all-start.4 = ((bf16[16,72,538]{2,1,0:T(8,128)(2,1)}), bf16[16,72,538]{2,1,0:T(8,128)(2,1)S(1)}, u32[]{:S(2)}, u32[]{:S(2)}) async-start(bf16[16,72,538]{2,1,0:T(8,128)(2,1)} %pad_maximum_fusion.10), calls=%async_computation.4 | async-start | bytes 2949120 | tf_op jit(solution)/shard_map/all_to_all | solution.py:81
  153.5 147.6 %all-gather.7.cloned.1.call-start = ((), (), s32[]{:S(2)}) async-start(), calls=%async_computation.13 | async-start | bytes 6684672 | tf_op jit(solution)/shard_map/all_gather | solution.py:66
  161.9 51.7 %collective-permute-start.10 = (bf16[256,1152]{1,0:T(8,128)(2,1)}, bf16[256,1152]{1,0:T(8,128)(2,1)}, u32[]{:S(2)}, u32[]{:S(2)}) collective-permute-start(bf16[256,1152]{1,0:T(8,128)(2,1)} %pad_maximum_fusion.17), channel_id=1, source_target_pairs={{0,4},{1,3},{4,8},{5,1},{8,12},{9,5},{12,14},{13,9},{14,10},{15,13... | collective-permute-start | bytes 1769480 | tf_op jit(solution)/shard_map/ppermute | solution.py:114
  213.6 24.4 %collective-permute-start.15 = (bf16[256,1152]{1,0:T(8,128)(2,1)}, bf16[256,1152]{1,0:T(8,128)(2,1)S(1)}, u32[]{:S(2)}, u32[]{:S(2)}) collective-permute-start(bf16[256,1152]{1,0:T(8,128)(2,1)} %collective-permute-done.10), channel_id=1, source_target_pairs={{0,1},{1,0},{2,3},{3,2},{4,5},{5,4},{6,7},{7,6},{8,9},{9,8},{10,11... | collective-permute-start | bytes 1769480 | tf_op jit(solution)/shard_map/ppermute | solution.py:117
  215.8 19.9 %collective-permute-start.11 = (bf16[256,1152]{1,0:T(8,128)(2,1)}, bf16[256,1152]{1,0:T(8,128)(2,1)S(1)}, u32[]{:S(2)}, u32[]{:S(2)}) collective-permute-start(bf16[256,1152]{1,0:T(8,128)(2,1)} %collective-permute-done.10), channel_id=1, source_target_pairs={{0,4},{1,3},{4,8},{5,1},{8,12},{9,5},{12,14},{13,9},{14,10},{15,13... | collective-permute-start | bytes 1769480 | tf_op jit(solution)/shard_map/ppermute | solution.py:114
  331.2 57.4 %collective-permute-start.34 = (bf16[256,2048]{1,0:T(8,128)(2,1)S(1)}, bf16[256,2048]{1,0:T(8,128)(2,1)S(1)}, u32[]{:S(2)}, u32[]{:S(2)}) collective-permute-start(bf16[256,2048]{1,0:T(8,128)(2,1)S(1)} %get-tuple-element.379), channel_id=1, source_target_pairs={{0,1},{1,0},{2,3},{3,2},{4,5},{5,4},{6,7},{7,6},{8,9},{9,8},{10,11... | collective-permute-start | bytes 3145736 | tf_op jit(solution)/shard_map/ppermute | solution.py:117
  348.9 22.0 %collective-permute-start.37 = (bf16[256,2048]{1,0:T(8,128)(2,1)S(1)}, bf16[256,2048]{1,0:T(8,128)(2,1)S(1)}, u32[]{:S(2)}, u32[]{:S(2)}) collective-permute-start(bf16[256,2048]{1,0:T(8,128)(2,1)S(1)} %get-tuple-element.383), channel_id=1, source_target_pairs={{0,1},{1,0},{2,3},{3,2},{4,5},{5,4},{6,7},{7,6},{8,9},{9,8},{10,11... | collective-permute-start | bytes 3145736 | tf_op jit(solution)/shard_map/ppermute | solution.py:117
  349.4 21.4 %collective-permute-start.48 = (bf16[256,2048]{1,0:T(8,128)(2,1)S(1)}, bf16[256,2048]{1,0:T(8,128)(2,1)S(1)}, u32[]{:S(2)}, u32[]{:S(2)}) collective-permute-start(bf16[256,2048]{1,0:T(8,128)(2,1)S(1)} %get-tuple-element.384), channel_id=1, source_target_pairs={{0,1},{1,0},{2,3},{3,2},{4,5},{5,4},{6,7},{7,6},{8,9},{9,8},{10,11... | collective-permute-start | bytes 3145736 | tf_op jit(solution)/shard_map/ppermute | solution.py:117
  369.9 19.2 %collective-permute-start.47 = (bf16[256,2048]{1,0:T(8,128)(2,1)S(1)}, bf16[256,2048]{1,0:T(8,128)(2,1)S(1)}, u32[]{:S(2)}, u32[]{:S(2)}) collective-permute-start(bf16[256,2048]{1,0:T(8,128)(2,1)S(1)} %get-tuple-element.380), channel_id=1, source_target_pairs={{0,1},{1,0},{2,3},{3,2},{4,5},{5,4},{6,7},{7,6},{8,9},{9,8},{10,11... | collective-permute-start | bytes 3145736 | tf_op jit(solution)/shard_map/ppermute | solution.py:117
  380.2 16.6 %collective-permute-start.42 = (bf16[256,2048]{1,0:T(8,128)(2,1)S(1)}, bf16[256,2048]{1,0:T(8,128)(2,1)S(1)}, u32[]{:S(2)}, u32[]{:S(2)}) collective-permute-start(bf16[256,2048]{1,0:T(8,128)(2,1)S(1)} %pad_maximum_fusion.11), channel_id=1, source_target_pairs={{0,4},{1,3},{4,8},{5,1},{8,12},{9,5},{12,14},{13,9},{14,10},{15,13... | collective-permute-start | bytes 3145736 | tf_op jit(solution)/shard_map/ppermute | solution.py:114
  385.8 22.3 %collective-permute-start.51 = (bf16[256,2048]{1,0:T(8,128)(2,1)S(1)}, bf16[256,2048]{1,0:T(8,128)(2,1)S(1)}, u32[]{:S(2)}, u32[]{:S(2)}) collective-permute-start(bf16[256,2048]{1,0:T(8,128)(2,1)S(1)} %pad_maximum_fusion.12), channel_id=1, source_target_pairs={{0,4},{1,3},{4,8},{5,1},{8,12},{9,5},{12,14},{13,9},{14,10},{15,13... | collective-permute-start | bytes 3145736 | tf_op jit(solution)/shard_map/ppermute | solution.py:114
  386.1 28.3 %collective-permute-start.31 = (bf16[256,2048]{1,0:T(8,128)(2,1)S(1)}, bf16[256,2048]{1,0:T(8,128)(2,1)S(1)}, u32[]{:S(2)}, u32[]{:S(2)}) collective-permute-start(bf16[256,2048]{1,0:T(8,128)(2,1)S(1)} %get-tuple-element.377), channel_id=1, source_target_pairs={{0,1},{1,0},{2,3},{3,2},{4,5},{5,4},{6,7},{7,6},{8,9},{9,8},{10,11... | collective-permute-start | bytes 3145736 | tf_op jit(solution)/shard_map/ppermute | solution.py:117
  388.6 25.9 %collective-permute-start.46 = (bf16[256,2048]{1,0:T(8,128)(2,1)S(1)}, bf16[256,2048]{1,0:T(8,128)(2,1)S(1)}, u32[]{:S(2)}, u32[]{:S(2)}) collective-permute-start(bf16[256,2048]{1,0:T(8,128)(2,1)S(1)} %get-tuple-element.378), channel_id=1, source_target_pairs={{0,1},{1,0},{2,3},{3,2},{4,5},{5,4},{6,7},{7,6},{8,9},{9,8},{10,11... | collective-permute-start | bytes 3145736 | tf_op jit(solution)/shard_map/ppermute | solution.py:117
  409.2 15.1 collective-permute-start.43
  409.5 26.0 %collective-permute-start.52 = (bf16[256,2048]{1,0:T(8,128)(2,1)S(1)}, bf16[256,2048]{1,0:T(8,128)(2,1)S(1)}, u32[]{:S(2)}, u32[]{:S(2)}) collective-permute-start(bf16[256,2048]{1,0:T(8,128)(2,1)S(1)} %get-tuple-element.350), channel_id=1, source_target_pairs={{0,4},{1,3},{4,8},{5,1},{8,12},{9,5},{12,14},{13,9},{14,10},{15,13... | collective-permute-start | bytes 3145736 | tf_op jit(solution)/shard_map/ppermute | solution.py:114
  437.6 15.1 %collective-permute-start.44 = (bf16[256,2048]{1,0:T(8,128)(2,1)}, bf16[256,2048]{1,0:T(8,128)(2,1)}, u32[]{:S(2)}, u32[]{:S(2)}) collective-permute-start(bf16[256,2048]{1,0:T(8,128)(2,1)} %get-tuple-element.347), channel_id=1, source_target_pairs={{0,4},{1,3},{4,8},{5,1},{8,12},{9,5},{12,14},{13,9},{14,10},{15,13... | collective-permute-start | bytes 3145736 | tf_op jit(solution)/shard_map/ppermute | solution.py:114
  444.2 19.7 %collective-permute-start.53 = (bf16[256,2048]{1,0:T(8,128)(2,1)S(1)}, bf16[256,2048]{1,0:T(8,128)(2,1)}, u32[]{:S(2)}, u32[]{:S(2)}) collective-permute-start(bf16[256,2048]{1,0:T(8,128)(2,1)S(1)} %get-tuple-element.348), channel_id=1, source_target_pairs={{0,4},{1,3},{4,8},{5,1},{8,12},{9,5},{12,14},{13,9},{14,10},{15,13... | collective-permute-start | bytes 3145736 | tf_op jit(solution)/shard_map/ppermute | solution.py:114
  473.4 23.6 %all-to-all-start.3 = ((bf16[16,64,384]{2,1,0:T(8,128)(2,1)}), bf16[16,64,384]{2,1,0:T(8,128)(2,1)}, u32[]{:S(2)}, u32[]{:S(2)}) async-start(bf16[16,64,384]{2,1,0:T(8,128)(2,1)} %pad_maximum_fusion.13), calls=%async_computation.3 | async-start | bytes 1572864 | tf_op jit(solution)/shard_map/all_to_all | solution.py:81
  488.4 16.6 %collective-permute-start.56 = (bf16[256,768]{1,0:T(8,128)(2,1)}, bf16[256,768]{1,0:T(8,128)(2,1)}, u32[]{:S(2)}, u32[]{:S(2)}) collective-permute-start(bf16[256,768]{1,0:T(8,128)(2,1)} %pad_maximum_fusion.25), channel_id=1, source_target_pairs={{0,4},{1,3},{4,8},{5,1},{8,12},{9,5},{12,14},{13,9},{14,10},{15,13... | collective-permute-start | bytes 1179656 | tf_op jit(solution)/shard_map/ppermute | solution.py:114
  497.0 88.5 %all-to-all-start.5 = ((bf16[16,96,256]{2,1,0:T(8,128)(2,1)}), bf16[16,96,256]{2,1,0:T(8,128)(2,1)}, u32[]{:S(2)}, u32[]{:S(2)}) async-start(bf16[16,96,256]{2,1,0:T(8,128)(2,1)} %copy.274), calls=%async_computation.5 | async-start | bytes 1572864 | tf_op jit(solution)/shard_map/all_to_all | solution.py:81
  502.4 371.1 %reduce-scatter.2.cloned.1.call-start = ((), (), s32[]{:S(2)}) async-start(), calls=%async_computation.14 | async-start | bytes 2228224 | tf_op jit(solution)/shard_map/reduce_scatter | solution.py:76
  505.0 19.4 %collective-permute-start.58 = (bf16[256,768]{1,0:T(8,128)(2,1)}, bf16[256,768]{1,0:T(8,128)(2,1)S(1)}, u32[]{:S(2)}, u32[]{:S(2)}) collective-permute-start(bf16[256,768]{1,0:T(8,128)(2,1)} %collective-permute-done.56), channel_id=1, source_target_pairs={{0,4},{1,3},{4,8},{5,1},{8,12},{9,5},{12,14},{13,9},{14,10},{15,13... | collective-permute-start | bytes 1179656 | tf_op jit(solution)/shard_map/ppermute | solution.py:114
  506.5 20.3 %collective-permute-start.57 = (bf16[256,768]{1,0:T(8,128)(2,1)}, bf16[256,768]{1,0:T(8,128)(2,1)S(1)}, u32[]{:S(2)}, u32[]{:S(2)}) collective-permute-start(bf16[256,768]{1,0:T(8,128)(2,1)} %collective-permute-done.56), channel_id=1, source_target_pairs={{0,1},{1,0},{2,3},{3,2},{4,5},{5,4},{6,7},{7,6},{8,9},{9,8},{10,11... | collective-permute-start | bytes 1179656 | tf_op jit(solution)/shard_map/ppermute | solution.py:117
  598.4 75.7 %collective-permute-start.27 = (bf16[256,4096]{1,0:T(8,128)(2,1)}, bf16[256,4096]{1,0:T(8,128)(2,1)S(1)}, u32[]{:S(2)}, u32[]{:S(2)}) collective-permute-start(bf16[256,4096]{1,0:T(8,128)(2,1)} %param.61), channel_id=1, source_target_pairs={{0,16},{16,0},{1,17},{17,1},{2,18},{18,2},{3,19},{19,3},{4,20},{20... | collective-permute-start | bytes 6291464 | tf_op jit(solution)/shard_map/ppermute | solution.py:419
  679.2 123.9 %collective-permute-start.180 = (bf16[256,4096]{1,0:T(8,128)(2,1)}, bf16[256,4096]{1,0:T(8,128)(2,1)}, u32[]{:S(2)}, u32[]{:S(2)}) collective-permute-start(bf16[256,4096]{1,0:T(8,128)(2,1)} %get-tuple-element.337), channel_id=1, source_target_pairs={{0,16},{16,0},{1,17},{17,1},{2,18},{18,2},{3,19},{19,3},{4,20},{20... | collective-permute-start | bytes 6291464 | tf_op jit(solution)/shard_map/ppermute | solution.py:419
  700.7 59.3 %collective-permute-start.181 = (bf16[256,3072]{1,0:T(8,128)(2,1)}, bf16[256,3072]{1,0:T(8,128)(2,1)S(1)}, u32[]{:S(2)}, u32[]{:S(2)}) collective-permute-start(bf16[256,3072]{1,0:T(8,128)(2,1)} %pad_maximum_fusion.9), channel_id=1, source_target_pairs={{0,16},{16,0},{1,17},{17,1},{2,18},{18,2},{3,19},{19,3},{4,20},{20... | collective-permute-start | bytes 4718600 | tf_op jit(solution)/shard_map/ppermute | solution.py:419
  707.8 56.2 %collective-permute-start.94 = (bf16[32,4096]{1,0:T(8,128)(2,1)S(1)}, bf16[32,4096]{1,0:T(8,128)(2,1)S(1)}, u32[]{:S(2)}, u32[]{:S(2)}) collective-permute-start(bf16[32,4096]{1,0:T(8,128)(2,1)S(1)} %collective-permute-done.92), channel_id=1, source_target_pairs={{0,4},{1,3},{4,8},{5,1},{8,12},{9,5},{12,14},{13,9},{14,10},{15,13... | collective-permute-start | bytes 786440 | tf_op jit(solution)/shard_map/ppermute | solution.py:114
  709.7 54.8 %collective-permute-start.93 = (bf16[32,4096]{1,0:T(8,128)(2,1)S(1)}, bf16[32,4096]{1,0:T(8,128)(2,1)S(1)}, u32[]{:S(2)}, u32[]{:S(2)}) collective-permute-start(bf16[32,4096]{1,0:T(8,128)(2,1)S(1)} %collective-permute-done.92), channel_id=1, source_target_pairs={{0,1},{1,0},{2,3},{3,2},{4,5},{5,4},{6,7},{7,6},{8,9},{9,8},{10,11... | collective-permute-start | bytes 786440 | tf_op jit(solution)/shard_map/ppermute | solution.py:117
  797.8 24.3 %all-to-all-start.6 = ((bf16[16,128,192]{1,2,0:T(8,128)(2,1)}), bf16[16,128,192]{1,2,0:T(8,128)(2,1)}, u32[]{:S(2)}, u32[]{:S(2)}) async-start(bf16[16,128,192]{1,2,0:T(8,128)(2,1)} %pad_maximum_fusion.14), calls=%async_computation.7 | async-start | bytes 1572864 | tf_op jit(solution)/shard_map/all_to_all | solution.py:81
  822.1 132.8 %all-to-all-start.7 = ((bf16[16,128,256]{2,1,0:T(8,128)(2,1)}), bf16[16,128,256]{2,1,0:T(8,128)(2,1)}, u32[]{:S(2)}, u32[]{:S(2)}) async-start(bf16[16,128,256]{2,1,0:T(8,128)(2,1)} %fusion.23), calls=%async_computation.8 | async-start | bytes 2097152 | tf_op jit(solution)/shard_map/all_to_all | solution.py:81
  827.4 127.5 %all-gather.9.cloned.1.call-start = ((), (), s32[]{:S(2)}) async-start(), calls=%async_computation.15 | async-start | bytes 3342336 | tf_op jit(solution)/shard_map/all_gather | solution.py:66
  843.6 18.9 %collective-permute-start.115 = (bf16[48,4096]{1,0:T(8,128)(2,1)}, bf16[48,4096]{1,0:T(8,128)(2,1)}, u32[]{:S(2)}, u32[]{:S(2)}) collective-permute-start(bf16[48,4096]{1,0:T(8,128)(2,1)} %get-tuple-element.422), channel_id=1, source_target_pairs={{0,1},{1,3},{2,5},{3,7},{4,9},{5,11},{6,13},{7,15},{8,17},{9,19},{... | collective-permute-start | bytes 1179656 | tf_op jit(solution)/shard_map/ppermute | solution.py:452
  845.1 26.4 %collective-permute-start.114 = (bf16[48,4096]{1,0:T(8,128)(2,1)S(1)}, bf16[48,4096]{1,0:T(8,128)(2,1)}, u32[]{:S(2)}, u32[]{:S(2)}) collective-permute-start(bf16[48,4096]{1,0:T(8,128)(2,1)S(1)} %get-tuple-element.421), channel_id=1, source_target_pairs={{0,0},{1,2},{2,4},{3,6},{4,8},{5,10},{6,12},{7,14},{8,16},{9,18},{... | collective-permute-start | bytes 1179656 | tf_op jit(solution)/shard_map/ppermute | solution.py:452
  851.6 186.4 %collective-permute-start.117 = (bf16[64,4096]{1,0:T(8,128)(2,1)}, bf16[64,4096]{1,0:T(8,128)(2,1)}, u32[]{:S(2)}, u32[]{:S(2)}) collective-permute-start(bf16[64,4096]{1,0:T(8,128)(2,1)} %reduce.5), channel_id=1, source_target_pairs={{0,16},{16,0},{1,17},{17,1},{2,18},{18,2},{3,19},{19,3},{4,20},{20... | collective-permute-start | bytes 1572872 | tf_op jit(solution)/shard_map/ppermute | solution.py:419
  855.9 40.6 %collective-permute-start.101 = (bf16[256,4096]{1,0:T(8,128)(2,1)}, bf16[256,4096]{1,0:T(8,128)(2,1)}, u32[]{:S(2)}, u32[]{:S(2)}) collective-permute-start(bf16[256,4096]{1,0:T(8,128)(2,1)} %pad_maximum_fusion.7), channel_id=1, source_target_pairs={{0,4},{1,3},{4,8},{5,1},{8,12},{9,5},{12,14},{13,9},{14,10},{15,13... | collective-permute-start | bytes 6291464 | tf_op jit(solution)/shard_map/ppermute | solution.py:114
  896.4 16.8 %collective-permute-start.102 = (bf16[256,4096]{1,0:T(8,128)(2,1)}, bf16[256,4096]{1,0:T(8,128)(2,1)S(1)}, u32[]{:S(2)}, u32[]{:S(2)}) collective-permute-start(bf16[256,4096]{1,0:T(8,128)(2,1)} %collective-permute-done.101), channel_id=1, source_target_pairs={{0,1},{1,0},{2,3},{3,2},{4,5},{5,4},{6,7},{7,6},{8,9},{9,8},{10,11... | collective-permute-start | bytes 6291464 | tf_op jit(solution)/shard_map/ppermute | solution.py:117
  899.1 39.2 %collective-permute-start.104 = (bf16[256,4096]{1,0:T(8,128)(2,1)}, bf16[256,4096]{1,0:T(8,128)(2,1)}, u32[]{:S(2)}, u32[]{:S(2)}) collective-permute-start(bf16[256,4096]{1,0:T(8,128)(2,1)} %collective-permute-done.101), channel_id=1, source_target_pairs={{0,4},{1,3},{4,8},{5,1},{8,12},{9,5},{12,14},{13,9},{14,10},{15,13... | collective-permute-start | bytes 6291464 | tf_op jit(solution)/shard_map/ppermute | solution.py:114
  909.5 170.4 %collective-permute-start.103 = (bf16[256,1152]{1,0:T(8,128)(2,1)}, bf16[256,1152]{1,0:T(8,128)(2,1)}, u32[]{:S(2)}, u32[]{:S(2)}) collective-permute-start(bf16[256,1152]{1,0:T(8,128)(2,1)} %fusion.6), channel_id=1, source_target_pairs={{0,1},{1,0},{2,3},{3,2},{4,5},{5,4},{6,7},{7,6},{8,9},{9,8},{10,11... | collective-permute-start | bytes 1769480 | tf_op jit(solution)/shard_map/ppermute | solution.py:117
  945.9 119.1 %collective-permute-start.106 = (bf16[256,1152]{1,0:T(8,128)(2,1)}, bf16[256,1152]{1,0:T(8,128)(2,1)}, u32[]{:S(2)}, u32[]{:S(2)}) collective-permute-start(bf16[256,1152]{1,0:T(8,128)(2,1)} %fusion.7), channel_id=1, source_target_pairs={{0,1},{1,0},{2,3},{3,2},{4,5},{5,4},{6,7},{7,6},{8,9},{9,8},{10,11... | collective-permute-start | bytes 1769480 | tf_op jit(solution)/shard_map/ppermute | solution.py:117
  946.4 31.6 %collective-permute-start.107 = (bf16[256,4096]{1,0:T(8,128)(2,1)}, bf16[256,4096]{1,0:T(8,128)(2,1)}, u32[]{:S(2)}, u32[]{:S(2)}) collective-permute-start(bf16[256,4096]{1,0:T(8,128)(2,1)} %collective-permute-done.104), channel_id=1, source_target_pairs={{0,4},{1,3},{4,8},{5,1},{8,12},{9,5},{12,14},{13,9},{14,10},{15,13... | collective-permute-start | bytes 6291464 | tf_op jit(solution)/shard_map/ppermute | solution.py:114
  979.3 27.9 %collective-permute-start.110 = (bf16[128,4096]{1,0:T(8,128)(2,1)S(1)}, bf16[128,4096]{1,0:T(8,128)(2,1)S(1)}, u32[]{:S(2)}, u32[]{:S(2)}) collective-permute-start(bf16[128,4096]{1,0:T(8,128)(2,1)S(1)} %slice.1035), channel_id=1, source_target_pairs={{0,4},{1,3},{4,8},{5,1},{8,12},{9,5},{12,14},{13,9},{14,10},{15,13... | collective-permute-start | bytes 3145736 | tf_op jit(solution)/shard_map/ppermute | solution.py:114
  979.6 28.6 %collective-permute-start.108 = (bf16[256,4096]{1,0:T(8,128)(2,1)}, bf16[256,4096]{1,0:T(8,128)(2,1)S(1)}, u32[]{:S(2)}, u32[]{:S(2)}) collective-permute-start(bf16[256,4096]{1,0:T(8,128)(2,1)} %collective-permute-done.107), channel_id=1, source_target_pairs={{0,1},{1,0},{2,3},{3,2},{4,5},{5,4},{6,7},{7,6},{8,9},{9,8},{10,11... | collective-permute-start | bytes 6291464 | tf_op jit(solution)/shard_map/ppermute | solution.py:117
  1008.3 139.7 %collective-permute-start.113 = (bf16[128,768]{1,0:T(8,128)(2,1)}, bf16[128,768]{1,0:T(8,128)(2,1)}, u32[]{:S(2)}, u32[]{:S(2)}) collective-permute-start(bf16[128,768]{1,0:T(8,128)(2,1)} %get-tuple-element.429), channel_id=1, source_target_pairs={{0,1},{1,3},{2,5},{3,7},{4,9},{5,11},{6,13},{7,15},{8,17},{9,19},{... | collective-permute-start | bytes 589832 | tf_op jit(solution)/shard_map/ppermute | solution.py:452
  1013.3 39.7 %collective-permute-start.109 = (bf16[256,1152]{1,0:T(8,128)(2,1)S(1)}, bf16[256,1152]{1,0:T(8,128)(2,1)}, u32[]{:S(2)}, u32[]{:S(2)}) collective-permute-start(bf16[256,1152]{1,0:T(8,128)(2,1)S(1)} %fusion.8), channel_id=1, source_target_pairs={{0,1},{1,0},{2,3},{3,2},{4,5},{5,4},{6,7},{7,6},{8,9},{9,8},{10,11... | collective-permute-start | bytes 1769480 | tf_op jit(solution)/shard_map/ppermute | solution.py:117
  1049.9 100.3 %collective-permute-start.112 = (bf16[128,768]{1,0:T(8,128)(2,1)}, bf16[128,768]{1,0:T(8,128)(2,1)}, u32[]{:S(2)}, u32[]{:S(2)}) collective-permute-start(bf16[128,768]{1,0:T(8,128)(2,1)} %get-tuple-element.428), channel_id=1, source_target_pairs={{0,0},{1,2},{2,4},{3,6},{4,8},{5,10},{6,12},{7,14},{8,16},{9,18},{... | collective-permute-start | bytes 589832 | tf_op jit(solution)/shard_map/ppermute | solution.py:452
  1065.0 359.1 %collective-permute-start.161 = (bf16[896,4096]{1,0:T(8,128)(2,1)}, bf16[896,4096]{1,0:T(8,128)(2,1)}, u32[]{:S(2)}, u32[]{:S(2)}) collective-permute-start(bf16[896,4096]{1,0:T(8,128)(2,1)} %convolution_convert_fusion), channel_id=1, source_target_pairs={{0,16},{16,0},{1,17},{17,1},{2,18},{18,2},{3,19},{19,3},{4,20},{20... | collective-permute-start | bytes 22020104 | tf_op jit(solution)/shard_map/ppermute | solution.py:419
  1124.4 260.2 %collective-permute-start.160 = (bf16[1152,1792]{0,1:T(8,128)(2,1)}, bf16[1152,1792]{0,1:T(8,128)(2,1)}, u32[]{:S(2)}, u32[]{:S(2)}) collective-permute-start(bf16[1152,1792]{0,1:T(8,128)(2,1)} %pad_maximum_fusion.2), channel_id=1, source_target_pairs={{0,16},{16,0},{1,17},{17,1},{2,18},{18,2},{3,19},{19,3},{4,20},{20... | collective-permute-start | bytes 12386312 | tf_op jit(solution)/shard_map/ppermute | solution.py:419
  1127.3 34.6 %collective-permute-start.125 = (bf16[256,1152]{1,0:T(8,128)(2,1)}, bf16[256,1152]{1,0:T(8,128)(2,1)}, u32[]{:S(2)}, u32[]{:S(2)}) collective-permute-start(bf16[256,1152]{1,0:T(8,128)(2,1)} %pad_maximum_fusion.21), channel_id=1, source_target_pairs={{0,4},{1,3},{4,8},{5,1},{8,12},{9,5},{12,14},{13,9},{14,10},{15,13... | collective-permute-start | bytes 1769480 | tf_op jit(solution)/shard_map/ppermute | solution.py:114
  1189.2 19.5 %collective-permute-start.178 = (f32[64,256]{1,0:T(8,128)S(1)}, f32[64,256]{1,0:T(8,128)S(1)}, u32[]{:S(2)}, u32[]{:S(2)}) collective-permute-start(f32[64,256]{1,0:T(8,128)S(1)} %get-tuple-element.446), channel_id=1, source_target_pairs={{0,4},{1,3},{4,8},{5,1},{8,12},{9,5},{12,14},{13,9},{14,10},{15,13... | collective-permute-start | bytes 196616 | tf_op jit(solution)/shard_map/ppermute | solution.py:114
  1246.2 20.0 %all-to-all-start.8 = ((bf16[16,128,128]{1,2,0:T(8,128)(2,1)}), bf16[16,128,128]{1,2,0:T(8,128)(2,1)S(1)}, u32[]{:S(2)}, u32[]{:S(2)}) async-start(bf16[16,128,128]{1,2,0:T(8,128)(2,1)} %pad.51), calls=%async_computation.9 | async-start | bytes 1048576 | tf_op jit(solution)/shard_map/all_to_all | solution.py:81
  1298.5 16.2 %collective-permute-start.145 = (bf16[128,1152]{1,0:T(8,128)(2,1)}, bf16[128,1152]{1,0:T(8,128)(2,1)}, u32[]{:S(2)}, u32[]{:S(2)}) collective-permute-start(bf16[128,1152]{1,0:T(8,128)(2,1)} %slice.1420), channel_id=1, source_target_pairs={{0,1},{1,0},{2,3},{3,2},{4,5},{5,4},{6,7},{7,6},{8,9},{9,8},{10,11... | collective-permute-start | bytes 884744 | tf_op jit(solution)/shard_map/ppermute | solution.py:117
  1318.9 17.4 %collective-permute-start.143 = (bf16[256,1152]{1,0:T(8,128)(2,1)}, bf16[256,1152]{1,0:T(8,128)(2,1)}, u32[]{:S(2)}, u32[]{:S(2)}) collective-permute-start(bf16[256,1152]{1,0:T(8,128)(2,1)} %convolution_convert_fusion.11), channel_id=1, source_target_pairs={{0,1},{1,0},{2,3},{3,2},{4,5},{5,4},{6,7},{7,6},{8,9},{9,8},{10,11... | collective-permute-start | bytes 1769480 | tf_op jit(solution)/shard_map/ppermute | solution.py:117
  1327.1 52.2 %all-to-all-start.10 = ((bf16[32,36,538]{2,1,0:T(8,128)(2,1)}), bf16[32,36,538]{2,1,0:T(8,128)(2,1)}, u32[]{:S(2)}, u32[]{:S(2)}) async-start(bf16[32,36,538]{2,1,0:T(8,128)(2,1)} %bitcast.379), calls=%async_computation.11 | async-start | bytes 3276800 | tf_op jit(solution)/shard_map/all_to_all | solution.py:81
  1334.6 17.2 %collective-permute-start.142 = (bf16[256,1152]{1,0:T(8,128)(2,1)}, bf16[256,1152]{1,0:T(8,128)(2,1)}, u32[]{:S(2)}, u32[]{:S(2)}) collective-permute-start(bf16[256,1152]{1,0:T(8,128)(2,1)} %convolution_convert_fusion.12), channel_id=1, source_target_pairs={{0,1},{1,0},{2,3},{3,2},{4,5},{5,4},{6,7},{7,6},{8,9},{9,8},{10,11... | collective-permute-start | bytes 1769480 | tf_op jit(solution)/shard_map/ppermute | solution.py:117
  1338.6 35.9 %collective-permute-start.148 = (bf16[256,1152]{1,0:T(8,128)(2,1)}, bf16[256,1152]{1,0:T(8,128)(2,1)}, u32[]{:S(2)}, u32[]{:S(2)}) collective-permute-start(bf16[256,1152]{1,0:T(8,128)(2,1)} %add_convert_fusion.2), channel_id=1, source_target_pairs={{0,4},{1,3},{4,8},{5,1},{8,12},{9,5},{12,14},{13,9},{14,10},{15,13... | collective-permute-start | bytes 1769480 | tf_op jit(solution)/shard_map/ppermute | solution.py:114
  1379.3 28.8 %all-to-all-start.9 = ((bf16[32,36,384]{2,1,0:T(8,128)(2,1)}), bf16[32,36,384]{2,1,0:T(8,128)(2,1)}, u32[]{:S(2)}, u32[]{:S(2)}) async-start(bf16[32,36,384]{2,1,0:T(8,128)(2,1)} %bitcast.385), calls=%async_computation.10 | async-start | bytes 1966080 | tf_op jit(solution)/shard_map/all_to_all | solution.py:81
  1384.5 100.1 %all-gather.11.cloned.1.call-start = ((), (), s32[]{:S(2)}) async-start(), calls=%async_computation.16 | async-start | bytes 5013504 | tf_op jit(solution)/shard_map/all_gather | solution.py:66
  1392.5 17.6 %collective-permute-start.150 = (bf16[128,1152]{1,0:T(8,128)(2,1)}, bf16[128,1152]{1,0:T(8,128)(2,1)}, u32[]{:S(2)}, u32[]{:S(2)}) collective-permute-start(bf16[128,1152]{1,0:T(8,128)(2,1)} %fusion.60), channel_id=1, source_target_pairs={{0,1},{1,0},{2,3},{3,2},{4,5},{5,4},{6,7},{7,6},{8,9},{9,8},{10,11... | collective-permute-start | bytes 884744 | tf_op jit(solution)/shard_map/ppermute | solution.py:117
  1413.7 28.0 %collective-permute-start.151 = (f32[176,128]{1,0:T(8,128)}, f32[176,128]{1,0:T(8,128)S(1)}, u32[]{:S(2)}, u32[]{:S(2)}) collective-permute-start(f32[176,128]{1,0:T(8,128)} %pad_bitcast_fusion.2), channel_id=1, source_target_pairs={{0,16},{16,0},{1,17},{17,1},{2,18},{18,2},{3,19},{19,3},{4,20},{20... | collective-permute-start | bytes 270344 | tf_op jit(solution)/shard_map/ppermute | solution.py:202
  1417.4 50.7 %collective-permute-start.156 = (bf16[16,36,384]{2,0,1:T(8,128)(2,1)}, bf16[16,36,384]{2,0,1:T(8,128)(2,1)}, u32[]{:S(2)}, u32[]{:S(2)}) collective-permute-start(bf16[16,36,384]{2,0,1:T(8,128)(2,1)} %bitcast.320), channel_id=1, source_target_pairs={{0,16},{16,0},{1,17},{17,1},{2,18},{18,2},{3,19},{19,3},{4,20},{20... | collective-permute-start | bytes 1327112 | tf_op jit(solution)/shard_map/ppermute | solution.py:419
  1423.8 54.9 %collective-permute-start.159 = (bf16[16,36,538]{2,0,1:T(8,128)(2,1)}, bf16[16,36,538]{2,0,1:T(8,128)(2,1)}, u32[]{:S(2)}, u32[]{:S(2)}) collective-permute-start(bf16[16,36,538]{2,0,1:T(8,128)(2,1)} %bitcast.319), channel_id=1, source_target_pairs={{0,16},{16,0},{1,17},{17,1},{2,18},{18,2},{3,19},{19,3},{4,20},{20... | collective-permute-start | bytes 1859336 | tf_op jit(solution)/shard_map/ppermute | solution.py:419
  (343 other events, 3099.2 us)
Sparse Core Ops, SparseCore 0:
  61.7 52.2 all-gather.4
  159.1 81.5 all-gather.6
  700.9 61.1 reduce-scatter.1
  875.3 52.1 all-gather.8
  1397.0 56.7 all-gather.10

commit v3 on v2

--- a/solution.py
+++ b/solution.py
@@ -123,35 +123,62 @@
         chip = self.ahead[place % self.chips]
         return [(2 * chip + core) * rows for core in cores]
 
-    def spread(self, array):
+    def spread(self, array, fill=()):
         if not self.short:
+            for work in fill:
+                work(array)
             return [lax.all_gather(array, "blk", axis=0, tiled=True)]
         rows = array.shape[0]
         chain = jnp.concatenate([array, self.swap(array)], axis=0)
         found = [chain]
-        for _ in range(1, self.far):
-            chain = self.advance(chain)
+        made = ()
+        for step in range(1, self.far):
+            sent = after(chain, *made) if made else chain
+            chain = self.advance(sent)
+            made = fill[step - 1](sent) if step <= len(fill) else ()
             found += [chain, self.swap(chain)]
-        end = self.advance(chain[:rows])
+        end = self.advance((after(chain, *made) if made else chain)[:rows])
         return found + [jnp.concatenate([end, self.swap(end)], axis=0)]
 
-    def gather(self, array):
+    def in_order(self, found):
         if not self.short:
-            return lax.all_gather(array, "blk", axis=0, tiled=True)
-        rows = array.shape[0]
-        whole = jnp.zeros((self.blocks * rows,) + array.shape[1:], array.dtype)
-        for index, block in enumerate(self.spread(array)):
+            return found[0]
+        rows = found[0].shape[0] // 2
+        whole = jnp.zeros((self.blocks * rows,) + found[0].shape[1:], found[0].dtype)
+        for index, block in enumerate(found):
             for half, first in enumerate(self.first_rows(index, rows)):
                 piece = block[half * rows : (half + 1) * rows]
                 whole = lax.dynamic_update_slice_in_dim(whole, piece, first, 0)
         return whole
 
-    def collect(self, part, chunks=1):
+    def gather(self, array, fill=()):
+        return self.in_order(self.spread(array, fill))
+
+    def in_own_order(self, array):
         if not self.short:
-            return scatter_sum(part(0))
-
-        def total(kept, given):
-            return kept.astype(wide) + self.swap(given.astype(low)).astype(wide)
+            return array
+        rows = array.shape[0] // self.blocks
+        firsts = [first for index in range(2 * self.far) for first in self.first_rows(index, rows)]
+        return jnp.concatenate([rows_at(array, first, rows) for first in firsts], axis=0)
+
+    def device_order(self):
+        if not self.short:
+            return jnp.arange(self.blocks, dtype=jnp.int32)
+        return jnp.stack(
+            [first for index in range(2 * self.far) for first in self.first_rows(index, 1)]
+        )
+
+    def collect(self, part, chunks=1, fill=()):
+        if not self.short:
+            terms = part(0)
+            for work in fill:
+                work(terms)
+            return scatter_sum(terms)
+
+        def total(kept, given, sent=()):
+            given = given.astype(low)
+            given = self.swap(after(given, *sent) if sent else given)
+            return kept.astype(wide) + given.astype(wide)
 
         def split(block):
             width = block.shape[1] // chunks
@@ -159,28 +186,32 @@
 
         block = part(2 * self.far - 1)
         rows = block.shape[0] // 2
-        chains = [
-            self.advance(total(piece[rows:], piece[:rows]).astype(low)) for piece in split(block)
-        ]
+        sent = tuple(total(piece[rows:], piece[:rows]).astype(low) for piece in split(block))
+        chains = [self.advance(one) for one in sent]
+        made = fill[0](sent[0]) if fill else ()
         for step in range(self.far - 1, 0, -1):
             ahead, behind = split(part(2 * step)), split(part(2 * step - 1))
+            before, sent = sent, ()
             for k in range(chunks):
-                terms = total(ahead[k], behind[k])
+                terms = total(ahead[k], behind[k], before)
                 arrived = chains[k].astype(wide)
                 if step == self.far - 1:
                     terms = jnp.concatenate([terms[:rows] + arrived, terms[rows:]], axis=0)
                 else:
                     terms = terms + arrived
-                chains[k] = self.advance(terms.astype(low))
+                terms = terms.astype(low)
+                sent += (after(terms, *made) if made else terms,)
+                chains[k] = self.advance(sent[-1])
+            made = fill[self.far - step](sent[0]) if self.far - step < len(fill) else ()
         sums = [
             total(own[:rows] + chain[rows:].astype(wide), own[rows:] + chain[:rows].astype(wide))
             for own, chain in zip(split(part(0)), chains)
         ]
         return sums[0] if chunks == 1 else jnp.concatenate(sums, axis=1)
 
-    def collect_rows(self, part, pack_rows):
+    def collect_rows(self, part, pack_rows, fill=()):
         if not self.short:
-            return scatter_sum(part(lambda array: array))
+            return self.collect(lambda _: part(lambda array: array), fill=fill)
         rows = pack_rows // self.blocks
 
         def of_block(index):
@@ -191,7 +222,7 @@
                 )
             )
 
-        return self.collect(of_block)
+        return self.collect(of_block, fill=fill)
 
 
 def sum_over_all(array, axes):
@@ -390,6 +421,60 @@
     return jnp.pad(array, gap)
 
 
+def context_back_kernel(
+    order_ref, context_ref, grad_ref, weight_ref, gain_ref, out_ref, scale_ref, gain_grad_ref
+):
+    step = pl.program_id(0)
+    grads = mat_times(grad_ref[...], weight_ref[...])
+    values = context_ref[...].astype(wide)
+    scale = lax.rsqrt(jnp.mean(values * values, axis=-1, keepdims=True) + norm_eps)
+    unit = values * scale
+    scaled = grads * gain_ref[...]
+    share = jnp.mean(scaled * unit, axis=-1, keepdims=True)
+    out_ref[...] = (scale * (scaled - unit * share)).astype(low)
+    scale_ref[...] = scale
+    gain_grad = jnp.sum(grads * unit, axis=0, keepdims=True)
+
+    @pl.when(step == 0)
+    def _():
+        gain_grad_ref[...] = gain_grad
+
+    @pl.when(step > 0)
+    def _():
+        gain_grad_ref[...] += gain_grad
+
+
+def context_back(order, context, grads, weight, gain):
+    pack_rows, model = context.shape
+    rows = pack_rows // order.shape[0]
+    width = grads.shape[1]
+    return pl.pallas_call(
+        context_back_kernel,
+        out_shape=[
+            jax.ShapeDtypeStruct((pack_rows, model), low),
+            jax.ShapeDtypeStruct((pack_rows, 1), wide),
+            jax.ShapeDtypeStruct((1, model), wide),
+        ],
+        grid_spec=pltpu.PrefetchScalarGridSpec(
+            num_scalar_prefetch=1,
+            grid=(order.shape[0],),
+            in_specs=[
+                pl.BlockSpec((rows, model), lambda i, order: (order[i], 0)),
+                pl.BlockSpec((rows, width), lambda i, order: (i, 0)),
+                pl.BlockSpec((width, model), lambda i, order: (0, 0)),
+                pl.BlockSpec((1, model), lambda i, order: (0, 0)),
+            ],
+            out_specs=[
+                pl.BlockSpec((rows, model), lambda i, order: (i, 0)),
+                pl.BlockSpec((rows, 1), lambda i, order: (i, 0)),
+                pl.BlockSpec((1, model), lambda i, order: (0, 0)),
+            ],
+        ),
+        compiler_params=pltpu.CompilerParams(vmem_limit_bytes=vmem_bytes),
+        name="context_back",
+    )(order, context, grads, weight, gain[None, :])
+
+
 def on_device(
     tokens, segment_ids, ln1_gain, ln1_bias, qkv_weight, q_bias, v_bias, out_weight, out_bias,
     ln2_gain, ln2_bias, fc1_weight, fc1_bias, fc2_weight, fc2_bias, bridge_gate, bridge_up,
@@ -418,18 +503,24 @@
     def other_plane(array, step=1):
         return lax.ppermute(array, "grp", [(k, (k + step) % planes) for k in range(planes)])
 
-    def both_planes(array):
-        pieces = [array] + [other_plane(array, step) for step in range(1, planes)]
+    def shared_from_other_plane(array):
+        core = me % 2
+        half = array.shape[0] // 2
+        own = other_plane(rows_at(array, core * half, half))
+        sibling = walk.swap(own)
         return jnp.concatenate(
-            [
-                functools.reduce(
-                    lambda held, step: jnp.where((plane - step) % planes == k, pieces[step], held),
-                    range(1, planes),
-                    pieces[0],
-                )
-                for k in range(planes)
-            ],
-            axis=0,
+            [jnp.where(core == 0, own, sibling), jnp.where(core == 0, sibling, own)], axis=0
+        )
+
+    def in_plane_order(array, other):
+        return jnp.concatenate(
+            [jnp.where(plane == 0, array, other), jnp.where(plane == 0, other, array)], axis=0
+        )
+
+    def plane_sum(mine, others, last):
+        others = lax.optimization_barrier((others, last))[0]
+        return functools.reduce(
+            lambda total, other: total + other.astype(wide), others, mine.astype(wide)
         )
 
     def joined(blocks):
@@ -453,12 +544,12 @@
             total = arrived if total is None else total + arrived
         return total
 
-    def share_columns(matrix, last):
+    def column_pieces(matrix):
         width = matrix.shape[0] // (planes * blocks)
-        pieces = matrix.astype(low).reshape(planes, blocks, width, -1)
-        arrived = swap_pieces(jnp.transpose(pieces, (1, 0, 2, 3)))
-        arrived = arrived.reshape(blocks, planes, width, -1)
-        arrived = after(arrived, last)
+        return jnp.transpose(matrix.reshape(planes, blocks, width, -1), (1, 0, 2, 3))
+
+    def plane_share(arrived):
+        arrived = arrived.reshape((blocks, planes, -1) + arrived.shape[2:])
         total = lax.dynamic_index_in_dim(arrived, plane, 1, keepdims=False).astype(wide)
         for step in range(1, planes):
             piece = lax.dynamic_index_in_dim(
@@ -467,9 +558,33 @@
             total = total + other_plane(piece, step).astype(wide)
         return total
 
+    made = {}
+
+    def filler(names, make):
+        def work(sent):
+            results = make(sent)
+            made.update(zip(names, results))
+            return tuple(results)
+
+        return work
+
+    def nothing(_):
+        return ()
+
     head_pieces = lane_pad(qkv_weight.reshape(-1, 3, HEADS, HEAD))
     head_pieces = jnp.transpose(head_pieces, (2, 0, 1, 3)).reshape(HEADS, -1, 3 * LANES)
-    head_weight = swap_pieces(jnp.repeat(head_pieces, copies, axis=0))
+    id_rows = jnp.pad(segment_ids.astype(low)[None, None, :], ((0, 0), (0, 7), (0, 0)))
+    id_rows = jnp.tile(id_rows, (blocks, 1, 3 * LANES // rows + 1))[..., : 3 * LANES]
+    head_pieces = jnp.concatenate(
+        [jnp.repeat(head_pieces, copies, axis=0), id_rows], axis=1
+    )
+
+    def bring_heads(sent):
+        arrived = swap_pieces(after(head_pieces, sent)).reshape(head_pieces.shape)
+        weight = arrived[:, : arrived.shape[1] - 8].reshape(-1, 3 * LANES)
+        ids = arrived[:, arrived.shape[1] - 8, :rows].reshape(-1)
+        return weight, ids.astype(jnp.int32)
+
     fc1_bias_own = rows_at(
         jnp.pad(fc1_bias, (0, unit_share * blocks - hidden_units)), me * unit_share, unit_share
     )
@@ -483,44 +598,51 @@
 
     inputs = tokens.astype(wide)
     normed, first_norm_back = jax.vjp(layer_norm, inputs, ln1_gain, ln1_bias)
-    first_rows = walk.gather(normed.astype(low))
-    all_ids = swap_pieces(jnp.tile(segment_ids[None, None], (blocks, 1, 1))).reshape(-1)
-    cotangent_both = both_planes(after(cotangent, first_rows))
+
+    def make_units(sent):
+        both = [to_columns(after(one, sent)) for one in (fc1_weight, fc2_weight)]
+        return (jnp.concatenate(both, axis=2),)
+
+    first_rows = walk.gather(
+        normed.astype(low),
+        [
+            filler(("unit_pieces",), make_units),
+            filler(("head_weight", "all_ids"), bring_heads),
+        ],
+    )
+    head_weight, all_ids = made["head_weight"], made["all_ids"]
+    cotangent = after(cotangent, first_rows)
     out_full = gather(after(out_weight, first_rows))
-    pair_weight = gather(
-        after(jnp.concatenate([key_weight, value_weight], axis=1), first_rows)
-    )
+    pair_half = jnp.where(plane == 0, key_weight, value_weight)
+    pair_half = gather(after(pair_half, out_full))
     row_ids = all_ids[:, None]
     col_ids = all_ids[None, :]
     heads = (mat_times(first_rows, head_weight) + head_bias).astype(low)
-    fc1_weight, fc2_weight = lax.optimization_barrier((fc1_weight, fc2_weight, first_rows))[:2]
-    unit_weights = swap_pieces(
-        jnp.concatenate([to_columns(fc1_weight), to_columns(fc2_weight)], axis=2)
-    )
+    unit_weights = swap_pieces(made["unit_pieces"])
     fc1_own = unit_weights[:, :unit_share]
     fc2_own = unit_weights[:, unit_share:]
-    attended_head = attend(heads, row_ids, col_ids)
+    attended_head = after(attend(heads, row_ids, col_ids), unit_weights)
     attended_pieces = swap_pieces(attended_head[:, :HEAD].reshape(blocks, rows, HEAD))
     attended_pieces = attended_pieces.reshape(blocks, rows, HEAD)[::copies]
     attended = jnp.transpose(attended_pieces, (1, 0, 2)).reshape(rows, features)
     hidden_state = inputs + mat_times(attended, out_full) + out_bias
 
     second, second_norm_back = jax.vjp(layer_norm, hidden_state, ln2_gain, ln2_bias)
-    second_blocks = walk.spread(second.astype(low))
+    cotangent_other = shared_from_other_plane(cotangent)
+
+    def use_cotangent(_):
+        return (cotangent_other,)
+
+    second_blocks = walk.spread(second.astype(low), [nothing, nothing, use_cotangent])
     pre_blocks = [mat_times(block, fc1_own) + fc1_bias_own for block in second_blocks]
     act_blocks = [smooth_gate(pre).astype(low) for pre in pre_blocks]
     encoded = walk.collect(lambda i: mat_times_t(act_blocks[i], fc2_own))
-    encoded = after(hidden_state + encoded + fc2_bias, pair_weight, cotangent_both)
+    encoded = after(hidden_state + encoded + fc2_bias, pair_half)
 
     bridge_blocks = walk.spread(encoded.astype(low))
     gate_blocks = [mat_times(block, bridge_gate) for block in bridge_blocks]
     up_blocks = [mat_times(block, bridge_up) for block in bridge_blocks]
     hidden_blocks = [swiglu(gate, up).astype(low) for gate, up in zip(gate_blocks, up_blocks)]
-    context = walk.collect(lambda i: mat_times(hidden_blocks[i], bridge_down), 2)
-
-    context_normed, context_norm_back = jax.vjp(rms_norm, context, context_gain)
-    context_in = context_normed.astype(low)
-    patch_pairs = walk.gather(mat_times(context_in, pair_weight).astype(low))
     latent_normed, latent_norm_back = jax.vjp(rms_norm, latents.astype(wide), latent_gain)
     latent_in = latent_normed.astype(low)
     latent_in_own = rows_at(latent_in, me * model_share, model_share, 1)
@@ -542,16 +664,40 @@
         axis=2,
     ).astype(low)
     mixer_pieces = jnp.transpose(mixer_weight.reshape(-1, blocks, model // blocks), (1, 0, 2))
-    latent_pieces, mixer_pieces = lax.optimization_barrier(
-        (latent_pieces, mixer_pieces, second_blocks[-1])
-    )[:2]
-    latent_proj = swap_pieces(latent_pieces).reshape(blocks, LATENTS, 3 * LANES)
-    latent_proj = jnp.sum(latent_proj.astype(wide), axis=0).astype(low)
-    mixer_own = swap_pieces(mixer_pieces)
+
+    def bring_latents(sent):
+        arrived = swap_pieces(after(latent_pieces, sent)).reshape(blocks, LATENTS, 3 * LANES)
+        return (jnp.sum(arrived.astype(wide), axis=0).astype(low),)
+
+    def bring_mixer(sent):
+        return (swap_pieces(after(mixer_pieces, sent)),)
+
+    def bring_pairs(sent):
+        halves = [after(one, sent) for one in (pair_half, other_half)]
+        key_full = jnp.where(plane == 0, halves[0], halves[1])
+        value_full = jnp.where(plane == 0, halves[1], halves[0])
+        pair_weight = jnp.concatenate([key_full, value_full], axis=1)
+        return pair_weight, jnp.transpose(pair_weight)
+
+    other_half = other_plane(pair_half)
+    context = walk.collect(
+        lambda i: mat_times(hidden_blocks[i], bridge_down),
+        2,
+        [
+            filler(("latent_proj",), bring_latents),
+            filler(("mixer_own",), bring_mixer),
+            filler(("pair_weight", "pair_turned"), bring_pairs),
+        ],
+    )
+    latent_proj, mixer_own = made["latent_proj"], made["mixer_own"]
+    pair_weight, pair_turned = made["pair_weight"], made["pair_turned"]
     latent_query = latent_proj[:, :LANES]
     latent_key = latent_proj[:, LANES : 2 * LANES]
     latent_value = latent_proj[:, 2 * LANES :]
 
+
+    context_in = rms_norm(context, context_gain).astype(low)
+    patch_pairs = walk.gather(mat_times(context_in, pair_weight).astype(low))
     def head_of(matrix, first, index):
         return lane_pad(rows_at(matrix, first + index * P_HEAD, P_HEAD, 1))
 
@@ -563,6 +709,7 @@
     attended_latent = walk.gather(attended_latent_head).reshape(blocks, lat_rows, P_HEAD)[::copies]
     attended_latent = jnp.transpose(attended_latent, (1, 0, 2)).reshape(lat_rows, query_width)
     mixed = walk.gather(mat_times(attended_latent, mixer_own).astype(low))
+    context_rows = gather(after(context.astype(low), mixed))
     mixed = jnp.transpose(mixed.reshape(blocks, lat_rows, -1), (1, 0, 2)).reshape(lat_rows, model)
     latent_state = jnp.tile(latents.astype(wide), (images, 1)) + mixed.astype(wide)
 
@@ -577,6 +724,8 @@
     )
     latent_gate_low = latent_gate_grad.astype(low)
     latent_up_low = latent_up_grad.astype(low)
+    lat_units = latent_hidden.shape[1]
+    units = jnp.concatenate([latent_gate_low, latent_up_low, latent_hidden], axis=1)
     post_part = mat_times_t(latent_gate_low, latent_gate) + mat_times_t(latent_up_low, latent_up)
     post_part = post_part.astype(low)
     post_grad = walk.collect_rows(lambda take: take(post_part), lat_rows)
@@ -586,8 +735,6 @@
     state_low = walk.gather(state_grad.astype(low))
     resid = jnp.sum(state_low.astype(wide).reshape(images, LATENTS, model), axis=0)
     resid_low = resid.astype(low)
-    resid_others = [other_plane(resid_low, step) for step in range(1, planes)]
-    latent_down_rows = scatter_sum(mat_times(latent_hidden, latent_down))
 
     latent_att_grad = mat_times_t(state_low, mixer_weight).astype(low)
     if copies > 1:
@@ -601,70 +748,122 @@
         )
     )
     scale_latent = P_HEAD ** (-0.5)
+    latent_table = jnp.concatenate(
+        [query_part * scale_latent, latent_key_part * scale_latent, latent_value_part], axis=1
+    )
+    latent_total = latent_table
+    for step in range(1, planes):
+        latent_total = latent_total + other_plane(latent_table, step)
     patch_part = jnp.concatenate(
         [patch_key_part[:, :P_HEAD] * scale_latent, patch_value_part[:, :P_HEAD]], axis=1
     ).astype(low)
     patch_part = swap_pieces(patch_part.reshape(blocks, rows, 2 * P_HEAD))
+    units_other = other_plane(after(units, latent_total))
+    post_other = shared_from_other_plane(after(post_in, latent_total))
+    patch_part = after(patch_part, context_rows)
     patch_part = patch_part.reshape(blocks, rows, 2, P_HEAD)[::copies].astype(wide)
     patch_grad = jnp.sum(
         patch_part.reshape(P_KV, P_HEADS // P_KV, rows, 2, P_HEAD), axis=1
     )
     patch_grad = jnp.transpose(patch_grad, (1, 2, 0, 3)).reshape(rows, 2 * pair_width).astype(low)
-    context_grad, context_gain_part = context_norm_back(mat_times_t(patch_grad, pair_weight))
-
-    units_both = both_planes(
-        jnp.concatenate([latent_gate_low, latent_up_low, latent_hidden], axis=1)
-    )
-    post_both = both_planes(post_in)
-    lat_units = latent_hidden.shape[1]
-    mixer_width = mixer_weight.shape[0]
-    grad_mixer = share_rows(
-        outer_sum(rows_at(attended_latent_head, part * mixer_width, mixer_width, 1), state_low)
-    )
-
-    context_blocks = walk.spread(context_grad.astype(low))
-    units_both = after(units_both, context_blocks[len(context_blocks) // 2])
-    grad_latent_gate = outer_sum(post_both, units_both[:, :lat_units])
-    grad_latent_up = outer_sum(post_both, units_both[:, lat_units : 2 * lat_units])
-    grad_latent_down = outer_sum(units_both[:, 2 * lat_units :], cotangent_both)
-    context_in_columns = swap_pieces(
-        jnp.transpose(context_in.reshape(rows, blocks, model_share), (1, 0, 2))
-    )
-    patch_grad_rows = gather(patch_grad)
-    grad_pair = share_rows(outer_sum(context_in_columns, patch_grad_rows))
-    latent_table = jnp.concatenate(
-        [query_part * scale_latent, latent_key_part * scale_latent, latent_value_part], axis=1
-    )
-    latent_total = latent_table
-    for step in range(1, planes):
-        latent_total = latent_total + other_plane(latent_table, step)
-    part_bridge_down = outer_sum(joined(hidden_blocks), joined(context_blocks)).astype(low)
-    part_bridge_down = after(part_bridge_down, grad_pair, grad_mixer, latent_total, resid_others)
+    latent_rows = gather(jnp.pad(latent_total.astype(low), ((0, 0), (0, LANES))))
+    patch_grad_rows = joined(walk.spread(patch_grad))
+    context_low, context_scale, context_gain_part = context_back(
+        walk.device_order(), context_rows, patch_grad_rows, pair_turned, context_gain
+    )
+    context_gain_part = jnp.where(me == 0, context_gain_part[0], 0.0)
+
+    size = bridge_blocks[0].shape[0]
+    context_blocks = [
+        context_low[k * size : (k + 1) * size] for k in range(len(bridge_blocks))
+    ]
+    gate_low, up_low = (
+        one.astype(low)
+        for one in swiglu_back(
+            joined(gate_blocks), joined(up_blocks), mat_times_t(context_low, bridge_down)
+        )
+    )
+    bridge_rows = joined(bridge_blocks)
+    hidden_joined = joined(hidden_blocks)
+
+    def encoded_terms(index):
+        span = slice(index * size, (index + 1) * size)
+        return mat_times_t(gate_low[span], bridge_gate) + mat_times_t(up_low[span], bridge_up)
+
+    def make_down(sent):
+        return (outer_sum(hidden_joined, after(context_low, sent)).astype(low),)
+
+    def make_gate(sent):
+        return (outer_sum(bridge_rows, after(gate_low, sent)).astype(low),)
+
+    def make_up(sent):
+        grad = outer_sum(bridge_rows, after(up_low, sent)).astype(low)
+        return grad, jnp.concatenate([made["gate"], grad], axis=1)
+
+    encoded_grad = walk.collect(
+        encoded_terms,
+        fill=[filler(("down",), make_down), filler(("gate",), make_gate), filler(("up", "gate_up"), make_up)],
+    )
+    part_bridge_down = made["down"]
     down_others = [other_plane(part_bridge_down, step) for step in range(1, planes)]
-    context_blocks[-1] = after(context_blocks[-1], part_bridge_down)
-    bridge_grads = [
-        swiglu_back(gate, up, mat_times_t(block, bridge_down))
-        for gate, up, block in zip(gate_blocks, up_blocks, context_blocks)
-    ]
-    gate_low_blocks = [gate.astype(low) for gate, _ in bridge_grads]
-    up_low_blocks = [up.astype(low) for _, up in bridge_grads]
-    encoded_grad = walk.collect(
-        lambda i: mat_times_t(gate_low_blocks[i], bridge_gate)
-        + mat_times_t(up_low_blocks[i], bridge_up)
-    )
-    bridge_rows = joined(bridge_blocks)
-    part_bridge_gate = outer_sum(bridge_rows, joined(gate_low_blocks)).astype(low)
-    part_bridge_up = outer_sum(bridge_rows, joined(up_low_blocks)).astype(low)
-    part_bridge_pair = jnp.concatenate([part_bridge_gate, part_bridge_up], axis=1)
-    pair_others = [other_plane(part_bridge_pair, step) for step in range(1, planes)]
-
-    encoded_blocks = walk.spread(encoded_grad.astype(low))
+    part_bridge_gate, part_bridge_up = made["gate"], made["up"]
+    pair_others = [other_plane(made["gate_up"], step) for step in range(1, planes)]
+
+    def rows_of_both(sent, array, other):
+        return in_plane_order(after(array, sent), after(other, sent))
+
+    def make_latent_gate(sent):
+        made["units"] = rows_of_both(sent, units, units_other)
+        made["post"] = rows_of_both(sent, post_in, post_other)
+        return (outer_sum(made["post"], made["units"][:, :lat_units]),)
+
+    def make_latent_up(sent):
+        both = after(made["units"], sent)
+        return (outer_sum(made["post"], both[:, lat_units : 2 * lat_units]),)
+
+    def make_latent_down(sent):
+        both = rows_of_both(sent, cotangent, cotangent_other)
+        return (outer_sum(made["units"][:, 2 * lat_units :], both),)
+
+    encoded_blocks = walk.spread(
+        encoded_grad.astype(low),
+        [
+            filler(("latent_gate",), make_latent_gate),
+            filler(("latent_up",), make_latent_up),
+            filler(("latent_down",), make_latent_down),
+        ],
+    )
+    grad_latent_gate, grad_latent_up = made["latent_gate"], made["latent_up"]
+    grad_latent_down = made["latent_down"]
     grad_fc2_bias = jnp.sum(encoded_grad, axis=0)
     pre_grad_blocks = [
         jax.vjp(smooth_gate, pre)[1](mat_times(block, fc2_own))[0].astype(low)
         for pre, block in zip(pre_blocks, encoded_blocks)
     ]
-    second_grad = walk.collect(lambda i: mat_times_t(pre_grad_blocks[i], fc1_own))
+
+    def make_pair(sent):
+        columns = walk.in_own_order(
+            rows_at(after(context_rows, sent), me * model_share, model_share, 1)
+        )
+        columns = columns.astype(wide) * context_scale
+        columns = columns * rows_at(context_gain, me * model_share, model_share)
+        return (outer_sum(columns.astype(low), patch_grad_rows),)
+
+    def make_fc1(sent):
+        return (outer_sum(after(joined(second_blocks), sent), joined(pre_grad_blocks)).astype(low),)
+
+    def make_fc2(sent):
+        grad = outer_sum(after(joined(encoded_blocks), sent), joined(act_blocks)).astype(low)
+        return (column_pieces(jnp.concatenate([made["fc1"], grad], axis=1)),)
+
+    second_grad = walk.collect(
+        lambda i: mat_times_t(pre_grad_blocks[i], fc1_own),
+        fill=[
+            filler(("pair",), make_pair),
+            filler(("fc1",), make_fc1),
+            filler(("unit_pieces_back",), make_fc2),
+        ],
+    )
     pre_grad = joined(pre_grad_blocks)
     grad_fc1_bias = jnp.sum(pre_grad.astype(wide), axis=0)
     hidden_norm_grad, grad_ln2_gain, grad_ln2_bias = second_norm_back(second_grad)
@@ -672,31 +871,94 @@
     grad_out_bias = jnp.sum(hidden_grad, axis=0)
     hidden_low = hidden_grad.astype(low)
 
-    attended_grad = mat_times_t(hidden_low, out_full).astype(low)
-    attended_grad = jnp.transpose(attended_grad.reshape(rows, HEADS, HEAD), (1, 0, 2))
-    attended_grad = swap_pieces(jnp.repeat(lane_pad(attended_grad), copies, axis=0))
+
+    def make_tables(sent):
+        latent_tables = after(latent_rows, sent)[:, : 3 * LANES]
+        latent_tables = latent_tables.reshape(blocks, LATENTS, 3, LANES)
+        latent_tables = latent_tables[::copies, :, :, :P_HEAD]
+        query_grad = jnp.transpose(latent_tables[:, :, 0], (1, 0, 2)).reshape(LATENTS, query_width)
+        pair_grad = jnp.sum(
+            latent_tables[:, :, 1:]
+            .astype(wide)
+            .reshape(P_KV, P_HEADS // P_KV, LATENTS, 2, P_HEAD),
+            axis=1,
+        )
+        pair_grad = jnp.transpose(pair_grad, (1, 2, 0, 3)).reshape(LATENTS, 2 * pair_width)
+        pair_grad = pair_grad.astype(low)
+        return query_grad, pair_grad
+
+    def make_latent_in(sent):
+        query_grad, pair_grad = after(made["query_grad"], sent), made["pair_grad"]
+        latent_in_grad = (
+            mat_times_t(query_grad, query_weight)
+            + mat_times_t(pair_grad[:, :pair_width], key_weight)
+            + mat_times_t(pair_grad[:, pair_width:], value_weight)
+        )
+        made["latent_in_grad"] = gather(latent_in_grad)
+        made["latents"] = scatter_sum(mat_times(after(latent_hidden, sent), latent_down))
+        return (latent_in_grad,)
+
+    def bring_units(sent):
+        made["unit_grads"] = swap_pieces(after(made["unit_pieces_back"], sent))
+        return ()
+
+    hidden_rows = walk.gather(
+        hidden_low,
+        [
+            bring_units,
+            filler(("query_grad", "pair_grad"), make_tables),
+        ],
+    )
+    out_own = rows_at(out_full, head * HEAD, HEAD) if copies > 1 else out_weight
+    attended_grad = lane_pad(mat_times_t(hidden_rows, out_own).astype(low))
+    attended_grad = after(attended_grad, made["unit_grads"])
     query_low, key_low, value_low = attend_back(heads, attended_grad, row_ids, col_ids)
     head_grad = jnp.concatenate([query_low, key_low, value_low], axis=1)
+
+    def make_heads(sent):
+        grad = outer_sum(after(first_rows, sent), head_grad).astype(low)
+        return (column_pieces(grad),)
+
+    def note_late(sent):
+        made["late"] = sent
+        return ()
+
+    bridge_units = bridge_gate.shape[1]
     first_weight = head_weight
     if copies > 1:
         first_weight = jnp.where(part == 0, head_weight, jnp.zeros((), low))
     first_grad = walk.collect_rows(
-        lambda take: mat_times_t(take(head_grad), first_weight), pack_rows
+        lambda take: mat_times_t(take(head_grad), first_weight),
+        pack_rows,
+        [
+            filler(("heads",), make_heads),
+            filler(("latent_part",), make_latent_in),
+            nothing,
+            note_late,
+        ],
     )
     input_norm_grad, grad_ln1_gain, grad_ln1_bias = first_norm_back(first_grad)
     grad_tokens = hidden_grad + input_norm_grad
 
-    hidden_rows = gather(hidden_low)
+    resid_others = [
+        other_plane(after(resid_low, first_grad), step) for step in range(1, planes)
+    ]
+    mixer_width = mixer_weight.shape[0]
+    grad_mixer = share_rows(
+        outer_sum(
+            rows_at(attended_latent_head, part * mixer_width, mixer_width, 1),
+            after(state_low, first_grad),
+        )
+    )
+    grad_pair = share_rows(after(made["pair"], first_grad))
     out_width = out_weight.shape[0]
     grad_out = outer_sum(rows_at(attended_head, part * out_width, out_width, 1), hidden_rows)
     grad_out = share_rows(after(grad_out, first_grad))
-    grad_fc1 = outer_sum(joined(second_blocks), pre_grad)
-    grad_fc2 = outer_sum(joined(encoded_blocks), joined(act_blocks))
-    units = share_columns(jnp.concatenate([grad_fc1, grad_fc2], axis=1), first_grad)
+    units = plane_share(after(made["unit_grads"], first_grad))
     units = jnp.transpose(
         units.reshape(blocks, units.shape[1], 2, unit_share), (2, 1, 0, 3)
     ).reshape(2, units.shape[1], -1)[:, :, :hidden_units]
-    grad_qkv = share_columns(outer_sum(first_rows, head_grad), first_grad)[::copies]
+    grad_qkv = plane_share(swap_pieces(made["heads"]))[::copies]
     grad_qkv = grad_qkv.reshape(HEADS, grad_qkv.shape[1], 3, LANES)[..., :HEAD]
     grad_qkv = jnp.transpose(grad_qkv, (1, 2, 0, 3)).reshape(-1, 3 * features)
     once = (part == 0).astype(wide)
@@ -734,40 +996,23 @@
         post_gain_part,
     )
     small = unpacked(sum_over_all(packed(small_terms), ("grp", "blk")), small_terms)
-    def plane_sum(mine, others):
-        others = lax.optimization_barrier((others, first_grad))[0]
-        return functools.reduce(
-            lambda total, other: total + other.astype(wide), others, mine.astype(wide)
-        )
-
     bridge_units = bridge_gate.shape[1]
-    grad_bridge_down = plane_sum(part_bridge_down, down_others)
+    grad_bridge_down = plane_sum(part_bridge_down, down_others, made["late"])
+    pair_others = [after(other, first_grad) for other in pair_others]
     grad_bridge_gate = plane_sum(
-        part_bridge_gate, [other[:, :bridge_units] for other in pair_others]
-    )
-    grad_bridge_up = plane_sum(part_bridge_up, [other[:, bridge_units:] for other in pair_others])
-    latents_out = (state_own + after(latent_down_rows, first_grad)).astype(low)
-
-    latent_tables = walk.gather(after(latent_total, encoded_grad).astype(low))
-    latent_tables = latent_tables.reshape(blocks, LATENTS, 3, LANES)[::copies, :, :, :P_HEAD]
-    query_grad = jnp.transpose(latent_tables[:, :, 0], (1, 0, 2)).reshape(LATENTS, query_width)
-    pair_grad = jnp.sum(
-        latent_tables[:, :, 1:]
-        .astype(wide)
-        .reshape(P_KV, P_HEADS // P_KV, LATENTS, 2, P_HEAD),
-        axis=1,
-    )
-    pair_grad = jnp.transpose(pair_grad, (1, 2, 0, 3)).reshape(LATENTS, 2 * pair_width)
-    pair_grad = pair_grad.astype(low)
-    latent_in_grad = (
-        mat_times_t(query_grad, query_weight)
-        + mat_times_t(pair_grad[:, :pair_width], key_weight)
-        + mat_times_t(pair_grad[:, pair_width:], value_weight)
-    )
-    latent_in_grad = walk.gather(latent_in_grad).reshape(blocks, LATENTS, model_share)
+        part_bridge_gate, [other[:, :bridge_units] for other in pair_others], first_grad
+    )
+    grad_bridge_up = plane_sum(
+        part_bridge_up, [other[:, bridge_units:] for other in pair_others], first_grad
+    )
+    latents_out = (state_own + after(made["latents"], first_grad)).astype(low)
+
+    query_grad, pair_grad = made["query_grad"], made["pair_grad"]
+    latent_in_grad = after(made["latent_in_grad"], first_grad)
+    latent_in_grad = latent_in_grad.reshape(blocks, LATENTS, model_share)
     latent_in_grad = jnp.transpose(latent_in_grad, (1, 0, 2)).reshape(LATENTS, model)
     latent_grad, grad_latent_gain = latent_norm_back(latent_in_grad)
-    grad_latents = latent_grad + plane_sum(resid_low, resid_others)
+    grad_latents = latent_grad + plane_sum(resid_low, resid_others, first_grad)
     share = model // (planes * blocks)
     latent_in_share = rows_at(latent_in, (plane * blocks + me) * share, share, 1)
     grad_query = outer_sum(latent_in_share, query_grad)

time: 1520 us -> 1510 us (level)
  waiting for transfers between devices: 537 us -> 505 us
  Pallas kernels: 47.5 us -> 78.4 us
  starting transfers between devices: 199 us -> 173 us
  other arithmetic: 143 us -> 164 us
    ppermute x72 -> x68, waiting for transfers between devices: 361 us -> 312 us  [advance(): return lax.ppermute(array, 'blk', pairs)]
    all_to_all x11 -> x8, waiting for transfers between devices: 97.5 us -> 60.6 us  [swap_pieces(): return lax.all_to_all(flat, 'blk', 0, 0, tiled=True)]
    ppermute x9 -> x10, waiting for transfers between devices: 49 us -> 81.1 us  [other_plane(): lax.ppermute(array, 'grp', [(k, (k + step) % planes) for k in range(plane...]
    pallas_call x0 -> x1, Pallas kernels: none -> 30.9 us  [context_back(): pl.pallas_call(context_back_kernel, out_shape=[jax.ShapeDtypeStruct((pack...]
    dot_general x71 -> x63, matrix products: 198 us -> 180 us  [contract(): lax.dot_general(left, right, (((left_dim,), (right_dim,)), ((), ())), pre...]
    all_to_all x11 -> x8, starting transfers between devices: 62.1 us -> 46 us  [swap_pieces(): return lax.all_to_all(flat, 'blk', 0, 0, tiled=True)]
    dynamic_update_slice x101 -> x86, local copies, waits for them, and re-layouts: 59.9 us -> 51.6 us  [in_order(): whole = lax.dynamic_update_slice_in_dim(whole, piece, first, 0)]
    ppermute x72 -> x68, starting transfers between devices: 82 us -> 87.6 us  [advance(): return lax.ppermute(array, 'blk', pairs)]
  transfers between devices with their start and end apart: 198 -> 190, of which waited for: 82 -> 85; matrix products, arithmetic and copies ran while one was open for 43% -> 43% of each run, Pallas kernels for 3% -> 5%
where the time goes in v3:
time: 1510 us; the launch traced here: 1500 us
  waiting for transfers between devices  505 us (33%)
  matrix products  288 us (19%)
  local copies, waits for them, and re-layouts  268 us (18%)
  starting transfers between devices  173 us (11%)
  other arithmetic  164 us (11%)
  Pallas kernels  78.4 us (5%)
  between operations  24.1 us (2%)
    ppermute x68, waiting for transfers between devices, advance(): return lax.ppermute(array, 'blk', pairs)  312 us
    dot_general x63, matrix products, contract(): lax.dot_general(left, right, (((left_dim,), (right_dim,)), ((), ())), pre...  180 us
    dot_general x50, matrix products, mat_times(): return jnp.dot(left, right, preferred_element_type=wide)  108 us
    ppermute x68, starting transfers between devices, advance(): return lax.ppermute(array, 'blk', pairs)  87.6 us
    unnamed x467, local copies, waits for them, and re-layouts  85.7 us
    ppermute x10, waiting for transfers between devices, other_plane(): lax.ppermute(array, 'grp', [(k, (k + step) % planes) for k in range(plane...  81.1 us
    all_to_all x8, waiting for transfers between devices, swap_pieces(): return lax.all_to_all(flat, 'blk', 0, 0, tiled=True)  60.6 us
    dynamic_update_slice x86, local copies, waits for them, and re-layouts, in_order(): whole = lax.dynamic_update_slice_in_dim(whole, piece, first, 0)  51.6 us
  transfers between devices with their start and end apart: 190, of which 85 were waited for; matrix products, arithmetic and copies ran while one was open for 43% of the time, Pallas kernels for 5%

profile of v3, /device:TPU:10, one launch (start us, length us, event | category | flops | bytes accessed | tf_op | source)
XLA Modules:
  0.0 1499.6 jit_solution(8025269949640496768)
XLA Ops:
  62.3 12.4 all-to-all-done
  80.7 5.1 collective-permute-done.5
  96.4 6.1 all-to-all-start.1
  106.7 6.5 add_convert_fusion.query_ref.key_ref.value_ref
  113.2 12.7 vision_attend.1
  125.9 18.8 %all-to-all-done.1 = bf16[16,72,538]{2,1,0:T(8,128)(2,1)S(1)} async-done(((bf16[16,72,538]{2,1,0:T(8,128)(2,1)}), bf16[16,72,538]{2,1,0:T(8,128)(2,1)S(1)}, u32[]{:S(2)}, u32[]{:S(2)}) %all-to-all-start.1) | async-done | bytes 1239584 | tf_op jit(solution)/shard_map/all_to_all | solution.py:81
  147.0 6.7 all-to-all-start.2
  156.8 5.9 all-to-all-done.2
  167.7 13.9 collective-permute-done.16
  198.2 5.3 collective-permute-done.12
  245.6 9.1 collective-permute-done.24
  262.8 10.1 collective-permute-done.26
  323.0 5.9 collective-permute-done.31
  385.8 8.0 collective-permute-done.41
  396.1 7.2 all-to-all-done.3
  406.3 7.5 all-to-all-start.4
  413.9 7.5 fusion.337
  421.4 5.5 fusion.338
  426.9 10.3 collective-permute-done.45
  449.4 6.0 broadcast_select_fusion.1
  455.4 6.3 fusion.305
  461.7 11.0 collective-permute-done.54
  478.8 5.5 fusion.336
  484.3 7.6 collective-permute-done.51
  492.1 11.0 collective-permute-done.55
  515.7 6.3 collective-permute-done.58
  523.4 6.4 collective-permute-done.60
  599.3 5.0 collective-permute-done.78
  634.7 5.9 fusion.341
  640.7 7.0 multiply_convert_fusion.8
  652.2 7.0 fusion.1
  677.7 9.2 collective-permute-done.90
  687.0 5.5 collective-permute-start.91
  694.4 15.6 %collective-permute-done.91 = bf16[32,4096]{1,0:T(8,128)(2,1)S(1)} collective-permute-done((bf16[32,4096]{1,0:T(8,128)(2,1)S(1)}, bf16[32,4096]{1,0:T(8,128)(2,1)S(1)}, u32[]{:S(2)}, u32[]{:S(2)}) %collective-permute-start.91) | collective-permute-done | bytes 262176 | tf_op jit(solution)/shard_map/ppermute | solution.py:114
  717.0 14.9 collective-permute-done.94
  735.2 14.7 collective-permute-done.96
  767.3 6.2 resampler_attend_back.1
  777.6 5.7 all-to-all-start.5
  790.8 11.4 all-to-all-done.5
  829.1 10.8 collective-permute-done.124
  849.5 30.9 %context_back.1 = (bf16[2048,4096]{1,0:T(8,128)(2,1)}, f32[2048,1]{1,0:T(8,128)}, f32[1,4096]{1,0:T(1,128)}) custom-call(s32[16]{0:T(128)} %stack.67.order_ref, bf16[2048,4096]{1,0:T(8,128)(2,1)} %all-gather.10.cloned.1.call-done.context_ref, bf16[2048,768]{1,0:T(8,128)(2,1)} %copy-done.50, bf16[768,4096]{1,0:T(8,128)(2,1)} %fusion.305, f32[1,4096]{1,0:T(1,128)} %bitcast.389), custom_call_target="tpu_custom_call" | custom-call | tf_op jit(solution)/shard_map/context_back/pallas_call | solution.py:451
  880.4 27.9 %multiply_convert_fusion = (bf16[2048,896]{1,0:T(8,128)(2,1)}, bf16[2048,896]{1,0:T(8,128)(2,1)}) fusion(f32[2048,896]{1,0:T(8,128)} %copy-done.141, f32[2048,896]{1,0:T(8,128)} %constant_dynamic-update-slice_fusion.12, bf16[2048,4096]{1,0:T(8,128)(2,1)} %get-tuple-element.168, bf16[896,4096]{1,0:T(8,128)(2,1)} %param.49), kind=kOutput, calls=%fused_computation.2 | convolution fusion | flops 15054405632 | bytes 46137344 | tf_op jit(solution)/shard_map/dot_general | solution.py:48
  924.4 22.1 %convolution_convert_fusion = bf16[896,4096]{1,0:T(8,128)(2,1)} fusion(bf16[2048,896]{1,0:T(8,128)(2,1)} %copy-done.186, bf16[2048,4096]{1,0:T(8,128)(2,1)} %get-tuple-element.168), kind=kOutput, calls=%fused_computation.5 | convolution fusion | flops 15036055552 | bytes 27787264 | tf_op jit(solution)/shard_map/dot_general | solution.py:48
  950.7 7.5 convolution_convert_fusion.6
  961.4 5.1 convolution_convert_fusion.5
  973.8 6.7 collective-permute-done.118
  990.8 8.6 fusion.10
  1002.4 8.5 fusion.9
  1020.3 8.6 fusion.5
  1063.6 6.8 collective-permute-done.137
  1085.2 8.4 collective-permute-done.140
  1116.1 5.3 all-to-all-start.6
  1122.6 14.8 all-gather.12.cloned.1.call-done
  1151.9 14.6 collective-permute-done.145
  1193.5 25.3 %vision_attend_back.1 = (bf16[2048,128]{1,0:T(8,128)(2,1)}, bf16[2048,128]{1,0:T(8,128)(2,1)}, bf16[2048,128]{1,0:T(8,128)(2,1)}) custom-call(bf16[2048,384]{1,0:T(8,128)(2,1)} %add_convert_fusion.query_ref.key_ref.value_ref, bf16[2048,384]{1,0:T(8,128)(2,1)} %add_convert_fusion.query_ref.key_ref.value_ref, ...), custom_call_target="tpu_custom_call" | custom-call | tf_op jit(solution)/shard_map/vision_attend_back/pallas_call | solution.py:309
  1246.2 5.3 all-to-all-start.7
  1264.2 21.5 %collective-permute-done.155 = bf16[256,1152]{1,0:T(8,128)(2,1)S(1)} collective-permute-done((bf16[256,1152]{1,0:T(8,128)(2,1)}, bf16[256,1152]{1,0:T(8,128)(2,1)S(1)}, u32[]{:S(2)}, u32[]{:S(2)}) %collective-permute-start.155) | collective-permute-done | bytes 589856 | tf_op jit(solution)/shard_map/ppermute | solution.py:114
  1289.5 7.0 convolution_convert_fusion.1
  1304.3 14.2 convert_add_fusion
  1320.4 47.4 %collective-permute-done.165 = bf16[16,36,384]{2,0,1:T(8,128)(2,1)} collective-permute-done((bf16[16,36,384]{2,0,1:T(8,128)(2,1)}, bf16[16,36,384]{2,0,1:T(8,128)(2,1)}, u32[]{:S(2)}, u32[]{:S(2)}) %collective-permute-start.165) | collective-permute-done | bytes 442400 | tf_op jit(solution)/shard_map/ppermute | solution.py:504
  1401.5 5.6 copy.355
  1411.8 5.6 copy.354
  1466.3 9.0 collective-permute-done.168
  1478.1 8.0 slice_reduce_fusion
  (1304 shorter events, 806.9 us)
Async XLA Ops:
  44.3 13.1 collective-permute-start.3
  45.9 28.8 %all-to-all-start = ((bf16[16,80,384]{2,1,0:T(8,128)(2,1)}), bf16[16,80,384]{2,1,0:T(8,128)(2,1)S(1)}, u32[]{:S(2)}, u32[]{:S(2)}) async-start(bf16[16,80,384]{2,1,0:T(8,128)(2,1)} %pad_maximum_fusion.14), calls=%async_computation | async-start | bytes 1966080 | tf_op jit(solution)/shard_map/all_to_all | solution.py:81
  50.4 112.2 %all-gather.6.cloned.1.call-start = ((), (), s32[]{:S(2)}) async-start(), calls=%async_computation.9 | async-start | bytes 2820096 | tf_op jit(solution)/shard_map/all_gather | solution.py:66
  57.4 19.9 %collective-permute-start.4 = (bf16[256,1152]{1,0:T(8,128)(2,1)}, bf16[256,1152]{1,0:T(8,128)(2,1)}, u32[]{:S(2)}, u32[]{:S(2)}) collective-permute-start(bf16[256,1152]{1,0:T(8,128)(2,1)} %collective-permute-done.3), channel_id=1, source_target_pairs={{0,1},{1,0},{2,3},{3,2},{4,5},{5,4},{6,7},{7,6},{8,9},{9,8},{10,11... | collective-permute-start | bytes 1769480 | tf_op jit(solution)/shard_map/ppermute | solution.py:117
  96.4 48.3 %all-to-all-start.1 = ((bf16[16,72,538]{2,1,0:T(8,128)(2,1)}), bf16[16,72,538]{2,1,0:T(8,128)(2,1)S(1)}, u32[]{:S(2)}, u32[]{:S(2)}) async-start(bf16[16,72,538]{2,1,0:T(8,128)(2,1)} %pad_maximum_fusion.10), calls=%async_computation.1 | async-start | bytes 2949120 | tf_op jit(solution)/shard_map/all_to_all | solution.py:81
  147.0 15.6 %all-to-all-start.2 = ((bf16[16,128,72]{1,2,0:T(8,128)(2,1)}), bf16[16,128,72]{1,2,0:T(8,128)(2,1)}, u32[]{:S(2)}, u32[]{:S(2)}) async-start(bf16[16,128,72]{1,2,0:T(8,128)(2,1)} %copy.310), calls=%async_computation.2 | async-start | bytes 589824 | tf_op jit(solution)/shard_map/all_to_all | solution.py:81
  153.7 141.0 %all-gather.8.cloned.1.call-start = ((), (), s32[]{:S(2)}) async-start(), calls=%async_computation.10 | async-start | bytes 3342336 | tf_op jit(solution)/shard_map/all_gather | solution.py:66
  156.1 25.5 %collective-permute-start.16 = (bf16[128,4096]{1,0:T(8,128)(2,1)}, bf16[128,4096]{1,0:T(8,128)(2,1)}, u32[]{:S(2)}, u32[]{:S(2)}) collective-permute-start(bf16[128,4096]{1,0:T(8,128)(2,1)} %constant_dynamic-slice_fusion.35), channel_id=1, source_target_pairs={{0,16},{16,0},{1,17},{17,1},{2,18},{18,2},{3,19},{19,3},{4,20},{20... | collective-permute-start | bytes 3145736 | tf_op jit(solution)/shard_map/ppermute | solution.py:504
  167.0 14.6 collective-permute-start.9
  181.6 13.3 collective-permute-start.17
  241.7 13.1 collective-permute-start.24
  255.8 17.1 %collective-permute-start.26 = (bf16[256,1152]{1,0:T(8,128)(2,1)}, bf16[256,1152]{1,0:T(8,128)(2,1)}, u32[]{:S(2)}, u32[]{:S(2)}) collective-permute-start(bf16[256,1152]{1,0:T(8,128)(2,1)} %add_convert_fusion.8), channel_id=1, source_target_pairs={{0,4},{1,3},{4,8},{5,1},{8,12},{9,5},{12,14},{13,9},{14,10},{15,13... | collective-permute-start | bytes 1769480 | tf_op jit(solution)/shard_map/ppermute | solution.py:114
  300.2 146.3 %collective-permute-start.50 = (bf16[4096,384]{0,1:T(8,128)(2,1)}, bf16[4096,384]{0,1:T(8,128)(2,1)}, u32[]{:S(2)}, u32[]{:S(2)}) collective-permute-start(bf16[4096,384]{0,1:T(8,128)(2,1)} %all-gather.8.cloned.1.call-done), channel_id=1, source_target_pairs={{0,16},{16,0},{1,17},{17,1},{2,18},{18,2},{3,19},{19,3},{4,20},{20... | collective-permute-start | bytes 9437192 | tf_op jit(solution)/shard_map/ppermute | solution.py:504
  372.5 21.4 %collective-permute-start.41 = (bf16[128,2048]{1,0:T(8,128)(2,1)}, bf16[128,2048]{1,0:T(8,128)(2,1)}, u32[]{:S(2)}, u32[]{:S(2)}) collective-permute-start(bf16[128,2048]{1,0:T(8,128)(2,1)} %get-tuple-element.498), channel_id=1, source_target_pairs={{0,4},{1,3},{4,8},{5,1},{8,12},{9,5},{12,14},{13,9},{14,10},{15,13... | collective-permute-start | bytes 1572872 | tf_op jit(solution)/shard_map/ppermute | solution.py:114
  373.8 29.5 %all-to-all-start.3 = ((bf16[16,64,384]{2,1,0:T(8,128)(2,1)}), bf16[16,64,384]{2,1,0:T(8,128)(2,1)}, u32[]{:S(2)}, u32[]{:S(2)}) async-start(bf16[16,64,384]{2,1,0:T(8,128)(2,1)} %pad_maximum_fusion.15), calls=%async_computation.3 | async-start | bytes 1572864 | tf_op jit(solution)/shard_map/all_to_all | solution.py:81
  404.5 22.5 %collective-permute-start.47 = (bf16[256,2048]{1,0:T(8,128)(2,1)}, bf16[256,2048]{1,0:T(8,128)(2,1)}, u32[]{:S(2)}, u32[]{:S(2)}) collective-permute-start(bf16[256,2048]{1,0:T(8,128)(2,1)} %pad_maximum_fusion.13), channel_id=1, source_target_pairs={{0,4},{1,3},{4,8},{5,1},{8,12},{9,5},{12,14},{13,9},{14,10},{15,13... | collective-permute-start | bytes 3145736 | tf_op jit(solution)/shard_map/ppermute | solution.py:114
  404.5 32.7 %collective-permute-start.45 = (bf16[256,2048]{1,0:T(8,128)(2,1)}, bf16[256,2048]{1,0:T(8,128)(2,1)}, u32[]{:S(2)}, u32[]{:S(2)}) collective-permute-start(bf16[256,2048]{1,0:T(8,128)(2,1)} %pad_maximum_fusion.12), channel_id=1, source_target_pairs={{0,4},{1,3},{4,8},{5,1},{8,12},{9,5},{12,14},{13,9},{14,10},{15,13... | collective-permute-start | bytes 3145736 | tf_op jit(solution)/shard_map/ppermute | solution.py:114
  404.6 22.3 %collective-permute-start.46 = (bf16[256,2048]{1,0:T(8,128)(2,1)}, bf16[256,2048]{1,0:T(8,128)(2,1)}, u32[]{:S(2)}, u32[]{:S(2)}) collective-permute-start(bf16[256,2048]{1,0:T(8,128)(2,1)} %get-tuple-element.151), channel_id=1, source_target_pairs={{0,1},{1,0},{2,3},{3,2},{4,5},{5,4},{6,7},{7,6},{8,9},{9,8},{10,11... | collective-permute-start | bytes 3145736 | tf_op jit(solution)/shard_map/ppermute | solution.py:117
  404.7 22.2 %collective-permute-start.44 = (bf16[256,2048]{1,0:T(8,128)(2,1)}, bf16[256,2048]{1,0:T(8,128)(2,1)}, u32[]{:S(2)}, u32[]{:S(2)}) collective-permute-start(bf16[256,2048]{1,0:T(8,128)(2,1)} %get-tuple-element.148), channel_id=1, source_target_pairs={{0,1},{1,0},{2,3},{3,2},{4,5},{5,4},{6,7},{7,6},{8,9},{9,8},{10,11... | collective-permute-start | bytes 3145736 | tf_op jit(solution)/shard_map/ppermute | solution.py:117
  406.3 40.2 %all-to-all-start.4 = ((bf16[16,96,256]{2,1,0:T(8,128)(2,1)}), bf16[16,96,256]{2,1,0:T(8,128)(2,1)}, u32[]{:S(2)}, u32[]{:S(2)}) async-start(bf16[16,96,256]{2,1,0:T(8,128)(2,1)} %copy.313), calls=%async_computation.4 | async-start | bytes 1572864 | tf_op jit(solution)/shard_map/all_to_all | solution.py:81
  413.8 389.4 %all-gather.10.cloned.1.call-start = ((), (), s32[]{:S(2)}) async-start(), calls=%async_computation.11 | async-start | bytes 17825792 | tf_op jit(solution)/shard_map/all_gather | solution.py:66
  446.5 26.1 %collective-permute-start.49 = (bf16[256,2048]{1,0:T(8,128)(2,1)S(1)}, bf16[256,2048]{1,0:T(8,128)(2,1)}, u32[]{:S(2)}, u32[]{:S(2)}) collective-permute-start(bf16[256,2048]{1,0:T(8,128)(2,1)S(1)} %get-tuple-element.150), channel_id=1, source_target_pairs={{0,4},{1,3},{4,8},{5,1},{8,12},{9,5},{12,14},{13,9},{14,10},{15,13... | collective-permute-start | bytes 3145736 | tf_op jit(solution)/shard_map/ppermute | solution.py:114
  446.5 26.1 %collective-permute-start.54 = (bf16[256,2048]{1,0:T(8,128)(2,1)}, bf16[256,2048]{1,0:T(8,128)(2,1)}, u32[]{:S(2)}, u32[]{:S(2)}) collective-permute-start(bf16[256,2048]{1,0:T(8,128)(2,1)} %get-tuple-element.152), channel_id=1, source_target_pairs={{0,4},{1,3},{4,8},{5,1},{8,12},{9,5},{12,14},{13,9},{14,10},{15,13... | collective-permute-start | bytes 3145736 | tf_op jit(solution)/shard_map/ppermute | solution.py:114
  448.0 13.7 collective-permute-start.53
  477.1 14.9 collective-permute-start.51
  477.1 26.0 %collective-permute-start.55 = (bf16[256,2048]{1,0:T(8,128)(2,1)S(1)}, bf16[256,2048]{1,0:T(8,128)(2,1)S(1)}, u32[]{:S(2)}, u32[]{:S(2)}) collective-permute-start(bf16[256,2048]{1,0:T(8,128)(2,1)S(1)} %get-tuple-element.158), channel_id=1, source_target_pairs={{0,4},{1,3},{4,8},{5,1},{8,12},{9,5},{12,14},{13,9},{14,10},{15,13... | collective-permute-start | bytes 3145736 | tf_op jit(solution)/shard_map/ppermute | solution.py:114
  673.0 13.9 collective-permute-start.90
  687.0 23.0 %collective-permute-start.91 = (bf16[32,4096]{1,0:T(8,128)(2,1)S(1)}, bf16[32,4096]{1,0:T(8,128)(2,1)S(1)}, u32[]{:S(2)}, u32[]{:S(2)}) collective-permute-start(bf16[32,4096]{1,0:T(8,128)(2,1)S(1)} %add_convert_fusion.10), channel_id=1, source_target_pairs={{0,4},{1,3},{4,8},{5,1},{8,12},{9,5},{12,14},{13,9},{14,10},{15,13... | collective-permute-start | bytes 786440 | tf_op jit(solution)/shard_map/ppermute | solution.py:114
  714.1 17.8 %collective-permute-start.94 = (bf16[32,4096]{1,0:T(8,128)(2,1)S(1)}, bf16[32,4096]{1,0:T(8,128)(2,1)S(1)}, u32[]{:S(2)}, u32[]{:S(2)}) collective-permute-start(bf16[32,4096]{1,0:T(8,128)(2,1)S(1)} %pad_maximum_fusion.33), channel_id=1, source_target_pairs={{0,4},{1,3},{4,8},{5,1},{8,12},{9,5},{12,14},{13,9},{14,10},{15,13... | collective-permute-start | bytes 786440 | tf_op jit(solution)/shard_map/ppermute | solution.py:114
  731.9 21.0 %collective-permute-start.95 = (bf16[32,4096]{1,0:T(8,128)(2,1)S(1)}, bf16[32,4096]{1,0:T(8,128)(2,1)S(1)}, u32[]{:S(2)}, u32[]{:S(2)}) collective-permute-start(bf16[32,4096]{1,0:T(8,128)(2,1)S(1)} %collective-permute-done.94), channel_id=1, source_target_pairs={{0,1},{1,0},{2,3},{3,2},{4,5},{5,4},{6,7},{7,6},{8,9},{9,8},{10,11... | collective-permute-start | bytes 786440 | tf_op jit(solution)/shard_map/ppermute | solution.py:117
  731.9 18.1 %collective-permute-start.96 = (bf16[32,4096]{1,0:T(8,128)(2,1)S(1)}, bf16[32,4096]{1,0:T(8,128)(2,1)S(1)}, u32[]{:S(2)}, u32[]{:S(2)}) collective-permute-start(bf16[32,4096]{1,0:T(8,128)(2,1)S(1)} %collective-permute-done.94), channel_id=1, source_target_pairs={{0,4},{1,3},{4,8},{5,1},{8,12},{9,5},{12,14},{13,9},{14,10},{15,13... | collective-permute-start | bytes 786440 | tf_op jit(solution)/shard_map/ppermute | solution.py:114
  777.6 24.7 %all-to-all-start.5 = ((bf16[16,128,192]{1,2,0:T(8,128)(2,1)}), bf16[16,128,192]{1,2,0:T(8,128)(2,1)S(1)}, u32[]{:S(2)}, u32[]{:S(2)}) async-start(bf16[16,128,192]{1,2,0:T(8,128)(2,1)} %pad_maximum_fusion.16), calls=%async_computation.5 | async-start | bytes 1572864 | tf_op jit(solution)/shard_map/all_to_all | solution.py:81
  783.3 354.1 %all-gather.12.cloned.1.call-start = ((), (), s32[]{:S(2)}) async-start(), calls=%async_computation.12 | async-start | bytes 1114112 | tf_op jit(solution)/shard_map/all_gather | solution.py:66
  790.8 18.4 %collective-permute-start.123 = (f32[64,384]{1,0:T(8,128)}, f32[64,384]{1,0:T(8,128)}, u32[]{:S(2)}, u32[]{:S(2)}) collective-permute-start(f32[64,384]{1,0:T(8,128)} %pad_maximum_fusion.35), channel_id=1, source_target_pairs={{0,16},{16,0},{1,17},{17,1},{2,18},{18,2},{3,19},{19,3},{4,20},{20... | collective-permute-start | bytes 294920 | tf_op jit(solution)/shard_map/ppermute | solution.py:504
  813.6 26.3 %collective-permute-start.124 = (bf16[128,4096]{1,0:T(8,128)(2,1)S(1)}, bf16[128,4096]{1,0:T(8,128)(2,1)}, u32[]{:S(2)}, u32[]{:S(2)}) collective-permute-start(bf16[128,4096]{1,0:T(8,128)(2,1)S(1)} %constant_dynamic-slice_fusion.19), channel_id=1, source_target_pairs={{0,16},{16,0},{1,17},{17,1},{2,18},{18,2},{3,19},{19,3},{4,20},{20... | collective-permute-start | bytes 3145736 | tf_op jit(solution)/shard_map/ppermute | solution.py:504
  823.0 17.6 %collective-permute-start.104 = (bf16[256,768]{1,0:T(8,128)(2,1)S(1)}, bf16[256,768]{1,0:T(8,128)(2,1)S(1)}, u32[]{:S(2)}, u32[]{:S(2)}) collective-permute-start(bf16[256,768]{1,0:T(8,128)(2,1)S(1)} %collective-permute-done.103), channel_id=1, source_target_pairs={{0,1},{1,0},{2,3},{3,2},{4,5},{5,4},{6,7},{7,6},{8,9},{9,8},{10,11... | collective-permute-start | bytes 1179656 | tf_op jit(solution)/shard_map/ppermute | solution.py:117
  826.5 14.0 collective-permute-start.107
  829.1 159.3 %collective-permute-start.126 = (bf16[256,3072]{1,0:T(8,128)(2,1)}, bf16[256,3072]{1,0:T(8,128)(2,1)}, u32[]{:S(2)}, u32[]{:S(2)}) collective-permute-start(bf16[256,3072]{1,0:T(8,128)(2,1)} %pad_maximum_fusion.9), channel_id=1, source_target_pairs={{0,16},{16,0},{1,17},{17,1},{2,18},{18,2},{3,19},{19,3},{4,20},{20... | collective-permute-start | bytes 4718600 | tf_op jit(solution)/shard_map/ppermute | solution.py:504
  839.8 140.8 %collective-permute-start.125 = (bf16[128,4096]{1,0:T(8,128)(2,1)}, bf16[128,4096]{1,0:T(8,128)(2,1)}, u32[]{:S(2)}, u32[]{:S(2)}) collective-permute-start(bf16[128,4096]{1,0:T(8,128)(2,1)} %collective-permute-done.124), channel_id=1, source_target_pairs={{0,1},{1,0},{2,3},{3,2},{4,5},{5,4},{6,7},{7,6},{8,9},{9,8},{10,11... | collective-permute-start | bytes 3145736 | tf_op jit(solution)/shard_map/ppermute | solution.py:117
  923.6 24.2 %collective-permute-start.113 = (bf16[128,1152]{1,0:T(8,128)(2,1)S(1)}, bf16[128,1152]{1,0:T(8,128)(2,1)}, u32[]{:S(2)}, u32[]{:S(2)}) collective-permute-start(bf16[128,1152]{1,0:T(8,128)(2,1)S(1)} %fusion.68), channel_id=1, source_target_pairs={{0,4},{1,3},{4,8},{5,1},{8,12},{9,5},{12,14},{13,9},{14,10},{15,13... | collective-permute-start | bytes 884744 | tf_op jit(solution)/shard_map/ppermute | solution.py:114
  923.7 22.9 %collective-permute-start.112 = (bf16[256,1152]{1,0:T(8,128)(2,1)S(1)}, bf16[256,1152]{1,0:T(8,128)(2,1)}, u32[]{:S(2)}, u32[]{:S(2)}) collective-permute-start(bf16[256,1152]{1,0:T(8,128)(2,1)S(1)} %fusion.13), channel_id=1, source_target_pairs={{0,1},{1,0},{2,3},{3,2},{4,5},{5,4},{6,7},{7,6},{8,9},{9,8},{10,11... | collective-permute-start | bytes 1769480 | tf_op jit(solution)/shard_map/ppermute | solution.py:117
  986.9 14.4 collective-permute-start.121
  1013.4 15.4 %collective-permute-start.129 = (bf16[256,1152]{1,0:T(8,128)(2,1)S(1)}, bf16[256,1152]{1,0:T(8,128)(2,1)S(1)}, u32[]{:S(2)}, u32[]{:S(2)}) collective-permute-start(bf16[256,1152]{1,0:T(8,128)(2,1)S(1)} %collective-permute-done.127), channel_id=1, source_target_pairs={{0,4},{1,3},{4,8},{5,1},{8,12},{9,5},{12,14},{13,9},{14,10},{15,13... | collective-permute-start | bytes 1769480 | tf_op jit(solution)/shard_map/ppermute | solution.py:114
  1040.5 19.8 %collective-permute-start.135 = (bf16[128,1152]{1,0:T(8,128)(2,1)S(1)}, bf16[128,1152]{1,0:T(8,128)(2,1)S(1)}, u32[]{:S(2)}, u32[]{:S(2)}) collective-permute-start(bf16[128,1152]{1,0:T(8,128)(2,1)S(1)} %fusion.64), channel_id=1, source_target_pairs={{0,4},{1,3},{4,8},{5,1},{8,12},{9,5},{12,14},{13,9},{14,10},{15,13... | collective-permute-start | bytes 884744 | tf_op jit(solution)/shard_map/ppermute | solution.py:114
  1041.8 18.3 %collective-permute-start.134 = (bf16[256,1152]{1,0:T(8,128)(2,1)S(1)}, bf16[256,1152]{1,0:T(8,128)(2,1)S(1)}, u32[]{:S(2)}, u32[]{:S(2)}) collective-permute-start(bf16[256,1152]{1,0:T(8,128)(2,1)S(1)} %convolution_convert_fusion.13), channel_id=1, source_target_pairs={{0,1},{1,0},{2,3},{3,2},{4,5},{5,4},{6,7},{7,6},{8,9},{9,8},{10,11... | collective-permute-start | bytes 1769480 | tf_op jit(solution)/shard_map/ppermute | solution.py:117
  1108.0 29.4 %collective-permute-start.143 = (bf16[256,1152]{1,0:T(8,128)(2,1)}, bf16[256,1152]{1,0:T(8,128)(2,1)}, u32[]{:S(2)}, u32[]{:S(2)}) collective-permute-start(bf16[256,1152]{1,0:T(8,128)(2,1)} %pad_maximum_fusion.24), channel_id=1, source_target_pairs={{0,4},{1,3},{4,8},{5,1},{8,12},{9,5},{12,14},{13,9},{14,10},{15,13... | collective-permute-start | bytes 1769480 | tf_op jit(solution)/shard_map/ppermute | solution.py:114
  1109.5 194.8 %collective-permute-start.170 = (bf16[896,4096]{1,0:T(8,128)(2,1)}, bf16[896,4096]{1,0:T(8,128)(2,1)}, u32[]{:S(2)}, u32[]{:S(2)}) collective-permute-start(bf16[896,4096]{1,0:T(8,128)(2,1)} %convolution_convert_fusion), channel_id=1, source_target_pairs={{0,16},{16,0},{1,17},{17,1},{2,18},{18,2},{3,19},{19,3},{4,20},{20... | collective-permute-start | bytes 22020104 | tf_op jit(solution)/shard_map/ppermute | solution.py:504
  1109.5 285.6 %collective-permute-start.169 = (bf16[1152,1792]{0,1:T(8,128)(2,1)}, bf16[1152,1792]{0,1:T(8,128)(2,1)}, u32[]{:S(2)}, u32[]{:S(2)}) collective-permute-start(bf16[1152,1792]{0,1:T(8,128)(2,1)} %pad_maximum_fusion.2), channel_id=1, source_target_pairs={{0,16},{16,0},{1,17},{17,1},{2,18},{18,2},{3,19},{19,3},{4,20},{20... | collective-permute-start | bytes 12386312 | tf_op jit(solution)/shard_map/ppermute | solution.py:504
  1116.1 77.4 %all-to-all-start.6 = ((bf16[32,36,538]{2,1,0:T(8,128)(2,1)}), bf16[32,36,538]{2,1,0:T(8,128)(2,1)}, u32[]{:S(2)}, u32[]{:S(2)}) async-start(bf16[32,36,538]{2,1,0:T(8,128)(2,1)} %bitcast.362), calls=%async_computation.6 | async-start | bytes 3276800 | tf_op jit(solution)/shard_map/all_to_all | solution.py:81
  1121.4 269.9 %all-gather.14.cloned.1.call-start = ((), (), s32[]{:S(2)}) async-start(), calls=%async_computation.14 | async-start | bytes 1114112 | tf_op jit(solution)/shard_map/all_gather | solution.py:66
  1143.7 25.2 %collective-permute-start.144 = (bf16[256,1152]{1,0:T(8,128)(2,1)}, bf16[256,1152]{1,0:T(8,128)(2,1)}, u32[]{:S(2)}, u32[]{:S(2)}) collective-permute-start(bf16[256,1152]{1,0:T(8,128)(2,1)} %collective-permute-done.143), channel_id=1, source_target_pairs={{0,1},{1,0},{2,3},{3,2},{4,5},{5,4},{6,7},{7,6},{8,9},{9,8},{10,11... | collective-permute-start | bytes 1769480 | tf_op jit(solution)/shard_map/ppermute | solution.py:117
  1144.0 22.5 %collective-permute-start.145 = (bf16[256,1152]{1,0:T(8,128)(2,1)}, bf16[256,1152]{1,0:T(8,128)(2,1)}, u32[]{:S(2)}, u32[]{:S(2)}) collective-permute-start(bf16[256,1152]{1,0:T(8,128)(2,1)} %collective-permute-done.143), channel_id=1, source_target_pairs={{0,4},{1,3},{4,8},{5,1},{8,12},{9,5},{12,14},{13,9},{14,10},{15,13... | collective-permute-start | bytes 1769480 | tf_op jit(solution)/shard_map/ppermute | solution.py:114
  1246.2 50.4 %all-to-all-start.7 = ((bf16[32,36,384]{2,1,0:T(8,128)(2,1)}), bf16[32,36,384]{2,1,0:T(8,128)(2,1)}, u32[]{:S(2)}, u32[]{:S(2)}) async-start(bf16[32,36,384]{2,1,0:T(8,128)(2,1)} %bitcast.367), calls=%async_computation.8 | async-start | bytes 1966080 | tf_op jit(solution)/shard_map/all_to_all | solution.py:81
  1251.6 238.1 %reduce-scatter.2.cloned.1.call-start = ((), (), s32[]{:S(2)}) async-start(), calls=%async_computation.13 | async-start | bytes 2228224 | tf_op jit(solution)/shard_map/reduce_scatter | solution.py:76
  1256.3 29.4 %collective-permute-start.155 = (bf16[256,1152]{1,0:T(8,128)(2,1)}, bf16[256,1152]{1,0:T(8,128)(2,1)S(1)}, u32[]{:S(2)}, u32[]{:S(2)}) collective-permute-start(bf16[256,1152]{1,0:T(8,128)(2,1)} %pad_maximum_fusion.25), channel_id=1, source_target_pairs={{0,4},{1,3},{4,8},{5,1},{8,12},{9,5},{12,14},{13,9},{14,10},{15,13... | collective-permute-start | bytes 1769480 | tf_op jit(solution)/shard_map/ppermute | solution.py:114
  1287.1 13.0 collective-permute-start.157
  1298.8 69.0 %collective-permute-start.165 = (bf16[16,36,384]{2,0,1:T(8,128)(2,1)}, bf16[16,36,384]{2,0,1:T(8,128)(2,1)}, u32[]{:S(2)}, u32[]{:S(2)}) collective-permute-start(bf16[16,36,384]{2,0,1:T(8,128)(2,1)} %bitcast.307), channel_id=1, source_target_pairs={{0,16},{16,0},{1,17},{17,1},{2,18},{18,2},{3,19},{19,3},{4,20},{20... | collective-permute-start | bytes 1327112 | tf_op jit(solution)/shard_map/ppermute | solution.py:504
  1302.5 16.1 %collective-permute-start.158 = (bf16[256,1152]{1,0:T(8,128)(2,1)}, bf16[256,1152]{1,0:T(8,128)(2,1)}, u32[]{:S(2)}, u32[]{:S(2)}) collective-permute-start(bf16[256,1152]{1,0:T(8,128)(2,1)} %add_convert_fusion.1), channel_id=1, source_target_pairs={{0,4},{1,3},{4,8},{5,1},{8,12},{9,5},{12,14},{13,9},{14,10},{15,13... | collective-permute-start | bytes 1769480 | tf_op jit(solution)/shard_map/ppermute | solution.py:114
  1320.4 56.7 %collective-permute-start.159 = (bf16[128,1152]{1,0:T(8,128)(2,1)}, bf16[128,1152]{1,0:T(8,128)(2,1)}, u32[]{:S(2)}, u32[]{:S(2)}) collective-permute-start(bf16[128,1152]{1,0:T(8,128)(2,1)} %fusion.58), channel_id=1, source_target_pairs={{0,1},{1,0},{2,3},{3,2},{4,5},{5,4},{6,7},{7,6},{8,9},{9,8},{10,11... | collective-permute-start | bytes 884744 | tf_op jit(solution)/shard_map/ppermute | solution.py:117
  1383.1 73.8 %collective-permute-start.174 = (bf16[48,4096]{1,0:T(8,128)(2,1)}, bf16[48,4096]{1,0:T(8,128)(2,1)}, u32[]{:S(2)}, u32[]{:S(2)}) collective-permute-start(bf16[48,4096]{1,0:T(8,128)(2,1)} %get-tuple-element.556), channel_id=1, source_target_pairs={{0,0},{1,2},{2,4},{3,6},{4,8},{5,10},{6,12},{7,14},{8,16},{9,18},{... | collective-permute-start | bytes 1179656 | tf_op jit(solution)/shard_map/ppermute | solution.py:543
  1385.0 71.9 %collective-permute-start.175 = (bf16[48,4096]{1,0:T(8,128)(2,1)}, bf16[48,4096]{1,0:T(8,128)(2,1)}, u32[]{:S(2)}, u32[]{:S(2)}) collective-permute-start(bf16[48,4096]{1,0:T(8,128)(2,1)} %get-tuple-element.557), channel_id=1, source_target_pairs={{0,1},{1,3},{2,5},{3,7},{4,9},{5,11},{6,13},{7,15},{8,17},{9,19},{... | collective-permute-start | bytes 1179656 | tf_op jit(solution)/shard_map/ppermute | solution.py:543
  1389.4 57.6 %collective-permute-start.172 = (bf16[128,768]{1,0:T(8,128)(2,1)}, bf16[128,768]{1,0:T(8,128)(2,1)}, u32[]{:S(2)}, u32[]{:S(2)}) collective-permute-start(bf16[128,768]{1,0:T(8,128)(2,1)} %get-tuple-element.564), channel_id=1, source_target_pairs={{0,0},{1,2},{2,4},{3,6},{4,8},{5,10},{6,12},{7,14},{8,16},{9,18},{... | collective-permute-start | bytes 589832 | tf_op jit(solution)/shard_map/ppermute | solution.py:543
  1444.7 20.3 %collective-permute-start.171 = (bf16[64,4096]{1,0:T(8,128)(2,1)S(1)}, bf16[64,4096]{1,0:T(8,128)(2,1)S(1)}, u32[]{:S(2)}, u32[]{:S(2)}) collective-permute-start(bf16[64,4096]{1,0:T(8,128)(2,1)S(1)} %copy-done.57), channel_id=1, source_target_pairs={{0,16},{16,0},{1,17},{17,1},{2,18},{18,2},{3,19},{19,3},{4,20},{20... | collective-permute-start | bytes 1572872 | tf_op jit(solution)/shard_map/ppermute | solution.py:504
  1447.1 28.3 %collective-permute-start.168 = (bf16[16,36,538]{2,0,1:T(8,128)(2,1)S(1)}, bf16[16,36,538]{2,0,1:T(8,128)(2,1)S(1)}, u32[]{:S(2)}, u32[]{:S(2)}) collective-permute-start(bf16[16,36,538]{2,0,1:T(8,128)(2,1)S(1)} %bitcast.383), channel_id=1, source_target_pairs={{0,16},{16,0},{1,17},{17,1},{2,18},{18,2},{3,19},{19,3},{4,20},{20... | collective-permute-start | bytes 1859336 | tf_op jit(solution)/shard_map/ppermute | solution.py:504
  (326 other events, 2818.6 us)
Sparse Core Ops, SparseCore 0:
  96.5 59.8 all-gather.5
  232.2 52.9 all-gather.7
  619.6 137.4 all-gather.9
  1095.3 42.0 all-gather.11
  1242.9 42.2 all-gather.13
  1296.7 61.8 reduce-scatter.1
